TPU v7x, 32 devices: a whole 2x2x4 slice. The times are simulated.
32 devices in a mesh: dp: 4 (over y, core), seq: 8 (over z, x).
Axes of the slice: x: 2, y: 2, z: 4, core: 2. Of those that a mesh axis runs over, the one named last changes fastest.
Arguments:
- queries: bfloat16 [8192, 4096], P(('dp', 'seq')), parts along dimension 0, may hold values from -6 to 6
- keys: bfloat16 [8192, 1024], P(('dp', 'seq')), parts along dimension 0, may hold values from -6 to 6
- values: bfloat16 [8192, 1024], P(('dp', 'seq')), parts along dimension 0, may hold values from -6 to 6
- lengths: int32 [32], P('dp'), parts along dimension 0, may hold values from 1 to 1024, 2048 in all
- span_order: int32 [128], P('dp'), parts along dimension 0, may hold values from 0 to 31, each once
Outputs:
- attended: bfloat16 [8192, 4096], P(('dp', 'seq')), parts along dimension 0
There are 4 independent parts, one for each index of `dp`. A program takes and returns all parts, laid end to end along the dimension named above; each array names one. Nothing has to cross between parts.
Inputs may be any that keep to these rules, and one draw needn't show every extreme that they name: The lengths of one packed sequence sum to 2048; the longest is exactly 1024. A permutation of the 32 spans: balanced row b * 64 + i holds loader token span_order[b] * 64 + i.
All inputs are finite; a program needn't handle non-finite values.
Results may differ from a plain program's by a relative error of at most 0.0034.
Values may be sent and summed in bfloat16 or wider, within the bound.
No kernel may reach another device: no remote copies, remote signals or barrier semaphores. Data moves between devices by JAX's collectives and lax.ppermute only.
A program may use at most 64 MiB of HBM per device.

v0:
```python
import jax
import jax.numpy as jnp
from jax import lax
from jax.sharding import PartitionSpec as P

HEADS = 32
KV_HEADS = 8
HEAD_DIM = 128
BLOCK = 64
DOC_MOST = 1024
QBLOCK = 512


def doc_numbers(lengths, places):
    doc_ends = jnp.cumsum(lengths)
    return jnp.sum((doc_ends[None, :] <= places[:, None]).astype(jnp.int32), axis=1)


def attend(head_queries, key_sets, value_sets, doc_ids):
    total_rows = head_queries.shape[0]
    heads_here = head_queries.shape[1]
    shared = key_sets.shape[1] == 1
    pad_keys = jnp.concatenate(
        [jnp.zeros((DOC_MOST,) + key_sets.shape[1:], key_sets.dtype), key_sets], 0
    )
    pad_values = jnp.concatenate(
        [jnp.zeros((DOC_MOST,) + value_sets.shape[1:], value_sets.dtype), value_sets], 0
    )
    pad_docs = jnp.concatenate([jnp.full((DOC_MOST,), -1, jnp.int32), doc_ids], 0)
    scale_factor = HEAD_DIM ** (-0.5)

    def one_block(block_index):
        row_start = block_index * QBLOCK
        query_block = lax.dynamic_slice_in_dim(head_queries, row_start, QBLOCK, 0)
        key_block = lax.dynamic_slice_in_dim(pad_keys, row_start, QBLOCK + DOC_MOST, 0)
        value_block = lax.dynamic_slice_in_dim(pad_values, row_start, QBLOCK + DOC_MOST, 0)
        query_docs = lax.dynamic_slice_in_dim(pad_docs, row_start + DOC_MOST, QBLOCK, 0)
        key_docs = lax.dynamic_slice_in_dim(pad_docs, row_start, QBLOCK + DOC_MOST, 0)
        query_pos = row_start + jnp.arange(QBLOCK, dtype=jnp.int32)
        key_pos = row_start - DOC_MOST + jnp.arange(QBLOCK + DOC_MOST, dtype=jnp.int32)
        allowed = (query_docs[:, None] == key_docs[None, :]) & (
            key_pos[None, :] <= query_pos[:, None]
        )
        if shared:
            scores = jnp.einsum(
                "qgd,kd->gqk", query_block, key_block[:, 0], preferred_element_type=jnp.float32
            )
        else:
            scores = jnp.einsum(
                "qgd,kgd->gqk", query_block, key_block, preferred_element_type=jnp.float32
            )
        scores = jnp.where(allowed[None], scores * scale_factor, -jnp.inf)
        row_top = jnp.max(scores, axis=-1, keepdims=True)
        weights = jnp.exp(scores - row_top)
        row_total = jnp.sum(weights, axis=-1, keepdims=True)
        rounded = weights.astype(jnp.bfloat16)
        if shared:
            mixed_rows = jnp.einsum(
                "gqk,kd->qgd", rounded, value_block[:, 0], preferred_element_type=jnp.float32
            )
        else:
            mixed_rows = jnp.einsum(
                "gqk,kgd->qgd", rounded, value_block, preferred_element_type=jnp.float32
            )
        return (mixed_rows / jnp.transpose(row_total, (1, 0, 2))).astype(jnp.bfloat16)

    blocks = lax.map(one_block, jnp.arange(total_rows // QBLOCK, dtype=jnp.int32))
    return blocks.reshape(total_rows, heads_here * HEAD_DIM)


def shards(queries, keys, values, lengths, span_order):
    seq_devices = lax.axis_size("seq")
    rows_here = queries.shape[0]
    total_rows = rows_here * seq_devices
    nchunk = span_order.shape[0]
    heads_here = HEADS // seq_devices
    group_size = HEADS // KV_HEADS
    inverse = (
        jnp.zeros((nchunk,), jnp.int32).at[span_order].set(jnp.arange(nchunk, dtype=jnp.int32))
    )

    def to_loader(array):
        return array.reshape(nchunk, BLOCK, -1)[inverse].reshape(total_rows, -1)

    wide_keys = jnp.repeat(
        keys.reshape(rows_here, KV_HEADS, 1, HEAD_DIM), group_size, axis=2
    ).reshape(rows_here, HEADS * HEAD_DIM)
    wide_values = jnp.repeat(
        values.reshape(rows_here, KV_HEADS, 1, HEAD_DIM), group_size, axis=2
    ).reshape(rows_here, HEADS * HEAD_DIM)
    head_q, head_k, head_v = (
        lax.all_to_all(queries, "seq", split_axis=1, concat_axis=0, tiled=True),
        lax.all_to_all(wide_keys, "seq", split_axis=1, concat_axis=0, tiled=True),
        lax.all_to_all(wide_values, "seq", split_axis=1, concat_axis=0, tiled=True),
    )
    key_sets = to_loader(head_k).reshape(total_rows, heads_here, HEAD_DIM)
    value_sets = to_loader(head_v).reshape(total_rows, heads_here, HEAD_DIM)
    loader_queries = to_loader(head_q).reshape(total_rows, heads_here, HEAD_DIM)
    doc_ids = doc_numbers(lengths, jnp.arange(total_rows, dtype=jnp.int32))
    loader_out = attend(loader_queries, key_sets, value_sets, doc_ids)
    balanced_out = loader_out.reshape(nchunk, BLOCK, -1)[span_order].reshape(total_rows, -1)
    return lax.all_to_all(balanced_out, "seq", split_axis=0, concat_axis=1, tiled=True)


def solution(mesh):
    placed = (
        P(("dp", "seq"), None),
        P(("dp", "seq"), None),
        P(("dp", "seq"), None),
        P("dp"),
        P("dp"),
    )
    return jax.shard_map(
        shards, mesh=mesh, in_specs=placed, out_specs=P(("dp", "seq"), None), check_vma=False
    )
```

profile of v0, /device:TPU:0, one launch (start us, length us, event | category | flops | bytes accessed | tf_op | source)
XLA Modules:
  0.0 314.1 jit_solution(4646948867326838813)
XLA Ops:
  0.0 1.0 copy-done
  1.7 2.2 broadcast_in_dim.69
  3.9 7.4 %all-to-all-start.2 = ((bf16[256,8,512]{2,0,1:T(8,128)(2,1)}), bf16[256,8,512]{2,0,1:T(8,128)(2,1)}, u32[]{:S(2)}, u32[]{:S(2)}) async-start(bf16[256,8,512]{2,0,1:T(8,128)(2,1)} %broadcast_in_dim.69), calls=%async_computation.2 | async-start | bytes 4194304 | tf_op jit(solution)/shard_map/all_to_all | solution.py:93
  12.0 2.2 broadcast_in_dim.65
  14.2 45.5 %all-to-all-done.2 = bf16[256,8,512]{2,0,1:T(8,128)(2,1)} async-done(((bf16[256,8,512]{2,0,1:T(8,128)(2,1)}), bf16[256,8,512]{2,0,1:T(8,128)(2,1)}, u32[]{:S(2)}, u32[]{:S(2)}) %all-to-all-start.2) | async-done | bytes 2097184 | tf_op jit(solution)/shard_map/all_to_all | solution.py:93
  59.6 3.6 %all-to-all-start = ((bf16[256,8,512]{2,0,1:T(8,128)(2,1)}), bf16[256,8,512]{2,0,1:T(8,128)(2,1)S(1)}, u32[]{:S(2)}, u32[]{:S(2)}) async-start(bf16[256,8,512]{2,0,1:T(8,128)(2,1)} %broadcast_in_dim.65), calls=%async_computation | async-start | bytes 4194304 | tf_op jit(solution)/shard_map/all_to_all | solution.py:94
  63.3 4.1 %copy.23 = bf16[256,4096]{0,1:T(8,128)(2,1)} copy(bf16[256,4096]{1,0:T(8,128)(2,1)} %param.7) | data formatting | bytes 4194304 | tf_op args[0]
  67.4 44.3 %all-to-all-done = bf16[256,8,512]{2,0,1:T(8,128)(2,1)S(1)} async-done(((bf16[256,8,512]{2,0,1:T(8,128)(2,1)}), bf16[256,8,512]{2,0,1:T(8,128)(2,1)S(1)}, u32[]{:S(2)}, u32[]{:S(2)}) %all-to-all-start) | async-done | bytes 2097184 | tf_op jit(solution)/shard_map/all_to_all | solution.py:94
  111.7 1.3 copy-done.2
  113.0 3.6 %all-to-all-start.1 = ((bf16[256,8,512]{0,2,1:T(8,128)(2,1)}), bf16[256,8,512]{0,2,1:T(8,128)(2,1)S(1)}, u32[]{:S(2)}, u32[]{:S(2)}) async-start(bf16[256,8,512]{0,2,1:T(8,128)(2,1)} %bitcast.10), calls=%async_computation.1 | async-start | bytes 4194304 | tf_op jit(solution)/shard_map/all_to_all | solution.py:92
  117.7 3.6 %gather_fusion.2 = bf16[32,64,512]{2,1,0:T(8,128)(2,1)} fusion(bf16[32,64,512]{2,1,0:T(8,128)(2,1)} %bitcast.14, s32[1024]{0:T(1024)S(1)} %pad_clamp_fusion.1), kind=kCustom, calls=%fused_computation.2 | custom fusion | bytes 4194432 | tf_op jit(solution)/shard_map/gather | solution.py:83
  121.3 4.0 %reshape_reshape.16 = bf16[2048,4,128]{2,1,0:T(4,128)(2,1)} reshape(bf16[32,64,512]{2,1,0:T(8,128)(2,1)} %gather_fusion.2) | data formatting | bytes 4194304 | tf_op jit(solution)/shard_map/reshape;reshape | solution.py:96
  125.3 3.6 %gather_fusion = bf16[32,64,512]{2,1,0:T(8,128)(2,1)} fusion(bf16[32,64,512]{2,1,0:T(8,128)(2,1)} %bitcast.51, s32[1024]{0:T(1024)S(1)} %pad_clamp_fusion.1), kind=kCustom, calls=%fused_computation | custom fusion | bytes 4194432 | tf_op jit(solution)/shard_map/gather | solution.py:83
  128.9 4.0 %reshape_reshape.14 = bf16[2048,4,128]{2,1,0:T(4,128)(2,1)} reshape(bf16[32,64,512]{2,1,0:T(8,128)(2,1)} %gather_fusion) | data formatting | bytes 4194304 | tf_op jit(solution)/shard_map/reshape;reshape | solution.py:97
  132.9 4.4 %concatenate.11 = bf16[3072,4,128]{2,1,0:T(4,128)(2,1)} pad(bf16[2048,4,128]{2,1,0:T(4,128)(2,1)} %reshape_reshape.16, bf16[]{:T(256)} %constant.69.clone.1), padding=1024_0x0_0x0_0 | pad | bytes 5242882 | tf_op jit(solution)/shard_map/concatenate | solution.py:23
  137.3 10.8 %concatenate.9 = bf16[3072,4,128]{2,1,0:T(4,128)(2,1)} pad(bf16[2048,4,128]{2,1,0:T(4,128)(2,1)S(1)} %copy-done.3, bf16[]{:T(256)} %constant.69.clone.1), padding=1024_0x0_0x0_0 | pad | bytes 5242882 | tf_op jit(solution)/shard_map/concatenate | solution.py:26
  148.0 17.1 %all-to-all-done.1 = bf16[256,8,512]{0,2,1:T(8,128)(2,1)S(1)} async-done(((bf16[256,8,512]{0,2,1:T(8,128)(2,1)}), bf16[256,8,512]{0,2,1:T(8,128)(2,1)S(1)}, u32[]{:S(2)}, u32[]{:S(2)}) %all-to-all-start.1) | async-done | bytes 2097184 | tf_op jit(solution)/shard_map/all_to_all | solution.py:92
  165.1 2.4 copy.24
  167.5 2.3 gather_fusion.1
  169.8 2.1 reshape_reshape.15
  171.9 79.0 %while.12 = (s32[]{:T(128)}, bf16[4,512,4,128]{3,2,1,0:T(4,128)(2,1)}, s32[4]{0:T(128)S(1)}, bf16[3072,4,128]{2,1,0:T(4,128)(2,1)}, s32[3072]{0:T(1024)S(1)}, /*...) while((s32[]{:T(128)}, ...), condition=%wide.region_6.7_spmd, body=%wide.region_3.6_spmd.sunk | while | flops 1648097280 | bytes 54608688 | solution.py:67
  173.9 3.4 %constant_dynamic-slice_fusion.5 = (bf16[1536,4,128]{2,1,0:T(4,128)(2,1)}, bf16[1536,4,128]{2,1,0:T(4,128)(2,1)S(1)}) fusion(bf16[3072,4,128]{2,1,0:T(4,128)(2,1)} %get-tuple-element.222, s32[]{:T(128)S(6)} %select_n.65, bf16[3072,4,128]{2,1,0:T(4,128)(2,1)} %get-tuple-element.219), kind=kLoop, calls=%fused_computation.23.clone.1 | loop fusion | bytes 6291460 | tf_op jit(solution)/shard_map/while/body/eval_jaxpr/dynamic_slice | solution.py:35
  177.3 1.2 constant_dynamic-slice_fusion.6
  178.6 4.3 %fusion.37 = (f32[4,512]{1,0:T(4,128)S(1)}, f32[4,512,1536]{2,1,0:T(8,128)S(1)}) fusion(pred[512,1536]{1,0:T(8,128)(4,1)S(1)} %compare_and_fusion.2, bf16[1536,4,128]{2,1,0:T(4,128)(2,1)} %get-tuple-element.182, bf16[512,4,128]{2,1,0:T(4,128)(2,1)S(1)} %constant_dynamic-slice_fusion.6), kind=kOutput, calls=%fused_computation.7.clone.1 | convolution fusion | flops 814741504 | bytes 15474688 | tf_op jit(solution)/shard_map/while/body/eval_jaxpr/qgd,kgd->gqk/dot_general | solution.py:49
  182.9 3.6 %fusion.38 = f32[4,512]{1,0:T(4,128)S(1)} fusion(f32[4,512,1536]{2,1,0:T(8,128)S(1)} %get-tuple-element.183, f32[4,512]{1,0:T(4,128)S(1)} %get-tuple-element.184, pred[512,1536]{1,0:T(8,128)(4,1)S(1)} %compare_and_fusion.2), kind=kLoop, calls=%fused_computation.8.clone.1 | loop fusion | flops 12580864 | bytes 13385728 | tf_op jit(solution)/shard_map/while/body/eval_jaxpr/reduce_sum | solution.py:55
  186.4 3.9 %fusion.39 = bf16[1,512,4,128]{1,3,2,0:T(8,128)(2,1)S(1)} fusion(f32[4,512,1536]{2,1,0:T(8,128)S(1)} %get-tuple-element.183, f32[4,512]{1,0:T(4,128)S(1)} %get-tuple-element.184, pred[512,1536]{1,0:T(8,128)(4,1)S(1)} %compare_and_fusion.2, bf16[1536,4,128]{2,1,0:T(4,128)(2,1)S(1)} %get-tuple-element.185, f32[512,4]{0,1:T(4,128)S(1)} %bitcast.56), kind=kOutput, calls=%fused_computation.18.clone.1 | convolution fusion | flops 818413568 | bytes 15482880 | tf_op jit(solution)/shard_map/while/body/eval_jaxpr/gqk,kgd->qgd/dot_general | solution.py:62
  190.7 1.0 constant_dynamic-update-slice_fusion.2
  193.7 3.4 %constant_dynamic-slice_fusion.5 = (bf16[1536,4,128]{2,1,0:T(4,128)(2,1)}, bf16[1536,4,128]{2,1,0:T(4,128)(2,1)S(1)}) fusion(bf16[3072,4,128]{2,1,0:T(4,128)(2,1)} %get-tuple-element.222, s32[]{:T(128)S(6)} %select_n.65, bf16[3072,4,128]{2,1,0:T(4,128)(2,1)} %get-tuple-element.219), kind=kLoop, calls=%fused_computation.23.clone.1 | loop fusion | bytes 6291460 | tf_op jit(solution)/shard_map/while/body/eval_jaxpr/dynamic_slice | solution.py:35
  197.1 1.2 constant_dynamic-slice_fusion.6
  198.3 4.3 %fusion.37 = (f32[4,512]{1,0:T(4,128)S(1)}, f32[4,512,1536]{2,1,0:T(8,128)S(1)}) fusion(pred[512,1536]{1,0:T(8,128)(4,1)S(1)} %compare_and_fusion.2, bf16[1536,4,128]{2,1,0:T(4,128)(2,1)} %get-tuple-element.182, bf16[512,4,128]{2,1,0:T(4,128)(2,1)S(1)} %constant_dynamic-slice_fusion.6), kind=kOutput, calls=%fused_computation.7.clone.1 | convolution fusion | flops 814741504 | bytes 15474688 | tf_op jit(solution)/shard_map/while/body/eval_jaxpr/qgd,kgd->gqk/dot_general | solution.py:49
  202.6 3.6 %fusion.38 = f32[4,512]{1,0:T(4,128)S(1)} fusion(f32[4,512,1536]{2,1,0:T(8,128)S(1)} %get-tuple-element.183, f32[4,512]{1,0:T(4,128)S(1)} %get-tuple-element.184, pred[512,1536]{1,0:T(8,128)(4,1)S(1)} %compare_and_fusion.2), kind=kLoop, calls=%fused_computation.8.clone.1 | loop fusion | flops 12580864 | bytes 13385728 | tf_op jit(solution)/shard_map/while/body/eval_jaxpr/reduce_sum | solution.py:55
  206.2 3.9 %fusion.39 = bf16[1,512,4,128]{1,3,2,0:T(8,128)(2,1)S(1)} fusion(f32[4,512,1536]{2,1,0:T(8,128)S(1)} %get-tuple-element.183, f32[4,512]{1,0:T(4,128)S(1)} %get-tuple-element.184, pred[512,1536]{1,0:T(8,128)(4,1)S(1)} %compare_and_fusion.2, bf16[1536,4,128]{2,1,0:T(4,128)(2,1)S(1)} %get-tuple-element.185, f32[512,4]{0,1:T(4,128)S(1)} %bitcast.56), kind=kOutput, calls=%fused_computation.18.clone.1 | convolution fusion | flops 818413568 | bytes 15482880 | tf_op jit(solution)/shard_map/while/body/eval_jaxpr/gqk,kgd->qgd/dot_general | solution.py:62
  213.4 3.4 %constant_dynamic-slice_fusion.5 = (bf16[1536,4,128]{2,1,0:T(4,128)(2,1)}, bf16[1536,4,128]{2,1,0:T(4,128)(2,1)S(1)}) fusion(bf16[3072,4,128]{2,1,0:T(4,128)(2,1)} %get-tuple-element.222, s32[]{:T(128)S(6)} %select_n.65, bf16[3072,4,128]{2,1,0:T(4,128)(2,1)} %get-tuple-element.219), kind=kLoop, calls=%fused_computation.23.clone.1 | loop fusion | bytes 6291460 | tf_op jit(solution)/shard_map/while/body/eval_jaxpr/dynamic_slice | solution.py:35
  216.8 1.2 constant_dynamic-slice_fusion.6
  218.0 4.3 %fusion.37 = (f32[4,512]{1,0:T(4,128)S(1)}, f32[4,512,1536]{2,1,0:T(8,128)S(1)}) fusion(pred[512,1536]{1,0:T(8,128)(4,1)S(1)} %compare_and_fusion.2, bf16[1536,4,128]{2,1,0:T(4,128)(2,1)} %get-tuple-element.182, bf16[512,4,128]{2,1,0:T(4,128)(2,1)S(1)} %constant_dynamic-slice_fusion.6), kind=kOutput, calls=%fused_computation.7.clone.1 | convolution fusion | flops 814741504 | bytes 15474688 | tf_op jit(solution)/shard_map/while/body/eval_jaxpr/qgd,kgd->gqk/dot_general | solution.py:49
  222.3 3.6 %fusion.38 = f32[4,512]{1,0:T(4,128)S(1)} fusion(f32[4,512,1536]{2,1,0:T(8,128)S(1)} %get-tuple-element.183, f32[4,512]{1,0:T(4,128)S(1)} %get-tuple-element.184, pred[512,1536]{1,0:T(8,128)(4,1)S(1)} %compare_and_fusion.2), kind=kLoop, calls=%fused_computation.8.clone.1 | loop fusion | flops 12580864 | bytes 13385728 | tf_op jit(solution)/shard_map/while/body/eval_jaxpr/reduce_sum | solution.py:55
  225.9 3.9 %fusion.39 = bf16[1,512,4,128]{1,3,2,0:T(8,128)(2,1)S(1)} fusion(f32[4,512,1536]{2,1,0:T(8,128)S(1)} %get-tuple-element.183, f32[4,512]{1,0:T(4,128)S(1)} %get-tuple-element.184, pred[512,1536]{1,0:T(8,128)(4,1)S(1)} %compare_and_fusion.2, bf16[1536,4,128]{2,1,0:T(4,128)(2,1)S(1)} %get-tuple-element.185, f32[512,4]{0,1:T(4,128)S(1)} %bitcast.56), kind=kOutput, calls=%fused_computation.18.clone.1 | convolution fusion | flops 818413568 | bytes 15482880 | tf_op jit(solution)/shard_map/while/body/eval_jaxpr/gqk,kgd->qgd/dot_general | solution.py:62
  233.2 3.4 %constant_dynamic-slice_fusion.5 = (bf16[1536,4,128]{2,1,0:T(4,128)(2,1)}, bf16[1536,4,128]{2,1,0:T(4,128)(2,1)S(1)}) fusion(bf16[3072,4,128]{2,1,0:T(4,128)(2,1)} %get-tuple-element.222, s32[]{:T(128)S(6)} %select_n.65, bf16[3072,4,128]{2,1,0:T(4,128)(2,1)} %get-tuple-element.219), kind=kLoop, calls=%fused_computation.23.clone.1 | loop fusion | bytes 6291460 | tf_op jit(solution)/shard_map/while/body/eval_jaxpr/dynamic_slice | solution.py:35
  236.5 1.2 constant_dynamic-slice_fusion.6
  237.8 4.3 %fusion.37 = (f32[4,512]{1,0:T(4,128)S(1)}, f32[4,512,1536]{2,1,0:T(8,128)S(1)}) fusion(pred[512,1536]{1,0:T(8,128)(4,1)S(1)} %compare_and_fusion.2, bf16[1536,4,128]{2,1,0:T(4,128)(2,1)} %get-tuple-element.182, bf16[512,4,128]{2,1,0:T(4,128)(2,1)S(1)} %constant_dynamic-slice_fusion.6), kind=kOutput, calls=%fused_computation.7.clone.1 | convolution fusion | flops 814741504 | bytes 15474688 | tf_op jit(solution)/shard_map/while/body/eval_jaxpr/qgd,kgd->gqk/dot_general | solution.py:49
  242.1 3.6 %fusion.38 = f32[4,512]{1,0:T(4,128)S(1)} fusion(f32[4,512,1536]{2,1,0:T(8,128)S(1)} %get-tuple-element.183, f32[4,512]{1,0:T(4,128)S(1)} %get-tuple-element.184, pred[512,1536]{1,0:T(8,128)(4,1)S(1)} %compare_and_fusion.2), kind=kLoop, calls=%fused_computation.8.clone.1 | loop fusion | flops 12580864 | bytes 13385728 | tf_op jit(solution)/shard_map/while/body/eval_jaxpr/reduce_sum | solution.py:55
  245.7 3.9 %fusion.39 = bf16[1,512,4,128]{1,3,2,0:T(8,128)(2,1)S(1)} fusion(f32[4,512,1536]{2,1,0:T(8,128)S(1)} %get-tuple-element.183, f32[4,512]{1,0:T(4,128)S(1)} %get-tuple-element.184, pred[512,1536]{1,0:T(8,128)(4,1)S(1)} %compare_and_fusion.2, bf16[1536,4,128]{2,1,0:T(4,128)(2,1)S(1)} %get-tuple-element.185, f32[512,4]{0,1:T(4,128)S(1)} %bitcast.56), kind=kOutput, calls=%fused_computation.18.clone.1 | convolution fusion | flops 818413568 | bytes 15482880 | tf_op jit(solution)/shard_map/while/body/eval_jaxpr/gqk,kgd->qgd/dot_general | solution.py:62
  249.9 1.0 constant_dynamic-update-slice_fusion.2
  250.9 2.7 reshape_reshape.17
  253.6 2.0 gather_fusion.3
  255.6 52.0 %all_to_all.61 = bf16[8,256,512]{2,1,0:T(8,128)(2,1)S(1)} all-to-all(bf16[8,256,512]{2,1,0:T(8,128)(2,1)} %bitcast.53), channel_id=1, replica_groups=mesh['dp'=4,'seq'=8] {'seq'}, dimensions={0} | all-to-all | bytes 4194304 | tf_op jit(solution)/shard_map/all_to_all | solution.py:102
  307.6 2.4 copy.30
  310.0 4.1 %copy.31 = bf16[256,4096]{1,0:T(8,128)(2,1)} copy(bf16[256,4096]{0,1:T(8,128)(2,1)} %bitcast.55) | data formatting | bytes 4194304 | tf_op jit(solution)/shard_map/all_to_all | solution.py:102
  (57 shorter events, 11.3 us)
Async XLA Ops:
  0.0 1.0 copy-start
  3.9 7.4 %copy-start.4 = (bf16[256,1024]{1,0:T(8,128)(2,1)S(1)}, bf16[256,1024]{1,0:T(8,128)(2,1)}, u32[]{:S(2)}) copy-start(bf16[256,1024]{1,0:T(8,128)(2,1)} %param.9) | copy-start | bytes 1572868
  3.9 55.7 %all-to-all-start.2 = ((bf16[256,8,512]{2,0,1:T(8,128)(2,1)}), bf16[256,8,512]{2,0,1:T(8,128)(2,1)}, u32[]{:S(2)}, u32[]{:S(2)}) async-start(bf16[256,8,512]{2,0,1:T(8,128)(2,1)} %broadcast_in_dim.69), calls=%async_computation.2 | async-start | bytes 4194304 | tf_op jit(solution)/shard_map/all_to_all | solution.py:93
  59.6 52.1 %all-to-all-start = ((bf16[256,8,512]{2,0,1:T(8,128)(2,1)}), bf16[256,8,512]{2,0,1:T(8,128)(2,1)S(1)}, u32[]{:S(2)}, u32[]{:S(2)}) async-start(bf16[256,8,512]{2,0,1:T(8,128)(2,1)} %broadcast_in_dim.65), calls=%async_computation | async-start | bytes 4194304 | tf_op jit(solution)/shard_map/all_to_all | solution.py:94
  111.7 1.3 copy-start.2
  111.7 5.0 %copy-start.5 = (s32[8]{0:T(128)S(1)}, s32[8]{0:T(128)}, u32[]{:S(2)}) copy-start(s32[8]{0:T(128)} %param.10) | copy-start | bytes 100
  111.7 5.2 %copy-start.6 = (s32[32]{0:T(128)S(1)}, s32[32]{0:T(128)}, u32[]{:S(2)}) copy-start(s32[32]{0:T(128)} %param.11) | copy-start | bytes 388
  113.0 52.1 %all-to-all-start.1 = ((bf16[256,8,512]{0,2,1:T(8,128)(2,1)}), bf16[256,8,512]{0,2,1:T(8,128)(2,1)S(1)}, u32[]{:S(2)}, u32[]{:S(2)}) async-start(bf16[256,8,512]{0,2,1:T(8,128)(2,1)} %bitcast.10), calls=%async_computation.1 | async-start | bytes 4194304 | tf_op jit(solution)/shard_map/all_to_all | solution.py:92
  132.9 4.4 %copy-start.3 = (bf16[2048,4,128]{2,1,0:T(4,128)(2,1)S(1)}, bf16[2048,4,128]{2,1,0:T(4,128)(2,1)}, u32[]{:S(2)}) copy-start(bf16[2048,4,128]{2,1,0:T(4,128)(2,1)} %reshape_reshape.14) | copy-start | bytes 6291460
  310.0 4.1 %copy-start.1 = (bf16[256,1024]{1,0:T(8,128)(2,1)S(1)}, bf16[256,1024]{1,0:T(8,128)(2,1)}, u32[]{:S(2)}) copy-start(bf16[256,1024]{1,0:T(8,128)(2,1)} %param.8) | copy-start | bytes 1572868
where the time goes:
time: 315 us; the launch traced here: 314 us
  waiting for transfers between devices  107 us (34%)
  local copies, waits for them, and re-layouts  87.8 us (28%)
  blocking collectives  52 us (17%)
  matrix products  32.8 us (10%)
  other arithmetic  17.4 us (6%)
  starting transfers between devices  14.7 us (5%)
    all_to_all x1, blocking collectives, shards(): lax.all_to_all(balanced_out, 'seq', split_axis=0, concat_axis=1, tiled=True)  52 us
    all_to_all x1, waiting for transfers between devices, shards(): lax.all_to_all(wide_keys, 'seq', split_axis=1, concat_axis=0, tiled=True)  45.5 us
    all_to_all x1, waiting for transfers between devices, shards(): lax.all_to_all(wide_values, 'seq', split_axis=1, concat_axis=0, tiled=True)  44.3 us
    dot_general x4, matrix products, one_block(): jnp.einsum('qgd,kgd->gqk', query_block, key_block, preferred_element_type...  17.2 us
    all_to_all x1, waiting for transfers between devices, shards(): lax.all_to_all(queries, 'seq', split_axis=1, concat_axis=0, tiled=True)  17.1 us
    dot_general x4, matrix products, one_block(): jnp.einsum('gqk,kgd->qgd', rounded, value_block, preferred_element_type=j...  15.6 us
    reduce_sum x4, other arithmetic, one_block(): row_total = jnp.sum(weights, axis=-1, keepdims=True)  14.3 us
    dynamic_slice x4, local copies, waits for them, and re-layouts, one_block(): lax.dynamic_slice_in_dim(pad_keys, row_start, QBLOCK + DOC_MOST, 0)  13.5 us
  transfers between devices with their start and end apart: 3, of which 3 were waited for; matrix products, arithmetic and copies ran while one was open for 12% of the time, Pallas kernels for 0%

commit v1 on v0

v1 whole, which is shorter than its diff:
```python
import math
import jax
import jax.numpy as jnp
from jax import lax
from jax.experimental import pallas as pl
from jax.experimental.pallas import tpu as pltpu
from jax.sharding import PartitionSpec as P

HEADS = 32
KV_HEADS = 8
HEAD_DIM = 128
BLOCK = 64
DOC_MOST = 1024
GROUP = HEADS // KV_HEADS
KEY_STEP = 128
MOST_STEPS = -(-(DOC_MOST + BLOCK) // KEY_STEP)
CHUNKS = 2
KV_CHUNK = KV_HEADS // 2 // CHUNKS
Q_CHUNK = KV_CHUNK * GROUP
PAD = 128
EXP_SCALE = HEAD_DIM**-0.5 * math.log2(math.e)


def attend_span(lengths, row0, load_q, store_out, kv):
    row = row0 + lax.broadcasted_iota(jnp.int32, (BLOCK, KEY_STEP), 0)
    low = jnp.int32(0)
    starts = jnp.zeros((BLOCK, KEY_STEP), jnp.int32)
    end = jnp.int32(0)
    for j in range(lengths.shape[0]):
        end = end + lengths[j]
        low = jnp.where(end <= row0, end, low)
        starts = jnp.where(end <= row, end, starts)
    first = pl.multiple_of((low // BLOCK) * BLOCK, BLOCK)
    steps = (row0 + BLOCK - first + KEY_STEP - 1) // KEY_STEP

    def variant(count):
        width = count * KEY_STEP
        biases = []
        for t in range(count):
            col = first + t * KEY_STEP + lax.broadcasted_iota(jnp.int32, (BLOCK, KEY_STEP), 1)
            biases.append(jnp.where((col >= starts) & (col <= row), 0.0, -1e30).astype(jnp.float32))
        bias = jnp.concatenate(biases, axis=1)
        bias = jnp.concatenate([bias] * GROUP, axis=0)
        ones = jnp.ones((width, HEAD_DIM), jnp.bfloat16)
        for g in range(KV_CHUNK):
            q = load_q(g)
            k = kv[pl.ds(first, width), g * HEAD_DIM : (g + 1) * HEAD_DIM]
            v = kv[pl.ds(first, width), (KV_CHUNK + g) * HEAD_DIM : (KV_CHUNK + g + 1) * HEAD_DIM]
            s = lax.dot_general(q, k, (((1,), (1,)), ((), ())), preferred_element_type=jnp.float32)
            s = s + bias
            top = jnp.max(s, axis=1, keepdims=True)
            p = jnp.exp2((s - top) * EXP_SCALE).astype(jnp.bfloat16)
            mixed = jnp.dot(p, jnp.concatenate([v, ones], axis=1), preferred_element_type=jnp.float32)
            store_out(g, (mixed[:, :HEAD_DIM] / mixed[:, HEAD_DIM:]).astype(jnp.bfloat16))

    for count in range(1, MOST_STEPS + 1):
        pl.when(steps == count)(lambda count=count: variant(count))


def attention_kernel(seq_devices, lengths, order, q_own, q_pair, *rest):
    line = seq_devices // 2
    shards = rest[: 2 * line - 1]
    out_own, out_pair, kv, sem = rest[2 * line - 1 :]
    spans = q_own.shape[0] // BLOCK
    total_rows = order.shape[0] * BLOCK
    me = lax.axis_index("seq")
    place = me // 2
    pair = me - 2 * place

    def copies(ref, owner_place):
        for half in range(2):
            owner = 2 * owner_place + (pair if half == 0 else 1 - pair)
            for t in range(spans):
                target = pl.multiple_of(order[owner * spans + t] * BLOCK, BLOCK)
                yield pltpu.make_async_copy(
                    ref.at[pl.ds((half * spans + t) * BLOCK, BLOCK), :], kv.at[pl.ds(target, BLOCK), :], sem
                )

    def each(action):
        def act(ref, owner_place):
            for copy in copies(ref, owner_place):
                action(copy)

        act(shards[0], place)
        for k in range(1, line):
            pl.when(place >= k)(lambda k=k: act(shards[k], place - k))
            pl.when(place < k)(lambda k=k: act(shards[line - 1 + line - k], place - k + line))

    each(lambda copy: copy.start())
    kv[pl.ds(total_rows, PAD), :] = jnp.zeros((PAD, kv.shape[1]), jnp.bfloat16)
    each(lambda copy: copy.wait())

    for half, (q_ref, out_ref) in enumerate(((q_own, out_own), (q_pair, out_pair))):
        owner = me if half == 0 else 2 * place + 1 - pair

        def one_span(i, carry, q_ref=q_ref, out_ref=out_ref, owner=owner):
            rows = pl.ds(pl.multiple_of(i * BLOCK, BLOCK), BLOCK)

            def load_q(g):
                return jnp.concatenate(
                    [q_ref[rows, (g * GROUP + j) * HEAD_DIM : (g * GROUP + j + 1) * HEAD_DIM] for j in range(GROUP)], axis=0
                )

            def store_out(g, o):
                for j in range(GROUP):
                    out_ref[rows, (g * GROUP + j) * HEAD_DIM : (g * GROUP + j + 1) * HEAD_DIM] = o[
                        j * BLOCK : (j + 1) * BLOCK
                    ]

            attend_span(lengths, order[owner * spans + i] * BLOCK, load_q, store_out, kv)
            return carry

        lax.fori_loop(0, spans, one_span, 0)


def attention(seq_devices, lengths, order, q_own, q_pair, shards):
    total_rows = order.shape[0] * BLOCK
    out = jax.ShapeDtypeStruct(q_own.shape, jnp.bfloat16)
    smem = pl.BlockSpec(memory_space=pltpu.SMEM)
    vmem = pl.BlockSpec(memory_space=pltpu.VMEM)
    hbm = pl.BlockSpec(memory_space=pl.ANY)
    pairs = 2 * q_own.shape[0] * Q_CHUNK * 600
    return pl.pallas_call(
        lambda *refs: attention_kernel(seq_devices, *refs),
        out_shape=(out, out),
        in_specs=[smem, smem, vmem, vmem] + [hbm] * len(shards),
        out_specs=(vmem, vmem),
        scratch_shapes=[
            pltpu.VMEM((total_rows + PAD, 2 * KV_CHUNK * HEAD_DIM), jnp.bfloat16),
            pltpu.SemaphoreType.DMA,
        ],
        compiler_params=pltpu.CompilerParams(vmem_limit_bytes=40 * 1024 * 1024),
        cost_estimate=pl.CostEstimate(
            flops=pairs * 4 * HEAD_DIM, bytes_accessed=4 * q_own.size * 2 + total_rows * 1024, transcendentals=pairs
        ),
        name="attention",
    )(lengths, order, q_own, q_pair, *shards)


def shards(queries, keys, values, lengths, order):
    seq_devices = lax.axis_size("seq")
    line = seq_devices // 2
    me = lax.axis_index("seq")
    pair = me % 2
    swap = [(i, i ^ 1) for i in range(seq_devices)]
    kv_half = KV_HEADS // 2 * HEAD_DIM
    q_half = HEADS // 2 * HEAD_DIM

    def columns(array, half, width, chunk, size):
        return lax.dynamic_slice_in_dim(array, half * width + chunk * size, size, 1)

    def kv_piece(half, chunk):
        size = KV_CHUNK * HEAD_DIM
        return jnp.concatenate(
            [columns(keys, half, kv_half, chunk, size), columns(values, half, kv_half, chunk, size)], axis=1
        )

    def gather(shard):
        right, left = [], []
        r = l = shard
        for k in range(1, line):
            r = lax.ppermute(r, "seq", [(2 * z + x, 2 * z + 2 + x) for z in range(k - 1, line - 1) for x in range(2)])
            l = lax.ppermute(l, "seq", [(2 * z + x, 2 * z - 2 + x) for z in range(1, line + 1 - k) for x in range(2)])
            right.append(r)
            left.append(l)
        return [shard] + right + left

    gathered, q_owns, q_pairs = [], [], []
    size = Q_CHUNK * HEAD_DIM
    for c in range(CHUNKS):
        got = lax.ppermute(kv_piece(1 - pair, c), "seq", swap)
        gathered.append(gather(jnp.concatenate([kv_piece(pair, c), got], axis=0)))
    for c in range(CHUNKS):
        q_owns.append(columns(queries, pair, q_half, c, size))
        q_pairs.append(lax.ppermute(columns(queries, 1 - pair, q_half, c, size), "seq", swap))
    mine, theirs = [], []
    for c in range(CHUNKS):
        own, other = attention(seq_devices, lengths, order, q_owns[c], q_pairs[c], gathered[c])
        mine.append(own)
        theirs.append(lax.ppermute(other, "seq", swap))
    mine, theirs = jnp.concatenate(mine, axis=1), jnp.concatenate(theirs, axis=1)
    return jnp.where(
        pair == 0, jnp.concatenate([mine, theirs], axis=1), jnp.concatenate([theirs, mine], axis=1)
    )


def solution(mesh):
    placed = (
        P(("dp", "seq"), None),
        P(("dp", "seq"), None),
        P(("dp", "seq"), None),
        P("dp"),
        P("dp"),
    )
    return jax.shard_map(
        shards, mesh=mesh, in_specs=placed, out_specs=P(("dp", "seq"), None), check_vma=False
    )
```

time: 315 us -> 113 us (0.36)
  local copies, waits for them, and re-layouts: 87.8 us -> 3.09 us
  blocking collectives: 52 us -> 0 us
  waiting for transfers between devices: 107 us -> 57.3 us
  matrix products: 32.8 us -> 0 us
  Pallas kernels: 0 us -> 21.5 us
  other arithmetic: 17.4 us -> 2.83 us
  starting transfers between devices: 14.7 us -> 27.5 us
    all_to_all x3 -> x0, waiting for transfers between devices: 107 us -> none  [the longest x1 45.5 us: shards(): lax.all_to_all(wide_keys, 'seq', split_axis=1, concat_axis=0, tiled=True)]
    ppermute x0 -> x18, waiting for transfers between devices: none -> 57.3 us  [the longest x6 36.6 us: gather(): lax.ppermute(l, 'seq', [(2 * z + x, 2 * z - 2 + x) for z in range(1, line...]
    all_to_all x1 -> x0, blocking collectives: 52 us -> none  [shards(): lax.all_to_all(balanced_out, 'seq', split_axis=0, concat_axis=1, tiled=True)]
    dot_general x8 -> x0, matrix products: 32.8 us -> none  [the longest x4 17.2 us: one_block(): jnp.einsum('qgd,kgd->gqk', query_block, key_block, preferred_element_type...]
    ppermute x0 -> x18, starting transfers between devices: none -> 27.5 us  [the longest x6 11.4 us: gather(): lax.ppermute(r, 'seq', [(2 * z + x, 2 * z + 2 + x) for z in range(k - 1,...]
    pallas_call x0 -> x2, Pallas kernels: none -> 21.5 us  [attention(): pl.pallas_call(lambda *refs: attention_kernel(seq_devices, *refs), out_sh...]
    dynamic_slice x20 -> x2, local copies, waits for them, and re-layouts: 21.4 us -> 3.07 us  [columns(): return lax.dynamic_slice_in_dim(array, half * width + chunk * size, size, 1)]
    concatenate x3 -> x0, local copies, waits for them, and re-layouts: 15.1 us -> none  [the longest x1 10.8 us: attend(): jnp.concatenate([jnp.zeros((DOC_MOST,) + value_sets.shape[1:], value_sets...]
  transfers between devices with their start and end apart: 3 -> 18, of which waited for: 3 -> 8; matrix products, arithmetic and copies ran while one was open for 12% -> 2% of each run, Pallas kernels for 0% -> 19%
where the time goes in v1:
time: 113 us; the launch traced here: 112 us
  waiting for transfers between devices  57.3 us (51%)
  starting transfers between devices  27.5 us (24%)
  Pallas kernels  21.5 us (19%)
  local copies, waits for them, and re-layouts  3.09 us (3%)
  other arithmetic  2.83 us (3%)
    ppermute x6, waiting for transfers between devices, gather(): lax.ppermute(l, 'seq', [(2 * z + x, 2 * z - 2 + x) for z in range(1, line...  36.6 us
    pallas_call x2, Pallas kernels, attention(): pl.pallas_call(lambda *refs: attention_kernel(seq_devices, *refs), out_sh...  21.5 us
    ppermute x6, starting transfers between devices, gather(): lax.ppermute(r, 'seq', [(2 * z + x, 2 * z + 2 + x) for z in range(k - 1,...  11.4 us
    ppermute x2, waiting for transfers between devices, shards(): theirs.append(lax.ppermute(other, 'seq', swap))  8.64 us
    ppermute x6, starting transfers between devices, gather(): lax.ppermute(l, 'seq', [(2 * z + x, 2 * z - 2 + x) for z in range(1, line...  7.71 us
    ppermute x2, waiting for transfers between devices, shards(): got = lax.ppermute(kv_piece(1 - pair, c), 'seq', swap)  7.03 us
    ppermute x6, waiting for transfers between devices, gather(): lax.ppermute(r, 'seq', [(2 * z + x, 2 * z + 2 + x) for z in range(k - 1,...  5.05 us
    ppermute x2, starting transfers between devices, shards(): lax.ppermute(columns(queries, 1 - pair, q_half, c, size), 'seq', swap)  3.11 us
  transfers between devices with their start and end apart: 18, of which 8 were waited for; matrix products, arithmetic and copies ran while one was open for 2% of the time, Pallas kernels for 19%

profile of v1, /device:TPU:0, one launch (start us, length us, event | category | flops | bytes accessed | tf_op | source)
XLA Modules:
  0.0 112.5 jit_solution(15769847555646919023)
XLA Ops:
  0.0 1.4 %constant_dynamic-slice_fusion.8 = (bf16[256,256]{1,0:T(8,128)(2,1)S(1)}, bf16[256,256]{1,0:T(8,128)(2,1)S(1)}, bf16[256,256]{1,0:T(8,128)(2,1)S(1)}, bf16[256,2...) fusion(bf16[256,1024]{1,0:T(8,128)(2,1)} %param.7, ...), kind=kLoop, calls=%fused_computation.13 | loop fusion | bytes 2097168 | tf_op jit(solution)/shard_map/dynamic_slice | solution.py:150
  1.4 3.0 %collective-permute-start.1 = (bf16[256,512]{1,0:T(8,128)(2,1)S(1)}, bf16[256,512]{1,0:T(8,128)(2,1)S(1)}, u32[]{:S(2)}, u32[]{:S(2)}) collective-permute-start(bf16[256,512]{1,0:T(8,128)(2,1)S(1)} %pad_maximum_fusion.2), channel_id=1, source_target_pairs={{0,1},{1,0},{2,3},{3,2},{4,5},{5,4},{6,7},{7,6},{8,9},{9,8},{10,11... | collective-permute-start | bytes 786440 | tf_op jit(solution)/shard_map/ppermute | solution.py:171
  4.4 0.1 collective-permute-start.9
  4.5 7.0 %collective-permute-done.1 = bf16[256,512]{1,0:T(8,128)(2,1)S(1)} collective-permute-done((bf16[256,512]{1,0:T(8,128)(2,1)S(1)}, bf16[256,512]{1,0:T(8,128)(2,1)S(1)}, u32[]{:S(2)}, u32[]{:S(2)}) %collective-permute-start.1) | collective-permute-done | bytes 262176 | tf_op jit(solution)/shard_map/ppermute | solution.py:171
  11.6 4.1 %collective-permute-start.2 = (bf16[512,512]{1,0:T(8,128)(2,1)S(1)}, bf16[512,512]{1,0:T(8,128)(2,1)S(1)}, u32[]{:S(2)}, u32[]{:S(2)}) collective-permute-start(bf16[512,512]{1,0:T(8,128)(2,1)S(1)} %pad_maximum_fusion.refs_4_), channel_id=1, source_target_pairs={{0,2},{1,3},{2,4},{3,5},{4,6},{5,7},{8,10},{9,11},{10,12},{11,13},... | collective-permute-start | bytes 1572872 | tf_op jit(solution)/shard_map/ppermute | solution.py:162
  15.7 1.3 %collective-permute-start.5 = (bf16[512,512]{1,0:T(8,128)(2,1)S(1)}, bf16[512,512]{1,0:T(8,128)(2,1)S(1)}, u32[]{:S(2)}, u32[]{:S(2)}) collective-permute-start(bf16[512,512]{1,0:T(8,128)(2,1)S(1)} %pad_maximum_fusion.refs_4_), channel_id=1, source_target_pairs={{2,0},{3,1},{4,2},{5,3},{6,4},{7,5},{10,8},{11,9},{12,10},{13,11},... | collective-permute-start | bytes 1572872 | tf_op jit(solution)/shard_map/ppermute | solution.py:163
  17.0 0.0 collective-permute-done.9
  17.0 4.6 %collective-permute-start.10 = (bf16[512,512]{1,0:T(8,128)(2,1)S(1)}, bf16[512,512]{1,0:T(8,128)(2,1)S(1)}, u32[]{:S(2)}, u32[]{:S(2)}) collective-permute-start(bf16[512,512]{1,0:T(8,128)(2,1)S(1)} %pad_maximum_fusion.1.refs_4_), channel_id=1, source_target_pairs={{0,2},{1,3},{2,4},{3,5},{4,6},{5,7},{8,10},{9,11},{10,12},{11,13},... | collective-permute-start | bytes 1572872 | tf_op jit(solution)/shard_map/ppermute | solution.py:162
  21.6 1.3 %collective-permute-start.13 = (bf16[512,512]{1,0:T(8,128)(2,1)S(1)}, bf16[512,512]{1,0:T(8,128)(2,1)S(1)}, u32[]{:S(2)}, u32[]{:S(2)}) collective-permute-start(bf16[512,512]{1,0:T(8,128)(2,1)S(1)} %pad_maximum_fusion.1.refs_4_), channel_id=1, source_target_pairs={{2,0},{3,1},{4,2},{5,3},{6,4},{7,5},{10,8},{11,9},{12,10},{13,11},... | collective-permute-start | bytes 1572872 | tf_op jit(solution)/shard_map/ppermute | solution.py:163
  22.9 0.0 copy-start.1
  22.9 0.0 copy-start.2
  22.9 5.0 %collective-permute-done.2.refs_5_ = bf16[512,512]{1,0:T(8,128)(2,1)S(1)} collective-permute-done((bf16[512,512]{1,0:T(8,128)(2,1)S(1)}, bf16[512,512]{1,0:T(8,128)(2,1)S(1)}, u32[]{:S(2)}, u32[]{:S(2)}) %collective-permute-start.2) | collective-permute-done | bytes 524320 | tf_op jit(solution)/shard_map/ppermute | solution.py:162
  28.0 0.7 collective-permute-start.3
  28.7 3.7 %collective-permute-done.5.refs_8_ = bf16[512,512]{1,0:T(8,128)(2,1)S(1)} collective-permute-done((bf16[512,512]{1,0:T(8,128)(2,1)S(1)}, bf16[512,512]{1,0:T(8,128)(2,1)S(1)}, u32[]{:S(2)}, u32[]{:S(2)}) %collective-permute-start.5) | collective-permute-done | bytes 524320 | tf_op jit(solution)/shard_map/ppermute | solution.py:163
  32.4 1.3 %collective-permute-start.6 = (bf16[512,512]{1,0:T(8,128)(2,1)S(1)}, bf16[512,512]{1,0:T(8,128)(2,1)S(1)}, u32[]{:S(2)}, u32[]{:S(2)}) collective-permute-start(bf16[512,512]{1,0:T(8,128)(2,1)S(1)} %collective-permute-done.5.refs_8_), channel_id=1, source_target_pairs={{2,0},{3,1},{4,2},{5,3},{10,8},{11,9},{12,10},{13,11},{18,16},{19,... | collective-permute-start | bytes 1572872 | tf_op jit(solution)/shard_map/ppermute | solution.py:163
  33.7 1.7 %constant_dynamic-slice_fusion.10 = (bf16[256,1024]{1,0:T(8,128)(2,1)S(1)}, bf16[256,1024]{1,0:T(8,128)(2,1)S(1)}, bf16[256,1024]{1,0:T(8,128)(2,1)S(1)}, bf16[256,1024]{1,0:T(8,128)(2,1)S(1)}) fusion(bf16[256,4096]{1,0:T(8,128)(2,1)} %param.5, s32[]{:T(128)S(6)} %select_n.46, s32[]{:T(128)S(6)} %select_n.45, s32[]{:T(128)S(6)} %select_n.50, s32[]{:T(128)S(6)} %select_n.49), kind=kLoop, calls=%fused_computation.15 | loop fusion | bytes 4194320 | tf_op jit(solution)/shard_map/dynamic_slice | solution.py:150
  35.4 1.6 %collective-permute-start = (bf16[256,1024]{1,0:T(8,128)(2,1)S(1)}, bf16[256,1024]{1,0:T(8,128)(2,1)S(1)}, u32[]{:S(2)}, u32[]{:S(2)}) collective-permute-start(bf16[256,1024]{1,0:T(8,128)(2,1)S(1)} %get-tuple-element.13), channel_id=1, source_target_pairs={{0,1},{1,0},{2,3},{3,2},{4,5},{5,4},{6,7},{7,6},{8,9},{9,8},{10,11... | collective-permute-start | bytes 1572872 | tf_op jit(solution)/shard_map/ppermute | solution.py:175
  37.0 0.0 collective-permute-done.10.refs_5_
  37.0 0.7 collective-permute-start.11
  37.7 6.0 %collective-permute-done.13.refs_8_ = bf16[512,512]{1,0:T(8,128)(2,1)S(1)} collective-permute-done((bf16[512,512]{1,0:T(8,128)(2,1)S(1)}, bf16[512,512]{1,0:T(8,128)(2,1)S(1)}, u32[]{:S(2)}, u32[]{:S(2)}) %collective-permute-start.13) | collective-permute-done | bytes 524320 | tf_op jit(solution)/shard_map/ppermute | solution.py:163
  43.7 1.3 %collective-permute-start.14 = (bf16[512,512]{1,0:T(8,128)(2,1)S(1)}, bf16[512,512]{1,0:T(8,128)(2,1)S(1)}, u32[]{:S(2)}, u32[]{:S(2)}) collective-permute-start(bf16[512,512]{1,0:T(8,128)(2,1)S(1)} %collective-permute-done.13.refs_8_), channel_id=1, source_target_pairs={{2,0},{3,1},{4,2},{5,3},{10,8},{11,9},{12,10},{13,11},{18,16},{19,... | collective-permute-start | bytes 1572872 | tf_op jit(solution)/shard_map/ppermute | solution.py:163
  44.9 0.0 collective-permute-done.3.refs_6_
  44.9 0.7 collective-permute-start.4
  45.7 9.2 %collective-permute-done.6.refs_9_ = bf16[512,512]{1,0:T(8,128)(2,1)S(1)} collective-permute-done((bf16[512,512]{1,0:T(8,128)(2,1)S(1)}, bf16[512,512]{1,0:T(8,128)(2,1)S(1)}, u32[]{:S(2)}, u32[]{:S(2)}) %collective-permute-start.6) | collective-permute-done | bytes 524320 | tf_op jit(solution)/shard_map/ppermute | solution.py:163
  54.9 1.3 %collective-permute-start.7 = (bf16[512,512]{1,0:T(8,128)(2,1)S(1)}, bf16[512,512]{1,0:T(8,128)(2,1)S(1)}, u32[]{:S(2)}, u32[]{:S(2)}) collective-permute-start(bf16[512,512]{1,0:T(8,128)(2,1)S(1)} %collective-permute-done.6.refs_9_), channel_id=1, source_target_pairs={{2,0},{3,1},{10,8},{11,9},{18,16},{19,17},{26,24},{27,25}} | collective-permute-start | bytes 1572872 | tf_op jit(solution)/shard_map/ppermute | solution.py:163
  56.2 0.0 collective-permute-done.refs_3_
  56.2 1.6 %collective-permute-start.8 = (bf16[256,1024]{1,0:T(8,128)(2,1)S(1)}, bf16[256,1024]{1,0:T(8,128)(2,1)S(1)}, u32[]{:S(2)}, u32[]{:S(2)}) collective-permute-start(bf16[256,1024]{1,0:T(8,128)(2,1)S(1)} %get-tuple-element.15), channel_id=1, source_target_pairs={{0,1},{1,0},{2,3},{3,2},{4,5},{5,4},{6,7},{7,6},{8,9},{9,8},{10,11... | collective-permute-start | bytes 1572872 | tf_op jit(solution)/shard_map/ppermute | solution.py:175
  57.7 0.0 collective-permute-done.11.refs_6_
  57.7 0.7 collective-permute-start.12
  58.4 7.7 %collective-permute-done.14.refs_9_ = bf16[512,512]{1,0:T(8,128)(2,1)S(1)} collective-permute-done((bf16[512,512]{1,0:T(8,128)(2,1)S(1)}, bf16[512,512]{1,0:T(8,128)(2,1)S(1)}, u32[]{:S(2)}, u32[]{:S(2)}) %collective-permute-start.14) | collective-permute-done | bytes 524320 | tf_op jit(solution)/shard_map/ppermute | solution.py:163
  66.1 1.3 %collective-permute-start.15 = (bf16[512,512]{1,0:T(8,128)(2,1)S(1)}, bf16[512,512]{1,0:T(8,128)(2,1)S(1)}, u32[]{:S(2)}, u32[]{:S(2)}) collective-permute-start(bf16[512,512]{1,0:T(8,128)(2,1)S(1)} %collective-permute-done.14.refs_9_), channel_id=1, source_target_pairs={{2,0},{3,1},{10,8},{11,9},{18,16},{19,17},{26,24},{27,25}} | collective-permute-start | bytes 1572872 | tf_op jit(solution)/shard_map/ppermute | solution.py:163
  67.4 0.0 collective-permute-done.4.refs_7_
  67.4 9.9 %collective-permute-done.7.refs_10_ = bf16[512,512]{1,0:T(8,128)(2,1)S(1)} collective-permute-done((bf16[512,512]{1,0:T(8,128)(2,1)S(1)}, bf16[512,512]{1,0:T(8,128)(2,1)S(1)}, u32[]{:S(2)}, u32[]{:S(2)}) %collective-permute-start.7) | collective-permute-done | bytes 524320 | tf_op jit(solution)/shard_map/ppermute | solution.py:163
  77.4 0.0 copy-done.1
  77.4 0.0 copy-done.2
  77.4 11.0 %attention.2 = (bf16[256,1024]{1,0:T(8,128)(2,1)S(1)}, bf16[256,1024]{1,0:T(8,128)(2,1)}) custom-call(s32[8]{0:T(128)S(1)} %copy-done.1, s32[32]{0:T(128)S(1)} %copy-done.2, bf16[256,1024]{1,0:T(8,128)(2,1)S(1)} %get-tuple-element.14.refs_2_, bf16[256,1024]{1,0:T(8,128)(2,1)S(1)} %collective-permute-done.refs_3_, ...), custom_call_target="tpu_custom_call" | custom-call | flops 1258291200 | bytes 4194304 | tf_op jit(solution)/shard_map/attention/pallas_call | solution.py:123
  88.4 0.0 copy-start
  88.4 1.6 %collective-permute-start.16 = (bf16[256,1024]{1,0:T(8,128)(2,1)}, bf16[256,1024]{1,0:T(8,128)(2,1)S(1)}, u32[]{:S(2)}, u32[]{:S(2)}) collective-permute-start(bf16[256,1024]{1,0:T(8,128)(2,1)} %get-tuple-element.11), channel_id=1, source_target_pairs={{0,1},{1,0},{2,3},{3,2},{4,5},{5,4},{6,7},{7,6},{8,9},{9,8},{10,11... | collective-permute-start | bytes 1572872 | tf_op jit(solution)/shard_map/ppermute | solution.py:180
  90.0 0.0 collective-permute-done.8.refs_3_
  90.0 0.0 collective-permute-done.12.refs_7_
  90.0 0.0 collective-permute-done.15.refs_10_
  90.0 10.5 %attention.3 = (bf16[256,1024]{1,0:T(8,128)(2,1)S(1)}, bf16[256,1024]{1,0:T(8,128)(2,1)S(1)}) custom-call(s32[8]{0:T(128)S(1)} %copy-done.1, s32[32]{0:T(128)S(1)} %copy-done.2, bf16[256,1024]{1,0:T(8,128)(2,1)S(1)} %get-tuple-element.16.refs_2_, bf16[256,1024]{1,0:T(8,128)(2,1)S(1)} %collective-permute-done.8.refs_3_, ...), custom_call_target="tpu_custom_call" | custom-call | flops 1258291200 | bytes 4194304 | tf_op jit(solution)/shard_map/attention/pallas_call | solution.py:123
  100.5 0.0 copy-done
  100.5 0.6 collective-permute-start.17
  101.1 0.0 collective-permute-done.16
  101.1 8.6 %collective-permute-done.17 = bf16[256,1024]{1,0:T(8,128)(2,1)S(1)} collective-permute-done((bf16[256,1024]{1,0:T(8,128)(2,1)S(1)}, bf16[256,1024]{1,0:T(8,128)(2,1)S(1)}, u32[]{:S(2)}, u32[]{:S(2)}) %collective-permute-start.17) | collective-permute-done | bytes 524320 | tf_op jit(solution)/shard_map/ppermute | solution.py:180
  109.8 2.7 %maximum_select_fusion = bf16[256,4096]{1,0:T(8,128)(2,1)} fusion(bf16[256,1024]{1,0:T(8,128)(2,1)S(1)} %collective-permute-done.17, bf16[256,1024]{1,0:T(8,128)(2,1)S(1)} %collective-permute-done.16, bf16[256,1024]{1,0:T(8,128)(2,1)S(1)} %get-tuple-element.10, bf16[256,1024]{1,0:T(8,128)(2,1)} %copy-done, pred[]{:T(512)S(6)} %eq.5), kind=kLoop, calls=%fused_computation | loop fusion | flops 17825792 | bytes 4194305 | tf_op jit(solution)/shard_map/jit(_where)/select_n | solution.py:182
  (4 shorter events, 0.1 us)
Async XLA Ops:
  1.4 10.1 %collective-permute-start.1 = (bf16[256,512]{1,0:T(8,128)(2,1)S(1)}, bf16[256,512]{1,0:T(8,128)(2,1)S(1)}, u32[]{:S(2)}, u32[]{:S(2)}) collective-permute-start(bf16[256,512]{1,0:T(8,128)(2,1)S(1)} %pad_maximum_fusion.2), channel_id=1, source_target_pairs={{0,1},{1,0},{2,3},{3,2},{4,5},{5,4},{6,7},{7,6},{8,9},{9,8},{10,11... | collective-permute-start | bytes 786440 | tf_op jit(solution)/shard_map/ppermute | solution.py:171
  4.4 12.5 %collective-permute-start.9 = (bf16[256,512]{1,0:T(8,128)(2,1)S(1)}, bf16[256,512]{1,0:T(8,128)(2,1)S(1)}, u32[]{:S(2)}, u32[]{:S(2)}) collective-permute-start(bf16[256,512]{1,0:T(8,128)(2,1)S(1)} %pad_maximum_fusion.3), channel_id=1, source_target_pairs={{0,1},{1,0},{2,3},{3,2},{4,5},{5,4},{6,7},{7,6},{8,9},{9,8},{10,11... | collective-permute-start | bytes 786440 | tf_op jit(solution)/shard_map/ppermute | solution.py:171
  11.6 16.4 %collective-permute-start.2 = (bf16[512,512]{1,0:T(8,128)(2,1)S(1)}, bf16[512,512]{1,0:T(8,128)(2,1)S(1)}, u32[]{:S(2)}, u32[]{:S(2)}) collective-permute-start(bf16[512,512]{1,0:T(8,128)(2,1)S(1)} %pad_maximum_fusion.refs_4_), channel_id=1, source_target_pairs={{0,2},{1,3},{2,4},{3,5},{4,6},{5,7},{8,10},{9,11},{10,12},{11,13},... | collective-permute-start | bytes 1572872 | tf_op jit(solution)/shard_map/ppermute | solution.py:162
  15.7 16.8 %collective-permute-start.5 = (bf16[512,512]{1,0:T(8,128)(2,1)S(1)}, bf16[512,512]{1,0:T(8,128)(2,1)S(1)}, u32[]{:S(2)}, u32[]{:S(2)}) collective-permute-start(bf16[512,512]{1,0:T(8,128)(2,1)S(1)} %pad_maximum_fusion.refs_4_), channel_id=1, source_target_pairs={{2,0},{3,1},{4,2},{5,3},{6,4},{7,5},{10,8},{11,9},{12,10},{13,11},... | collective-permute-start | bytes 1572872 | tf_op jit(solution)/shard_map/ppermute | solution.py:163
  17.0 20.0 %collective-permute-start.10 = (bf16[512,512]{1,0:T(8,128)(2,1)S(1)}, bf16[512,512]{1,0:T(8,128)(2,1)S(1)}, u32[]{:S(2)}, u32[]{:S(2)}) collective-permute-start(bf16[512,512]{1,0:T(8,128)(2,1)S(1)} %pad_maximum_fusion.1.refs_4_), channel_id=1, source_target_pairs={{0,2},{1,3},{2,4},{3,5},{4,6},{5,7},{8,10},{9,11},{10,12},{11,13},... | collective-permute-start | bytes 1572872 | tf_op jit(solution)/shard_map/ppermute | solution.py:162
  21.6 22.0 %collective-permute-start.13 = (bf16[512,512]{1,0:T(8,128)(2,1)S(1)}, bf16[512,512]{1,0:T(8,128)(2,1)S(1)}, u32[]{:S(2)}, u32[]{:S(2)}) collective-permute-start(bf16[512,512]{1,0:T(8,128)(2,1)S(1)} %pad_maximum_fusion.1.refs_4_), channel_id=1, source_target_pairs={{2,0},{3,1},{4,2},{5,3},{6,4},{7,5},{10,8},{11,9},{12,10},{13,11},... | collective-permute-start | bytes 1572872 | tf_op jit(solution)/shard_map/ppermute | solution.py:163
  22.9 54.4 %copy-start.1 = (s32[8]{0:T(128)S(1)}, s32[8]{0:T(128)}, u32[]{:S(2)}) copy-start(s32[8]{0:T(128)} %refs_0_.3) | copy-start | bytes 100
  22.9 54.4 %copy-start.2 = (s32[32]{0:T(128)S(1)}, s32[32]{0:T(128)}, u32[]{:S(2)}) copy-start(s32[32]{0:T(128)} %refs_1_.3) | copy-start | bytes 388
  28.0 17.0 %collective-permute-start.3 = (bf16[512,512]{1,0:T(8,128)(2,1)S(1)}, bf16[512,512]{1,0:T(8,128)(2,1)S(1)}, u32[]{:S(2)}, u32[]{:S(2)}) collective-permute-start(bf16[512,512]{1,0:T(8,128)(2,1)S(1)} %collective-permute-done.2.refs_5_), channel_id=1, source_target_pairs={{2,4},{3,5},{4,6},{5,7},{10,12},{11,13},{12,14},{13,15},{18,20},{1... | collective-permute-start | bytes 1572872 | tf_op jit(solution)/shard_map/ppermute | solution.py:162
  32.4 22.5 %collective-permute-start.6 = (bf16[512,512]{1,0:T(8,128)(2,1)S(1)}, bf16[512,512]{1,0:T(8,128)(2,1)S(1)}, u32[]{:S(2)}, u32[]{:S(2)}) collective-permute-start(bf16[512,512]{1,0:T(8,128)(2,1)S(1)} %collective-permute-done.5.refs_8_), channel_id=1, source_target_pairs={{2,0},{3,1},{4,2},{5,3},{10,8},{11,9},{12,10},{13,11},{18,16},{19,... | collective-permute-start | bytes 1572872 | tf_op jit(solution)/shard_map/ppermute | solution.py:163
  35.4 20.8 %collective-permute-start = (bf16[256,1024]{1,0:T(8,128)(2,1)S(1)}, bf16[256,1024]{1,0:T(8,128)(2,1)S(1)}, u32[]{:S(2)}, u32[]{:S(2)}) collective-permute-start(bf16[256,1024]{1,0:T(8,128)(2,1)S(1)} %get-tuple-element.13), channel_id=1, source_target_pairs={{0,1},{1,0},{2,3},{3,2},{4,5},{5,4},{6,7},{7,6},{8,9},{9,8},{10,11... | collective-permute-start | bytes 1572872 | tf_op jit(solution)/shard_map/ppermute | solution.py:175
  37.0 20.8 %collective-permute-start.11 = (bf16[512,512]{1,0:T(8,128)(2,1)S(1)}, bf16[512,512]{1,0:T(8,128)(2,1)S(1)}, u32[]{:S(2)}, u32[]{:S(2)}) collective-permute-start(bf16[512,512]{1,0:T(8,128)(2,1)S(1)} %collective-permute-done.10.refs_5_), channel_id=1, source_target_pairs={{2,4},{3,5},{4,6},{5,7},{10,12},{11,13},{12,14},{13,15},{18,20},{1... | collective-permute-start | bytes 1572872 | tf_op jit(solution)/shard_map/ppermute | solution.py:162
  43.7 22.5 %collective-permute-start.14 = (bf16[512,512]{1,0:T(8,128)(2,1)S(1)}, bf16[512,512]{1,0:T(8,128)(2,1)S(1)}, u32[]{:S(2)}, u32[]{:S(2)}) collective-permute-start(bf16[512,512]{1,0:T(8,128)(2,1)S(1)} %collective-permute-done.13.refs_8_), channel_id=1, source_target_pairs={{2,0},{3,1},{4,2},{5,3},{10,8},{11,9},{12,10},{13,11},{18,16},{19,... | collective-permute-start | bytes 1572872 | tf_op jit(solution)/shard_map/ppermute | solution.py:163
  44.9 22.5 %collective-permute-start.4 = (bf16[512,512]{1,0:T(8,128)(2,1)S(1)}, bf16[512,512]{1,0:T(8,128)(2,1)S(1)}, u32[]{:S(2)}, u32[]{:S(2)}) collective-permute-start(bf16[512,512]{1,0:T(8,128)(2,1)S(1)} %collective-permute-done.3.refs_6_), channel_id=1, source_target_pairs={{4,6},{5,7},{12,14},{13,15},{20,22},{21,23},{28,30},{29,31}} | collective-permute-start | bytes 1572872 | tf_op jit(solution)/shard_map/ppermute | solution.py:162
  54.9 22.5 %collective-permute-start.7 = (bf16[512,512]{1,0:T(8,128)(2,1)S(1)}, bf16[512,512]{1,0:T(8,128)(2,1)S(1)}, u32[]{:S(2)}, u32[]{:S(2)}) collective-permute-start(bf16[512,512]{1,0:T(8,128)(2,1)S(1)} %collective-permute-done.6.refs_9_), channel_id=1, source_target_pairs={{2,0},{3,1},{10,8},{11,9},{18,16},{19,17},{26,24},{27,25}} | collective-permute-start | bytes 1572872 | tf_op jit(solution)/shard_map/ppermute | solution.py:163
  56.2 33.8 %collective-permute-start.8 = (bf16[256,1024]{1,0:T(8,128)(2,1)S(1)}, bf16[256,1024]{1,0:T(8,128)(2,1)S(1)}, u32[]{:S(2)}, u32[]{:S(2)}) collective-permute-start(bf16[256,1024]{1,0:T(8,128)(2,1)S(1)} %get-tuple-element.15), channel_id=1, source_target_pairs={{0,1},{1,0},{2,3},{3,2},{4,5},{5,4},{6,7},{7,6},{8,9},{9,8},{10,11... | collective-permute-start | bytes 1572872 | tf_op jit(solution)/shard_map/ppermute | solution.py:175
  57.7 32.2 %collective-permute-start.12 = (bf16[512,512]{1,0:T(8,128)(2,1)S(1)}, bf16[512,512]{1,0:T(8,128)(2,1)S(1)}, u32[]{:S(2)}, u32[]{:S(2)}) collective-permute-start(bf16[512,512]{1,0:T(8,128)(2,1)S(1)} %collective-permute-done.11.refs_6_), channel_id=1, source_target_pairs={{4,6},{5,7},{12,14},{13,15},{20,22},{21,23},{28,30},{29,31}} | collective-permute-start | bytes 1572872 | tf_op jit(solution)/shard_map/ppermute | solution.py:162
  66.1 23.8 %collective-permute-start.15 = (bf16[512,512]{1,0:T(8,128)(2,1)S(1)}, bf16[512,512]{1,0:T(8,128)(2,1)S(1)}, u32[]{:S(2)}, u32[]{:S(2)}) collective-permute-start(bf16[512,512]{1,0:T(8,128)(2,1)S(1)} %collective-permute-done.14.refs_9_), channel_id=1, source_target_pairs={{2,0},{3,1},{10,8},{11,9},{18,16},{19,17},{26,24},{27,25}} | collective-permute-start | bytes 1572872 | tf_op jit(solution)/shard_map/ppermute | solution.py:163
  88.4 12.1 %copy-start = (bf16[256,1024]{1,0:T(8,128)(2,1)}, bf16[256,1024]{1,0:T(8,128)(2,1)S(1)}, u32[]{:S(2)}) copy-start(bf16[256,1024]{1,0:T(8,128)(2,1)S(1)} %get-tuple-element.9) | copy-start | bytes 1572868
  88.4 12.7 %collective-permute-start.16 = (bf16[256,1024]{1,0:T(8,128)(2,1)}, bf16[256,1024]{1,0:T(8,128)(2,1)S(1)}, u32[]{:S(2)}, u32[]{:S(2)}) collective-permute-start(bf16[256,1024]{1,0:T(8,128)(2,1)} %get-tuple-element.11), channel_id=1, source_target_pairs={{0,1},{1,0},{2,3},{3,2},{4,5},{5,4},{6,7},{7,6},{8,9},{9,8},{10,11... | collective-permute-start | bytes 1572872 | tf_op jit(solution)/shard_map/ppermute | solution.py:180
  100.5 9.2 %collective-permute-start.17 = (bf16[256,1024]{1,0:T(8,128)(2,1)S(1)}, bf16[256,1024]{1,0:T(8,128)(2,1)S(1)}, u32[]{:S(2)}, u32[]{:S(2)}) collective-permute-start(bf16[256,1024]{1,0:T(8,128)(2,1)S(1)} %get-tuple-element.12), channel_id=1, source_target_pairs={{0,1},{1,0},{2,3},{3,2},{4,5},{5,4},{6,7},{7,6},{8,9},{9,8},{10,11... | collective-permute-start | bytes 1572872 | tf_op jit(solution)/shard_map/ppermute | solution.py:180

commit v2 on v0

v2 whole, which is shorter than its diff:
```python
import math
import jax
import jax.numpy as jnp
from jax import lax
from jax.experimental import pallas as pl
from jax.experimental.pallas import tpu as pltpu
from jax.sharding import PartitionSpec as P

HEADS = 32
KV_HEADS = 8
HEAD_DIM = 128
BLOCK = 64
DOC_MOST = 1024
GROUP = HEADS // KV_HEADS
KV_HALF = KV_HEADS // 2
KEY_STEP = 128
MOST_STEPS = -(-(DOC_MOST + BLOCK) // KEY_STEP)
EXP_SCALE = HEAD_DIM**-0.5 * math.log2(math.e)
GQ = GROUP * HEAD_DIM
VMEM_BYTES = 60 * 1024 * 1024
COUNTS = tuple(range(1, MOST_STEPS + 1))
TOGETHER = {1: 2, 2: 2}


def attend_spans(lengths, positions, heads, load_q, store_out, kv):
    spans = []
    most = jnp.int32(0)
    for row0 in positions:
        row = row0 + lax.broadcasted_iota(jnp.int32, (BLOCK, KEY_STEP), 0)
        low = jnp.int32(0)
        starts = jnp.zeros((BLOCK, KEY_STEP), jnp.int32)
        end = jnp.int32(0)
        for j in range(lengths.shape[0]):
            end = end + lengths[j]
            low = jnp.where(end <= row0, end, low)
            starts = jnp.where(end <= row, end, starts)
        spans.append((row0, row, starts))
        most = jnp.maximum(most, row0 + BLOCK - (low // BLOCK) * BLOCK)
    steps = (most + KEY_STEP - 1) // KEY_STEP

    def variant(count):
        width = count * KEY_STEP
        tiles = []
        for u, (row0, row, starts) in enumerate(spans):
            first = pl.multiple_of(jnp.maximum(row0 + BLOCK - width, 0), BLOCK)
            biases = []
            for t in range(count):
                col = first + t * KEY_STEP + lax.broadcasted_iota(jnp.int32, (BLOCK, KEY_STEP), 1)
                biases.append(jnp.where((col >= starts) & (col <= row), 0.0, -1e30).astype(jnp.float32))
            bias = jnp.concatenate(biases, axis=1)
            bias = jnp.concatenate([bias] * GROUP, axis=0)
            for g in range(heads):
                k = kv[pl.ds(first, width), g * HEAD_DIM : (g + 1) * HEAD_DIM]
                s = lax.dot_general(load_q(u, g), k, (((1,), (1,)), ((), ())), preferred_element_type=jnp.float32)
                tiles.append((u, g, first, s + bias))
        for u, g, first, s in tiles:
            v = kv[pl.ds(first, width), (heads + g) * HEAD_DIM : (heads + g + 1) * HEAD_DIM]
            top = jnp.max(s, axis=1, keepdims=True)
            p = jnp.exp2((s - top) * EXP_SCALE)
            total = jnp.sum(p, axis=1, keepdims=True)
            mixed = jnp.dot(p.astype(jnp.bfloat16), v, preferred_element_type=jnp.float32)
            store_out(u, g, (mixed / total).astype(jnp.bfloat16))

    def choose(counts):
        if len(counts) == 1:
            variant(counts[0])
            return
        half = len(counts) // 2
        small = steps <= counts[half - 1]
        pl.when(small)(lambda: choose(counts[:half]))
        pl.when(jnp.logical_not(small))(lambda: choose(counts[half:]))

    choose(COUNTS)


def attention(name, heads, lengths, order, arrays, q_plan, kv_plan, active=None, wide=None, column=None):
    total_rows = order.shape[0] * BLOCK
    rows_here = total_rows // lax.axis_size("seq")
    spans = rows_here // BLOCK
    q_width, kv_width = heads * GQ, 2 * heads * HEAD_DIM
    blocks = len(q_plan(0, 0))
    together = TOGETHER[heads]

    def kernel(lengths, order, *refs):
        inputs, outs = refs[: len(arrays)], refs[-5 - blocks : -5]
        kv, q_all, o_all, sem_in, sem_out = refs[-5:]
        me = lax.axis_index("seq")
        place = me // 2
        pair = me - 2 * place
        queries = q_plan(place, pair)

        def q_copy(b):
            array, row, column, _ = queries[b]
            return pltpu.make_async_copy(
                inputs[array].at[pl.ds(row, rows_here), pl.ds(column, q_width)],
                q_all.at[pl.ds(b * rows_here, rows_here), :],
                sem_in,
            )

        def out_copy(b, i):
            source = pl.multiple_of(b * rows_here + i * BLOCK, BLOCK)
            target = pl.multiple_of(i * BLOCK, BLOCK)
            size = together * BLOCK
            place = outs[b].at[pl.ds(target, size), :]
            if column is not None and b == blocks - 1:
                place = outs[b].at[pl.ds(target, size), pl.ds(column(pair), q_width)]
            return pltpu.make_async_copy(
                o_all.at[pl.ds(source, size), :], place, sem_out
            )

        def each_kv(action):
            for condition, array, row, column, owner in kv_plan(place, pair):

                def act(array=array, row=row, column=column, owner=owner):
                    for t in range(spans):
                        target = pl.multiple_of(order[owner * spans + t] * BLOCK, BLOCK)
                        action(
                            pltpu.make_async_copy(
                                inputs[array].at[pl.ds(row + t * BLOCK, BLOCK), pl.ds(column, kv_width)],
                                kv.at[pl.ds(target, BLOCK), :],
                                sem_in,
                            )
                        )

                act() if condition is None else pl.when(condition)(act)

        def one_group(i, carry):
            block = i * together // spans
            owner = queries[0][3]
            for b in range(1, blocks):
                owner = jnp.where(block == b, queries[b][3], owner)
            within = i * together - block * spans

            def rows(u):
                return pl.ds(pl.multiple_of((i * together + u) * BLOCK, BLOCK), BLOCK)

            def load_q(u, g):
                return jnp.concatenate(
                    [q_all[rows(u), (g * GROUP + j) * HEAD_DIM : (g * GROUP + j + 1) * HEAD_DIM] for j in range(GROUP)],
                    axis=0,
                )

            def store_out(u, g, o):
                for j in range(GROUP):
                    o_all[rows(u), (g * GROUP + j) * HEAD_DIM : (g * GROUP + j + 1) * HEAD_DIM] = o[
                        j * BLOCK : (j + 1) * BLOCK
                    ]

            positions = [order[owner * spans + within + u] * BLOCK for u in range(together)]
            attend_spans(lengths, positions, heads, load_q, store_out, kv)
            for b in range(blocks):
                pl.when(block == b)(lambda b=b: out_copy(b, within).start())
            return carry

        def body():
            each_kv(lambda copy: copy.start())
            for b in range(blocks):
                q_copy(b).start()
            pltpu.make_async_copy(kv.at[pl.ds(0, total_rows), :], kv.at[pl.ds(0, total_rows), :], sem_in).wait()
            for b in range(blocks):
                q_copy(b).wait()
            lax.fori_loop(0, blocks * spans // together, one_group, 0)
            for b in range(blocks):
                for i in range(0, spans, together):
                    out_copy(b, i).wait()

        body() if active is None else pl.when(active(place))(body)

    smem = pl.BlockSpec(memory_space=pltpu.SMEM)
    hbm = pl.BlockSpec(memory_space=pl.ANY)
    pairs = blocks * rows_here * heads * GROUP * 600
    shapes = [jax.ShapeDtypeStruct((rows_here, q_width), jnp.bfloat16)] * blocks
    if column is not None:
        shapes[-1] = jax.ShapeDtypeStruct((rows_here, HEADS * HEAD_DIM), jnp.bfloat16)
    given = [] if wide is None else [wide]
    return pl.pallas_call(
        kernel,
        out_shape=shapes,
        in_specs=[smem, smem] + [hbm] * (len(arrays) + len(given)),
        out_specs=[hbm] * blocks,
        scratch_shapes=[
            pltpu.VMEM((total_rows, kv_width), jnp.bfloat16),
            pltpu.VMEM((blocks * rows_here, q_width), jnp.bfloat16),
            pltpu.VMEM((blocks * rows_here, q_width), jnp.bfloat16),
            pltpu.SemaphoreType.DMA,
            pltpu.SemaphoreType.DMA,
        ],
        compiler_params=pltpu.CompilerParams(vmem_limit_bytes=VMEM_BYTES),
        cost_estimate=pl.CostEstimate(
            flops=pairs * 4 * HEAD_DIM, bytes_accessed=4 * blocks * rows_here * q_width, transcendentals=pairs
        ),
        input_output_aliases={2 + len(arrays): blocks - 1} if given else {},
        name=name,
    )(lengths, order, *arrays, *given)


def split(name, arrays, widths, plan):
    n, count = arrays[0].shape[0], len(widths)

    def kernel(*refs):
        inputs, outs = refs[: len(arrays)], refs[len(arrays) : len(arrays) + count]
        held, sems, sem_out = refs[len(arrays) + count : -2], refs[-2], refs[-1]
        pair = lax.axis_index("seq") % 2

        def ins(o):
            to = 0
            for array, first, size in plan(pair)[o]:
                yield pltpu.make_async_copy(
                    inputs[array].at[:, pl.ds(first, size)], held[o].at[:, pl.ds(to, size)], sems.at[o]
                )
                to += size

        for o in range(count):
            for copy in ins(o):
                copy.start()
        for o in range(count):
            for copy in ins(o):
                copy.wait()
            pltpu.make_async_copy(held[o], outs[o], sem_out).start()
        for o in range(count):
            pltpu.make_async_copy(held[o], outs[o], sem_out).wait()

    hbm = pl.BlockSpec(memory_space=pl.ANY)
    return pl.pallas_call(
        kernel,
        out_shape=[jax.ShapeDtypeStruct((n, width), jnp.bfloat16) for width in widths],
        in_specs=[hbm] * len(arrays),
        out_specs=[hbm] * count,
        scratch_shapes=[pltpu.VMEM((n, width), jnp.bfloat16) for width in widths]
        + [pltpu.SemaphoreType.DMA((count,)), pltpu.SemaphoreType.DMA],
        compiler_params=pltpu.CompilerParams(vmem_limit_bytes=VMEM_BYTES),
        cost_estimate=pl.CostEstimate(flops=0, bytes_accessed=4 * n * sum(widths), transcendentals=0),
        name=name,
    )(*arrays)


def columns(array, first, size):
    return lax.dynamic_slice_in_dim(array, first, size, 1)


def kv_columns(keys, values, half, head, count):
    first, size = (half * KV_HALF + head) * HEAD_DIM, count * HEAD_DIM
    return [columns(keys, first, size), columns(values, first, size)]


def assemble(pair, mine, theirs):
    mine, theirs = jnp.concatenate(mine, axis=1), jnp.concatenate(theirs, axis=1)
    return jnp.where(
        pair == 0, jnp.concatenate([mine, theirs], axis=1), jnp.concatenate([theirs, mine], axis=1)
    )


def line_shards(queries, keys, values, lengths, order):
    devices = lax.axis_size("seq")
    line = devices // 2
    pair = lax.axis_index("seq") % 2
    rows_here = queries.shape[0]
    swap = [(i, i ^ 1) for i in range(devices)]

    def gather(shard):
        right, left = [], []
        r = l = shard
        for k in range(1, line):
            r = lax.ppermute(r, "seq", [(2 * z + x, 2 * z + 2 + x) for z in range(k - 1, line - 1) for x in range(2)])
            l = lax.ppermute(l, "seq", [(2 * z + x, 2 * z - 2 + x) for z in range(1, line + 1 - k) for x in range(2)])
            right.append(r)
            left.append(l)
        return [shard] + right + left

    mine, theirs = [], []
    heads = KV_HALF // 2
    for c in range(2):
        own = jnp.concatenate(kv_columns(keys, values, pair, c * heads, heads), axis=1)
        other = jnp.concatenate(kv_columns(keys, values, 1 - pair, c * heads, heads), axis=1)
        gathered = gather(jnp.concatenate([own, lax.ppermute(other, "seq", swap)], axis=0))
        q_other = lax.ppermute(
            columns(queries, (1 - pair) * KV_HALF * GQ + c * heads * GQ, heads * GQ), "seq", swap
        )

        def q_plan(place, pair, c=c):
            me = 2 * place + pair
            return [(0, 0, pair * KV_HALF * GQ + c * heads * GQ, me), (1, 0, 0, 2 * place + 1 - pair)]

        def kv_plan(place, pair):
            plan = []
            for half, x in enumerate((pair, 1 - pair)):
                row = half * rows_here
                plan.append((None, 2, row, 0, 2 * place + x))
                for k in range(1, line):
                    plan.append((place >= k, 2 + k, row, 0, 2 * (place - k) + x))
                    plan.append((place < k, 2 + line - 1 + line - k, row, 0, 2 * (place - k + line) + x))
            return plan

        a, b = attention("attention", heads, lengths, order, [queries, q_other] + gathered, q_plan, kv_plan)
        mine.append(a)
        theirs.append(lax.ppermute(b, "seq", swap))
    return assemble(pair, mine, theirs)


def after(array, *others):
    return lax.optimization_barrier((array,) + others)[0]


def short_shards(queries, keys, values, lengths, order):
    pair = lax.axis_index("seq") % 2
    n = queries.shape[0]
    parts = lax.axis_size("dp")
    both = ("dp", "seq")

    def permutation(links):
        return [(8 * d + 2 * a + x, 8 * d + 2 * b + x) for d in range(parts) for a, b in links for x in range(2)]

    outer = permutation([(0, 1), (1, 0), (2, 3), (3, 2)])
    inner = permutation([(1, 2), (2, 1)])
    inner += [(8 * d + 2 * z + x, 8 * (d ^ 1) + 2 * z + x) for d in range(parts) for z in (0, 3) for x in range(2)]
    across = [(8 * d + i, 8 * d + (i ^ 1)) for d in range(parts) for i in range(8)]

    def swap_x(a):
        return lax.ppermute(a, both, across)

    def swap_outer(a):
        return lax.ppermute(a, both, outer)

    def swap_inner(a):
        return lax.ppermute(a, both, inner)

    def rows(*blocks):
        return jnp.concatenate(blocks, axis=0)

    def middle(place):
        return (place == 1) | (place == 2)

    def end(place):
        return jnp.logical_not(middle(place))

    def near(place):
        return place + 1 - 2 * (place % 2)

    one, two = HEAD_DIM, 2 * HEAD_DIM
    kv_half, q_half = KV_HALF * HEAD_DIM, KV_HALF * GQ

    def t_plan(pair):
        return [[(a, half * kv_half, two) for a in range(2)] for half in (pair, 1 - pair)]

    def w_plan(pair):
        return [
            [(a, half * kv_half + head * one, one) for head in (2, 3) for a in range(2)] for half in (pair, 1 - pair)
        ]

    def q_plan(pair):
        return [[(0, (1 - pair) * q_half + i * 2 * GQ, 2 * GQ)] for i in range(2)]

    t_own, t_send = split("split_t", [keys, values], [2 * two] * 2, t_plan)
    t_par = swap_x(t_send)
    t_near_own = swap_outer(t_own)
    t_in_own = swap_inner(t_own)
    w_own, w_send = split("split_w", [keys, after(values, t_own)], [2 * two] * 2, w_plan)
    w_par = swap_x(w_send)
    qt_send, qw_send = split("split_q", [after(queries, w_own)], [2 * GQ] * 2, q_plan)
    t_near_par = swap_outer(t_par)
    t_in_par = swap_inner(t_par)
    w_shard = rows(w_own, w_par)
    qt_par = swap_x(after(qt_send, w_par))
    t_far_own = swap_inner(t_near_own)
    t_out_own = swap_outer(t_in_own)
    t_far_par = swap_inner(t_near_par)
    t_out_par = swap_outer(t_in_par)
    w_near = swap_outer(w_shard)
    w_in = swap_inner(w_shard)
    qw_par = swap_x(after(qw_send, qt_par))
    t_out_far_own = swap_outer(t_far_own)
    t_out_far_par = swap_outer(t_far_par)
    w_out = swap_outer(w_in)
    w_far = swap_inner(w_near)

    def each_half(plan):
        def full(place, pair):
            return [
                (condition, array, row, column, 2 * owner + x)
                for half, x in enumerate((pair, 1 - pair))
                for condition, array, row, column, owner in plan(place, half)
            ]

        return full

    def t_queries(place, pair):
        return [(1, 0, 0, 2 * place + 1 - pair), (0, 0, pair * q_half, 2 * place + pair)]

    def t_keys(place, half):
        return [
            (None, 2 + half, 0, 0, place),
            (None, 4 + half, 0, 0, near(place)),
            (middle(place), 6 + half, 0, 0, 3 - place),
            (middle(place), 8 + half, 0, 0, 3 - near(place)),
            (end(place), 10 + half, 0, 0, 3 - near(place)),
            (end(place), 12 + half, 0, 0, 3 - place),
        ]

    t_other, wide = attention(
        "attention_t",
        2,
        lengths,
        order,
        [queries, qt_par, t_own, t_par, t_near_own, t_near_par, t_in_own, t_in_par]
        + [t_far_own, t_far_par, t_out_own, t_out_par, t_out_far_own, t_out_far_par],
        t_queries,
        each_half(t_keys),
        column=lambda pair: pair * q_half,
    )
    t_theirs = swap_x(t_other)

    mine, theirs = pair * q_half, (1 - pair) * q_half
    blocks = [(t_theirs, theirs)]
    for head in (2, 3):
        first = (head - 2) * two
        far = swap_outer(w_far[:, first : first + two])

        def w_queries(place, pair, head=head):
            return [(1, 0, (head - 2) * GQ, 2 * place + 1 - pair), (0, 0, pair * q_half + head * GQ, 2 * place + pair)]

        def w_keys(place, half, first=first):
            return [
                (None, 2, half * n, first, place),
                (None, 3, half * n, first, near(place)),
                (middle(place), 4, half * n, first, 3 - place),
                (middle(place), 5, half * n, first, 3 - near(place)),
                (end(place), 6, half * n, first, 3 - near(place)),
                (end(place), 7, half * n, 0, 3 - place),
            ]

        other, wide = attention(
            "attention_" + str(head),
            1,
            lengths,
            order,
            [queries, qw_par, w_shard, w_near, w_in, w_far, w_out, far],
            w_queries,
            each_half(w_keys),
            wide=wide,
            column=lambda pair, head=head: pair * q_half + head * GQ,
        )
        blocks.append((swap_x(other), theirs + head * GQ))
    for block, column in blocks:
        wide = lax.dynamic_update_slice_in_dim(wide, block, column, 1)
    return wide


def shards(queries, keys, values, lengths, order):
    whole = short_shards if lax.axis_size("seq") == 8 else line_shards
    return whole(queries, keys, values, lengths, order)


def solution(mesh):
    placed = (
        P(("dp", "seq"), None),
        P(("dp", "seq"), None),
        P(("dp", "seq"), None),
        P("dp"),
        P("dp"),
    )
    return jax.shard_map(
        shards, mesh=mesh, in_specs=placed, out_specs=P(("dp", "seq"), None), check_vma=False
    )
```

time: 315 us -> 102 us (0.32)
  local copies, waits for them, and re-layouts: 87.8 us -> 6.26 us
  waiting for transfers between devices: 107 us -> 31.4 us
  blocking collectives: 52 us -> 0 us
  matrix products: 32.8 us -> 0 us
  Pallas kernels: 0 us -> 26.5 us
  starting transfers between devices: 14.7 us -> 36.7 us
  other arithmetic: 17.4 us -> 0 us
    all_to_all x3 -> x0, waiting for transfers between devices: 107 us -> none  [the longest x1 45.5 us: shards(): lax.all_to_all(wide_keys, 'seq', split_axis=1, concat_axis=0, tiled=True)]
    all_to_all x1 -> x0, blocking collectives: 52 us -> none  [shards(): lax.all_to_all(balanced_out, 'seq', split_axis=0, concat_axis=1, tiled=True)]
    ppermute x0 -> x23, starting transfers between devices: none -> 36.7 us  [the longest x10 26.2 us: swap_outer(): return lax.ppermute(a, both, outer)]
    dot_general x8 -> x0, matrix products: 32.8 us -> none  [the longest x4 17.2 us: one_block(): jnp.einsum('qgd,kgd->gqk', query_block, key_block, preferred_element_type...]
    ppermute x0 -> x23, waiting for transfers between devices: none -> 31.4 us  [the longest x10 23.6 us: swap_outer(): return lax.ppermute(a, both, outer)]
    pallas_call x0 -> x6, Pallas kernels: none -> 26.5 us  [the longest x3 20.7 us: attention(): pl.pallas_call(kernel, out_shape=shapes, in_specs=[smem, smem] + [hbm] *...]
    dynamic_slice x20 -> x0, local copies, waits for them, and re-layouts: 21.4 us -> none  [the longest x4 13.5 us: one_block(): lax.dynamic_slice_in_dim(pad_keys, row_start, QBLOCK + DOC_MOST, 0)]
    concatenate x3 -> x1, local copies, waits for them, and re-layouts: 15.1 us -> 0.02 us  [rows(): return jnp.concatenate(blocks, axis=0)]
  transfers between devices with their start and end apart: 3 -> 23, of which waited for: 3 -> 6; matrix products, arithmetic and copies ran while one was open for 12% -> 3% of each run, Pallas kernels for 0% -> 23%
where the time goes in v2:
time: 102 us; the launch traced here: 101 us
  starting transfers between devices  36.7 us (36%)
  waiting for transfers between devices  31.4 us (31%)
  Pallas kernels  26.5 us (26%)
  local copies, waits for them, and re-layouts  6.26 us (6%)
    ppermute x10, starting transfers between devices, swap_outer(): return lax.ppermute(a, both, outer)  26.2 us
    ppermute x10, waiting for transfers between devices, swap_outer(): return lax.ppermute(a, both, outer)  23.6 us
    pallas_call x3, Pallas kernels, attention(): pl.pallas_call(kernel, out_shape=shapes, in_specs=[smem, smem] + [hbm] *...  20.7 us
    ppermute x7, starting transfers between devices, swap_x(): return lax.ppermute(a, both, across)  10.4 us
    ppermute x7, waiting for transfers between devices, swap_x(): return lax.ppermute(a, both, across)  7.82 us
    pallas_call x3, Pallas kernels, split(): pl.pallas_call(kernel, out_shape=[jax.ShapeDtypeStruct((n, width), jnp.bf...  5.73 us
    unnamed x39, local copies, waits for them, and re-layouts  3.94 us
    dynamic_update_slice x3, local copies, waits for them, and re-layouts, short_shards(): wide = lax.dynamic_update_slice_in_dim(wide, block, column, 1)  2.27 us
  transfers between devices with their start and end apart: 23, of which 6 were waited for; matrix products, arithmetic and copies ran while one was open for 3% of the time, Pallas kernels for 23%

profile of v2, /device:TPU:0, one launch (start us, length us, event | category | flops | bytes accessed | tf_op | source)
XLA Modules:
  0.0 101.1 jit_solution(16504854871905438136)
XLA Ops:
  0.0 1.8 %split_t.1 = (bf16[256,512]{1,0:T(8,128)(2,1)}, bf16[256,512]{1,0:T(8,128)(2,1)}) custom-call(bf16[256,1024]{1,0:T(8,128)(2,1)} %refs_0_.6, bf16[256,1024]{1,0:T(8,128)(2,1)} %refs_1_.2), custom_call_target="tpu_custom_call" | custom-call | bytes 1048576 | tf_op jit(solution)/shard_map/split_t/pallas_call | solution.py:224
  1.9 1.8 %split_w.1 = (bf16[256,512]{1,0:T(8,128)(2,1)}, bf16[256,512]{1,0:T(8,128)(2,1)}) custom-call(bf16[256,1024]{1,0:T(8,128)(2,1)} %refs_0_.6, bf16[256,1024]{1,0:T(8,128)(2,1)} %refs_1_.2), custom_call_target="tpu_custom_call" | custom-call | bytes 1048576 | tf_op jit(solution)/shard_map/split_w/pallas_call | solution.py:224
  3.7 3.0 %collective-permute-start = (bf16[256,512]{1,0:T(8,128)(2,1)}, bf16[256,512]{1,0:T(8,128)(2,1)S(1)}, u32[]{:S(2)}, u32[]{:S(2)}) collective-permute-start(bf16[256,512]{1,0:T(8,128)(2,1)} %get-tuple-element.27), channel_id=1, source_target_pairs={{0,1},{1,0},{2,3},{3,2},{4,5},{5,4},{6,7},{7,6},{8,9},{9,8},{10,11... | collective-permute-start | bytes 786440 | tf_op jit(solution)/shard_map/ppermute | solution.py:319
  6.7 1.6 %collective-permute-start.10 = (bf16[256,512]{1,0:T(8,128)(2,1)}, bf16[256,512]{1,0:T(8,128)(2,1)S(1)}, u32[]{:S(2)}, u32[]{:S(2)}) collective-permute-start(bf16[256,512]{1,0:T(8,128)(2,1)} %get-tuple-element.21.refs_2_), channel_id=1, source_target_pairs={{0,2},{1,3},{2,0},{3,1},{4,6},{5,7},{6,4},{7,5},{8,10},{9,11},{10,... | collective-permute-start | bytes 786440 | tf_op jit(solution)/shard_map/ppermute | solution.py:322
  8.3 0.0 collective-permute-start.12
  8.3 0.5 collective-permute-start.9
  8.8 1.0 constant_dynamic-update-slice_fusion.1
  9.8 4.3 %collective-permute-done = bf16[256,512]{1,0:T(8,128)(2,1)S(1)} collective-permute-done((bf16[256,512]{1,0:T(8,128)(2,1)}, bf16[256,512]{1,0:T(8,128)(2,1)S(1)}, u32[]{:S(2)}, u32[]{:S(2)}) %collective-permute-start) | collective-permute-done | bytes 262176 | tf_op jit(solution)/shard_map/ppermute | solution.py:319
  14.1 2.2 %collective-permute-start.3 = (bf16[512,512]{1,0:T(8,128)(2,1)S(1)}, bf16[512,512]{1,0:T(8,128)(2,1)S(1)}, u32[]{:S(2)}, u32[]{:S(2)}) collective-permute-start(bf16[512,512]{1,0:T(8,128)(2,1)S(1)} %constant_dynamic-update-slice_fusion.refs_2_), channel_id=1, source_target_pairs={{0,2},{1,3},{2,0},{3,1},{4,6},{5,7},{6,4},{7,5},{8,10},{9,11},{10,... | collective-permute-start | bytes 1572872 | tf_op jit(solution)/shard_map/ppermute | solution.py:322
  16.3 2.1 %split_q.1 = (bf16[256,1024]{1,0:T(8,128)(2,1)}, bf16[256,1024]{1,0:T(8,128)(2,1)}) custom-call(bf16[256,4096]{1,0:T(8,128)(2,1)} %refs_0_.10), custom_call_target="tpu_custom_call" | custom-call | bytes 2097152 | tf_op jit(solution)/shard_map/split_q/pallas_call | solution.py:224
  18.4 0.1 collective-permute-start.14
  18.4 1.6 %collective-permute-start.1 = (bf16[256,1024]{1,0:T(8,128)(2,1)}, bf16[256,1024]{1,0:T(8,128)(2,1)S(1)}, u32[]{:S(2)}, u32[]{:S(2)}) collective-permute-start(bf16[256,1024]{1,0:T(8,128)(2,1)} %get-tuple-element.28), channel_id=1, source_target_pairs={{0,1},{1,0},{2,3},{3,2},{4,5},{5,4},{6,7},{7,6},{8,9},{9,8},{10,11... | collective-permute-start | bytes 1572872 | tf_op jit(solution)/shard_map/ppermute | solution.py:319
  20.0 3.1 %collective-permute-start.11 = (bf16[256,512]{1,0:T(8,128)(2,1)S(1)}, bf16[256,512]{1,0:T(8,128)(2,1)S(1)}, u32[]{:S(2)}, u32[]{:S(2)}) collective-permute-start(bf16[256,512]{1,0:T(8,128)(2,1)S(1)} %collective-permute-done.9.refs_3_), channel_id=1, source_target_pairs={{0,2},{1,3},{2,0},{3,1},{4,6},{5,7},{6,4},{7,5},{8,10},{9,11},{10,... | collective-permute-start | bytes 786440 | tf_op jit(solution)/shard_map/ppermute | solution.py:322
  23.1 0.0 collective-permute-done.12.refs_6_
  23.1 0.1 collective-permute-start.16
  23.2 0.0 collective-permute-start.13
  23.2 11.5 %collective-permute-done.11.refs_5_ = bf16[256,512]{1,0:T(8,128)(2,1)S(1)} collective-permute-done((bf16[256,512]{1,0:T(8,128)(2,1)S(1)}, bf16[256,512]{1,0:T(8,128)(2,1)S(1)}, u32[]{:S(2)}, u32[]{:S(2)}) %collective-permute-start.11) | collective-permute-done | bytes 262176 | tf_op jit(solution)/shard_map/ppermute | solution.py:322
  34.7 2.9 %collective-permute-done.16.refs_10_ = bf16[256,512]{1,0:T(8,128)(2,1)S(1)} collective-permute-done((bf16[256,512]{1,0:T(8,128)(2,1)S(1)}, bf16[256,512]{1,0:T(8,128)(2,1)S(1)}, u32[]{:S(2)}, u32[]{:S(2)}) %collective-permute-start.16) | collective-permute-done | bytes 262176 | tf_op jit(solution)/shard_map/ppermute | solution.py:322
  37.7 0.7 copy-done.12
  38.4 0.0 collective-permute-done.3.refs_3_
  38.4 0.0 collective-permute-done.13.refs_7_
  38.4 3.1 %collective-permute-start.18 = (bf16[256,512]{1,0:T(8,128)(2,1)S(1)}, bf16[256,512]{1,0:T(8,128)(2,1)S(1)}, u32[]{:S(2)}, u32[]{:S(2)}) collective-permute-start(bf16[256,512]{1,0:T(8,128)(2,1)S(1)} %collective-permute-done.14.refs_8_), channel_id=1, source_target_pairs={{0,2},{1,3},{2,0},{3,1},{4,6},{5,7},{6,4},{7,5},{8,10},{9,11},{10,... | collective-permute-start | bytes 786440 | tf_op jit(solution)/shard_map/ppermute | solution.py:322
  41.5 0.0 collective-permute-done.1.refs_1_
  41.5 0.1 collective-permute-start.17
  41.6 13.9 %collective-permute-start.19 = (bf16[256,512]{1,0:T(8,128)(2,1)S(1)}, bf16[256,512]{1,0:T(8,128)(2,1)}, u32[]{:S(2)}, u32[]{:S(2)}) collective-permute-start(bf16[256,512]{1,0:T(8,128)(2,1)S(1)} %collective-permute-done.15.refs_9_), channel_id=1, source_target_pairs={{0,2},{1,3},{2,0},{3,1},{4,6},{5,7},{6,4},{7,5},{8,10},{9,11},{10,... | collective-permute-start | bytes 786440 | tf_op jit(solution)/shard_map/ppermute | solution.py:322
  55.5 0.0 collective-permute-done.18.refs_12_
  55.5 1.6 %collective-permute-start.2 = (bf16[256,1024]{1,0:T(8,128)(2,1)}, bf16[256,1024]{1,0:T(8,128)(2,1)S(1)}, u32[]{:S(2)}, u32[]{:S(2)}) collective-permute-start(bf16[256,1024]{1,0:T(8,128)(2,1)} %get-tuple-element.29), channel_id=1, source_target_pairs={{0,1},{1,0},{2,3},{3,2},{4,5},{5,4},{6,7},{7,6},{8,9},{9,8},{10,11... | collective-permute-start | bytes 1572872 | tf_op jit(solution)/shard_map/ppermute | solution.py:319
  57.1 0.1 collective-permute-start.6
  57.2 0.0 collective-permute-done.17.refs_11_
  57.2 0.8 copy-done.16
  58.0 4.8 %collective-permute-done.19.refs_13_ = bf16[256,512]{1,0:T(8,128)(2,1)} collective-permute-done((bf16[256,512]{1,0:T(8,128)(2,1)S(1)}, bf16[256,512]{1,0:T(8,128)(2,1)}, u32[]{:S(2)}, u32[]{:S(2)}) %collective-permute-start.19) | collective-permute-done | bytes 262176 | tf_op jit(solution)/shard_map/ppermute | solution.py:322
  62.8 8.4 %attention_t.1 = (bf16[256,1024]{1,0:T(8,128)(2,1)}, bf16[256,4096]{1,0:T(8,128)(2,1)}) custom-call(s32[8]{0:T(128)} %lengths.5, s32[32]{0:T(128)} %order.5, bf16[256,4096]{1,0:T(8,128)(2,1)} %refs_0_.10, bf16[256,1024]{1,0:T(8,128)(2,1)} %copy-done.6, bf16[256,512]{1,0:T(8,128)(2,1)} %get-tuple-element.21.refs_2_, bf16[256,512]{1,0:T(8,128)(2,1)} %copy-done.9, ...), custom_call_target="tpu_custom_call" | custom-call | flops 1258291200 | bytes 2097152 | tf_op jit(solution)/shard_map/attention_t/pallas_call | solution.py:176
  71.3 1.6 %collective-permute-start.20 = (bf16[256,1024]{1,0:T(8,128)(2,1)}, bf16[256,1024]{1,0:T(8,128)(2,1)S(1)}, u32[]{:S(2)}, u32[]{:S(2)}) collective-permute-start(bf16[256,1024]{1,0:T(8,128)(2,1)} %get-tuple-element.34), channel_id=1, source_target_pairs={{0,1},{1,0},{2,3},{3,2},{4,5},{5,4},{6,7},{7,6},{8,9},{9,8},{10,11... | collective-permute-start | bytes 1572872 | tf_op jit(solution)/shard_map/ppermute | solution.py:319
  72.9 1.6 %collective-permute-start.8 = (bf16[512,256]{1,0:T(8,128)(2,1)S(1)}, bf16[512,256]{1,0:T(8,128)(2,1)S(1)}, u32[]{:S(2)}, u32[]{:S(2)}) collective-permute-start(bf16[512,256]{1,0:T(8,128)(2,1)S(1)} %get-tuple-element.37), channel_id=1, source_target_pairs={{0,2},{1,3},{2,0},{3,1},{4,6},{5,7},{6,4},{7,5},{8,10},{9,11},{10,... | collective-permute-start | bytes 786440 | tf_op jit(solution)/shard_map/ppermute | solution.py:322
  74.5 0.5 collective-permute-start.7
  75.0 4.3 %collective-permute-done.8.refs_7_ = bf16[512,256]{1,0:T(8,128)(2,1)S(1)} collective-permute-done((bf16[512,256]{1,0:T(8,128)(2,1)S(1)}, bf16[512,256]{1,0:T(8,128)(2,1)S(1)}, u32[]{:S(2)}, u32[]{:S(2)}) %collective-permute-start.8) | collective-permute-done | bytes 262176 | tf_op jit(solution)/shard_map/ppermute | solution.py:322
  79.4 0.7 copy-done.18
  80.1 6.1 %attention_2.1 = (bf16[256,512]{1,0:T(8,128)(2,1)}, bf16[256,4096]{1,0:T(8,128)(2,1)}) custom-call(s32[8]{0:T(128)} %lengths.5, s32[32]{0:T(128)} %order.5, bf16[256,4096]{1,0:T(8,128)(2,1)} %refs_0_.10, bf16[256,1024]{1,0:T(8,128)(2,1)} %copy-done.4, bf16[512,512]{1,0:T(8,128)(2,1)} %copy-done.1, ...), custom_call_target="tpu_custom_call", output_to_operand_aliasing={{1}: (10, {})} | custom-call | flops 629145600 | bytes 1048576 | tf_op jit(solution)/shard_map/attention_2/pallas_call | solution.py:176
  86.2 0.6 collective-permute-start.21
  86.8 0.0 collective-permute-done.7.refs_7_
  86.8 0.7 copy-done.17
  87.6 6.1 %attention_3.1 = (bf16[256,512]{1,0:T(8,128)(2,1)}, bf16[256,4096]{1,0:T(8,128)(2,1)}) custom-call(s32[8]{0:T(128)} %lengths.5, s32[32]{0:T(128)} %order.5, bf16[256,4096]{1,0:T(8,128)(2,1)} %refs_0_.10, bf16[256,1024]{1,0:T(8,128)(2,1)} %copy-done.4, bf16[512,512]{1,0:T(8,128)(2,1)} %copy-done.1, ...), custom_call_target="tpu_custom_call", output_to_operand_aliasing={{1}: (10, {})} | custom-call | flops 629145600 | bytes 1048576 | tf_op jit(solution)/shard_map/attention_3/pallas_call | solution.py:176
  93.7 1.5 %collective-permute-start.22 = (bf16[256,512]{1,0:T(8,128)(2,1)}, bf16[256,512]{1,0:T(8,128)(2,1)S(1)}, u32[]{:S(2)}, u32[]{:S(2)}) collective-permute-start(bf16[256,512]{1,0:T(8,128)(2,1)} %get-tuple-element.36), channel_id=1, source_target_pairs={{0,1},{1,0},{2,3},{3,2},{4,5},{5,4},{6,7},{7,6},{8,9},{9,8},{10,11... | collective-permute-start | bytes 786440 | tf_op jit(solution)/shard_map/ppermute | solution.py:319
  95.3 0.8 constant_dynamic-update-slice_fusion.4
  96.1 0.0 collective-permute-done.21
  96.1 0.7 constant_dynamic-update-slice_fusion.3
  96.8 3.5 %collective-permute-done.22 = bf16[256,512]{1,0:T(8,128)(2,1)S(1)} collective-permute-done((bf16[256,512]{1,0:T(8,128)(2,1)}, bf16[256,512]{1,0:T(8,128)(2,1)S(1)}, u32[]{:S(2)}, u32[]{:S(2)}) %collective-permute-start.22) | collective-permute-done | bytes 262176 | tf_op jit(solution)/shard_map/ppermute | solution.py:319
  100.4 0.7 constant_dynamic-update-slice_fusion.2
  (48 shorter events, 0.1 us)
Async XLA Ops:
  3.7 10.3 %collective-permute-start = (bf16[256,512]{1,0:T(8,128)(2,1)}, bf16[256,512]{1,0:T(8,128)(2,1)S(1)}, u32[]{:S(2)}, u32[]{:S(2)}) collective-permute-start(bf16[256,512]{1,0:T(8,128)(2,1)} %get-tuple-element.27), channel_id=1, source_target_pairs={{0,1},{1,0},{2,3},{3,2},{4,5},{5,4},{6,7},{7,6},{8,9},{9,8},{10,11... | collective-permute-start | bytes 786440 | tf_op jit(solution)/shard_map/ppermute | solution.py:319
  6.7 11.7 %collective-permute-start.10 = (bf16[256,512]{1,0:T(8,128)(2,1)}, bf16[256,512]{1,0:T(8,128)(2,1)S(1)}, u32[]{:S(2)}, u32[]{:S(2)}) collective-permute-start(bf16[256,512]{1,0:T(8,128)(2,1)} %get-tuple-element.21.refs_2_), channel_id=1, source_target_pairs={{0,2},{1,3},{2,0},{3,1},{4,6},{5,7},{6,4},{7,5},{8,10},{9,11},{10,... | collective-permute-start | bytes 786440 | tf_op jit(solution)/shard_map/ppermute | solution.py:322
  8.3 14.8 %collective-permute-start.12 = (bf16[256,512]{1,0:T(8,128)(2,1)}, bf16[256,512]{1,0:T(8,128)(2,1)S(1)}, u32[]{:S(2)}, u32[]{:S(2)}) collective-permute-start(bf16[256,512]{1,0:T(8,128)(2,1)} %get-tuple-element.21.refs_2_), channel_id=1, source_target_pairs={{2,4},{3,5},{4,2},{5,3},{10,12},{11,13},{12,10},{13,11},{18,20},{1... | collective-permute-start | bytes 786440 | tf_op jit(solution)/shard_map/ppermute | solution.py:325
  8.3 11.7 %collective-permute-start.9 = (bf16[256,512]{1,0:T(8,128)(2,1)}, bf16[256,512]{1,0:T(8,128)(2,1)S(1)}, u32[]{:S(2)}, u32[]{:S(2)}) collective-permute-start(bf16[256,512]{1,0:T(8,128)(2,1)} %get-tuple-element.30), channel_id=1, source_target_pairs={{0,1},{1,0},{2,3},{3,2},{4,5},{5,4},{6,7},{7,6},{8,9},{9,8},{10,11... | collective-permute-start | bytes 786440 | tf_op jit(solution)/shard_map/ppermute | solution.py:319
  14.1 57.2 %copy-start.1 = (bf16[512,512]{1,0:T(8,128)(2,1)}, bf16[512,512]{1,0:T(8,128)(2,1)S(1)}, u32[]{:S(2)}) copy-start(bf16[512,512]{1,0:T(8,128)(2,1)S(1)} %constant_dynamic-update-slice_fusion.refs_2_) | copy-start | bytes 1572868
  14.1 24.3 %collective-permute-start.3 = (bf16[512,512]{1,0:T(8,128)(2,1)S(1)}, bf16[512,512]{1,0:T(8,128)(2,1)S(1)}, u32[]{:S(2)}, u32[]{:S(2)}) collective-permute-start(bf16[512,512]{1,0:T(8,128)(2,1)S(1)} %constant_dynamic-update-slice_fusion.refs_2_), channel_id=1, source_target_pairs={{0,2},{1,3},{2,0},{3,1},{4,6},{5,7},{6,4},{7,5},{8,10},{9,11},{10,... | collective-permute-start | bytes 1572872 | tf_op jit(solution)/shard_map/ppermute | solution.py:322
  18.4 44.5 %copy-start.7 = (bf16[256,512]{1,0:T(8,128)(2,1)}, bf16[256,512]{1,0:T(8,128)(2,1)S(1)}, u32[]{:S(2)}) copy-start(bf16[256,512]{1,0:T(8,128)(2,1)S(1)} %collective-permute-done.10.refs_4_) | copy-start | bytes 786436
  18.4 4.8 %collective-permute-start.14 = (bf16[256,512]{1,0:T(8,128)(2,1)S(1)}, bf16[256,512]{1,0:T(8,128)(2,1)S(1)}, u32[]{:S(2)}, u32[]{:S(2)}) collective-permute-start(bf16[256,512]{1,0:T(8,128)(2,1)S(1)} %collective-permute-done.10.refs_4_), channel_id=1, source_target_pairs={{2,4},{3,5},{4,2},{5,3},{10,12},{11,13},{12,10},{13,11},{18,20},{1... | collective-permute-start | bytes 786440 | tf_op jit(solution)/shard_map/ppermute | solution.py:325
  18.4 23.0 %collective-permute-start.1 = (bf16[256,1024]{1,0:T(8,128)(2,1)}, bf16[256,1024]{1,0:T(8,128)(2,1)S(1)}, u32[]{:S(2)}, u32[]{:S(2)}) collective-permute-start(bf16[256,1024]{1,0:T(8,128)(2,1)} %get-tuple-element.28), channel_id=1, source_target_pairs={{0,1},{1,0},{2,3},{3,2},{4,5},{5,4},{6,7},{7,6},{8,9},{9,8},{10,11... | collective-permute-start | bytes 1572872 | tf_op jit(solution)/shard_map/ppermute | solution.py:319
  20.0 35.5 %copy-start.9 = (bf16[256,512]{1,0:T(8,128)(2,1)}, bf16[256,512]{1,0:T(8,128)(2,1)S(1)}, u32[]{:S(2)}) copy-start(bf16[256,512]{1,0:T(8,128)(2,1)S(1)} %collective-permute-done.9.refs_3_) | copy-start | bytes 786436
  20.0 14.7 %collective-permute-start.11 = (bf16[256,512]{1,0:T(8,128)(2,1)S(1)}, bf16[256,512]{1,0:T(8,128)(2,1)S(1)}, u32[]{:S(2)}, u32[]{:S(2)}) collective-permute-start(bf16[256,512]{1,0:T(8,128)(2,1)S(1)} %collective-permute-done.9.refs_3_), channel_id=1, source_target_pairs={{0,2},{1,3},{2,0},{3,1},{4,6},{5,7},{6,4},{7,5},{8,10},{9,11},{10,... | collective-permute-start | bytes 786440 | tf_op jit(solution)/shard_map/ppermute | solution.py:322
  23.1 14.6 %copy-start.8 = (bf16[256,512]{1,0:T(8,128)(2,1)}, bf16[256,512]{1,0:T(8,128)(2,1)S(1)}, u32[]{:S(2)}) copy-start(bf16[256,512]{1,0:T(8,128)(2,1)S(1)} %collective-permute-done.12.refs_6_) | copy-start | bytes 786436
  23.1 14.6 %collective-permute-start.16 = (bf16[256,512]{1,0:T(8,128)(2,1)S(1)}, bf16[256,512]{1,0:T(8,128)(2,1)S(1)}, u32[]{:S(2)}, u32[]{:S(2)}) collective-permute-start(bf16[256,512]{1,0:T(8,128)(2,1)S(1)} %collective-permute-done.12.refs_6_), channel_id=1, source_target_pairs={{0,2},{1,3},{2,0},{3,1},{4,6},{5,7},{6,4},{7,5},{8,10},{9,11},{10,... | collective-permute-start | bytes 786440 | tf_op jit(solution)/shard_map/ppermute | solution.py:322
  23.2 32.3 %copy-start.10 = (bf16[256,512]{1,0:T(8,128)(2,1)}, bf16[256,512]{1,0:T(8,128)(2,1)S(1)}, u32[]{:S(2)}) copy-start(bf16[256,512]{1,0:T(8,128)(2,1)S(1)} %collective-permute-done.14.refs_8_) | copy-start | bytes 786436
  23.2 15.2 %collective-permute-start.13 = (bf16[256,512]{1,0:T(8,128)(2,1)S(1)}, bf16[256,512]{1,0:T(8,128)(2,1)S(1)}, u32[]{:S(2)}, u32[]{:S(2)}) collective-permute-start(bf16[256,512]{1,0:T(8,128)(2,1)S(1)} %collective-permute-done.9.refs_3_), channel_id=1, source_target_pairs={{2,4},{3,5},{4,2},{5,3},{10,12},{11,13},{12,10},{13,11},{18,20},{1... | collective-permute-start | bytes 786440 | tf_op jit(solution)/shard_map/ppermute | solution.py:325
  34.7 22.3 %copy-start.11 = (bf16[256,512]{1,0:T(8,128)(2,1)}, bf16[256,512]{1,0:T(8,128)(2,1)S(1)}, u32[]{:S(2)}) copy-start(bf16[256,512]{1,0:T(8,128)(2,1)S(1)} %collective-permute-done.11.refs_5_) | copy-start | bytes 786436
  34.7 22.4 %collective-permute-start.4 = (bf16[512,512]{1,0:T(8,128)(2,1)S(1)}, bf16[512,512]{1,0:T(8,128)(2,1)S(1)}, u32[]{:S(2)}, u32[]{:S(2)}) collective-permute-start(bf16[512,512]{1,0:T(8,128)(2,1)S(1)} %constant_dynamic-update-slice_fusion.refs_2_), channel_id=1, source_target_pairs={{2,4},{3,5},{4,2},{5,3},{10,12},{11,13},{12,10},{13,11},{18,20},{1... | collective-permute-start | bytes 1572872 | tf_op jit(solution)/shard_map/ppermute | solution.py:325
  37.6 0.7 copy-start.12
  37.6 3.9 %collective-permute-start.15 = (bf16[256,512]{1,0:T(8,128)(2,1)S(1)}, bf16[256,512]{1,0:T(8,128)(2,1)S(1)}, u32[]{:S(2)}, u32[]{:S(2)}) collective-permute-start(bf16[256,512]{1,0:T(8,128)(2,1)S(1)} %collective-permute-done.11.refs_5_), channel_id=1, source_target_pairs={{2,4},{3,5},{4,2},{5,3},{10,12},{11,13},{12,10},{13,11},{18,20},{1... | collective-permute-start | bytes 786440 | tf_op jit(solution)/shard_map/ppermute | solution.py:325
  38.4 32.9 %copy-start.2 = (bf16[512,512]{1,0:T(8,128)(2,1)}, bf16[512,512]{1,0:T(8,128)(2,1)S(1)}, u32[]{:S(2)}) copy-start(bf16[512,512]{1,0:T(8,128)(2,1)S(1)} %collective-permute-done.3.refs_3_) | copy-start | bytes 1572868
  38.4 34.5 %collective-permute-start.5 = (bf16[512,512]{1,0:T(8,128)(2,1)S(1)}, bf16[512,512]{1,0:T(8,128)(2,1)S(1)}, u32[]{:S(2)}, u32[]{:S(2)}) collective-permute-start(bf16[512,512]{1,0:T(8,128)(2,1)S(1)} %collective-permute-done.3.refs_3_), channel_id=1, source_target_pairs={{2,4},{3,5},{4,2},{5,3},{10,12},{11,13},{12,10},{13,11},{18,20},{1... | collective-permute-start | bytes 1572872 | tf_op jit(solution)/shard_map/ppermute | solution.py:325
  38.4 18.7 %copy-start.13 = (bf16[256,512]{1,0:T(8,128)(2,1)}, bf16[256,512]{1,0:T(8,128)(2,1)S(1)}, u32[]{:S(2)}) copy-start(bf16[256,512]{1,0:T(8,128)(2,1)S(1)} %collective-permute-done.13.refs_7_) | copy-start | bytes 786436
  38.4 17.1 %collective-permute-start.18 = (bf16[256,512]{1,0:T(8,128)(2,1)S(1)}, bf16[256,512]{1,0:T(8,128)(2,1)S(1)}, u32[]{:S(2)}, u32[]{:S(2)}) collective-permute-start(bf16[256,512]{1,0:T(8,128)(2,1)S(1)} %collective-permute-done.14.refs_8_), channel_id=1, source_target_pairs={{0,2},{1,3},{2,0},{3,1},{4,6},{5,7},{6,4},{7,5},{8,10},{9,11},{10,... | collective-permute-start | bytes 786440 | tf_op jit(solution)/shard_map/ppermute | solution.py:322
  41.5 21.4 %copy-start.6 = (bf16[256,1024]{1,0:T(8,128)(2,1)}, bf16[256,1024]{1,0:T(8,128)(2,1)S(1)}, u32[]{:S(2)}) copy-start(bf16[256,1024]{1,0:T(8,128)(2,1)S(1)} %collective-permute-done.1.refs_1_) | copy-start | bytes 1572868
  41.5 15.7 %collective-permute-start.17 = (bf16[256,512]{1,0:T(8,128)(2,1)S(1)}, bf16[256,512]{1,0:T(8,128)(2,1)S(1)}, u32[]{:S(2)}, u32[]{:S(2)}) collective-permute-start(bf16[256,512]{1,0:T(8,128)(2,1)S(1)} %collective-permute-done.13.refs_7_), channel_id=1, source_target_pairs={{0,2},{1,3},{2,0},{3,1},{4,6},{5,7},{6,4},{7,5},{8,10},{9,11},{10,... | collective-permute-start | bytes 786440 | tf_op jit(solution)/shard_map/ppermute | solution.py:322
  41.6 15.6 %copy-start.14 = (bf16[256,512]{1,0:T(8,128)(2,1)}, bf16[256,512]{1,0:T(8,128)(2,1)S(1)}, u32[]{:S(2)}) copy-start(bf16[256,512]{1,0:T(8,128)(2,1)S(1)} %collective-permute-done.15.refs_9_) | copy-start | bytes 786436
  41.6 21.3 %collective-permute-start.19 = (bf16[256,512]{1,0:T(8,128)(2,1)S(1)}, bf16[256,512]{1,0:T(8,128)(2,1)}, u32[]{:S(2)}, u32[]{:S(2)}) collective-permute-start(bf16[256,512]{1,0:T(8,128)(2,1)S(1)} %collective-permute-done.15.refs_9_), channel_id=1, source_target_pairs={{0,2},{1,3},{2,0},{3,1},{4,6},{5,7},{6,4},{7,5},{8,10},{9,11},{10,... | collective-permute-start | bytes 786440 | tf_op jit(solution)/shard_map/ppermute | solution.py:322
  55.5 1.6 %copy-start.15 = (bf16[256,512]{1,0:T(8,128)(2,1)}, bf16[256,512]{1,0:T(8,128)(2,1)S(1)}, u32[]{:S(2)}) copy-start(bf16[256,512]{1,0:T(8,128)(2,1)S(1)} %collective-permute-done.18.refs_12_) | copy-start | bytes 786436
  55.5 19.5 %collective-permute-start.2 = (bf16[256,1024]{1,0:T(8,128)(2,1)}, bf16[256,1024]{1,0:T(8,128)(2,1)S(1)}, u32[]{:S(2)}, u32[]{:S(2)}) collective-permute-start(bf16[256,1024]{1,0:T(8,128)(2,1)} %get-tuple-element.29), channel_id=1, source_target_pairs={{0,1},{1,0},{2,3},{3,2},{4,5},{5,4},{6,7},{7,6},{8,9},{9,8},{10,11... | collective-permute-start | bytes 1572872 | tf_op jit(solution)/shard_map/ppermute | solution.py:319
  57.1 14.2 %copy-start.3 = (bf16[512,512]{1,0:T(8,128)(2,1)}, bf16[512,512]{1,0:T(8,128)(2,1)S(1)}, u32[]{:S(2)}) copy-start(bf16[512,512]{1,0:T(8,128)(2,1)S(1)} %collective-permute-done.4.refs_4_) | copy-start | bytes 1572868
  57.1 17.9 %collective-permute-start.6 = (bf16[512,512]{1,0:T(8,128)(2,1)S(1)}, bf16[512,512]{1,0:T(8,128)(2,1)S(1)}, u32[]{:S(2)}, u32[]{:S(2)}) collective-permute-start(bf16[512,512]{1,0:T(8,128)(2,1)S(1)} %collective-permute-done.4.refs_4_), channel_id=1, source_target_pairs={{0,2},{1,3},{2,0},{3,1},{4,6},{5,7},{6,4},{7,5},{8,10},{9,11},{10,... | collective-permute-start | bytes 1572872 | tf_op jit(solution)/shard_map/ppermute | solution.py:322
  57.2 0.8 copy-start.16
  71.3 24.0 %collective-permute-start.20 = (bf16[256,1024]{1,0:T(8,128)(2,1)}, bf16[256,1024]{1,0:T(8,128)(2,1)S(1)}, u32[]{:S(2)}, u32[]{:S(2)}) collective-permute-start(bf16[256,1024]{1,0:T(8,128)(2,1)} %get-tuple-element.34), channel_id=1, source_target_pairs={{0,1},{1,0},{2,3},{3,2},{4,5},{5,4},{6,7},{7,6},{8,9},{9,8},{10,11... | collective-permute-start | bytes 1572872 | tf_op jit(solution)/shard_map/ppermute | solution.py:319
  72.9 6.5 %copy-start = (bf16[512,512]{1,0:T(8,128)(2,1)}, bf16[512,512]{1,0:T(8,128)(2,1)S(1)}, u32[]{:S(2)}) copy-start(bf16[512,512]{1,0:T(8,128)(2,1)S(1)} %collective-permute-done.5.refs_5_) | copy-start | bytes 1572868
  72.9 6.4 %collective-permute-start.8 = (bf16[512,256]{1,0:T(8,128)(2,1)S(1)}, bf16[512,256]{1,0:T(8,128)(2,1)S(1)}, u32[]{:S(2)}, u32[]{:S(2)}) collective-permute-start(bf16[512,256]{1,0:T(8,128)(2,1)S(1)} %get-tuple-element.37), channel_id=1, source_target_pairs={{0,2},{1,3},{2,0},{3,1},{4,6},{5,7},{6,4},{7,5},{8,10},{9,11},{10,... | collective-permute-start | bytes 786440 | tf_op jit(solution)/shard_map/ppermute | solution.py:322
  74.5 12.3 %collective-permute-start.7 = (bf16[512,256]{1,0:T(8,128)(2,1)S(1)}, bf16[512,256]{1,0:T(8,128)(2,1)S(1)}, u32[]{:S(2)}, u32[]{:S(2)}) collective-permute-start(bf16[512,256]{1,0:T(8,128)(2,1)S(1)} %get-tuple-element.38), channel_id=1, source_target_pairs={{0,2},{1,3},{2,0},{3,1},{4,6},{5,7},{6,4},{7,5},{8,10},{9,11},{10,... | collective-permute-start | bytes 786440 | tf_op jit(solution)/shard_map/ppermute | solution.py:322
  75.0 4.3 %copy-start.4 = (bf16[256,1024]{1,0:T(8,128)(2,1)}, bf16[256,1024]{1,0:T(8,128)(2,1)S(1)}, u32[]{:S(2)}) copy-start(bf16[256,1024]{1,0:T(8,128)(2,1)S(1)} %collective-permute-done.2.refs_1_) | copy-start | bytes 1572868
  75.0 4.3 %copy-start.5 = (bf16[512,512]{1,0:T(8,128)(2,1)}, bf16[512,512]{1,0:T(8,128)(2,1)S(1)}, u32[]{:S(2)}) copy-start(bf16[512,512]{1,0:T(8,128)(2,1)S(1)} %collective-permute-done.6.refs_6_) | copy-start | bytes 1572868
  79.3 0.7 copy-start.18
  86.2 9.9 %collective-permute-start.21 = (bf16[256,512]{1,0:T(8,128)(2,1)}, bf16[256,512]{1,0:T(8,128)(2,1)S(1)}, u32[]{:S(2)}, u32[]{:S(2)}) collective-permute-start(bf16[256,512]{1,0:T(8,128)(2,1)} %get-tuple-element.35), channel_id=1, source_target_pairs={{0,1},{1,0},{2,3},{3,2},{4,5},{5,4},{6,7},{7,6},{8,9},{9,8},{10,11... | collective-permute-start | bytes 786440 | tf_op jit(solution)/shard_map/ppermute | solution.py:319
  86.8 0.7 copy-start.17
  93.7 6.6 %collective-permute-start.22 = (bf16[256,512]{1,0:T(8,128)(2,1)}, bf16[256,512]{1,0:T(8,128)(2,1)S(1)}, u32[]{:S(2)}, u32[]{:S(2)}) collective-permute-start(bf16[256,512]{1,0:T(8,128)(2,1)} %get-tuple-element.36), channel_id=1, source_target_pairs={{0,1},{1,0},{2,3},{3,2},{4,5},{5,4},{6,7},{7,6},{8,9},{9,8},{10,11... | collective-permute-start | bytes 786440 | tf_op jit(solution)/shard_map/ppermute | solution.py:319

commit v3 on v2

--- a/solution.py
+++ b/solution.py
@@ -17,8 +17,10 @@
 MOST_STEPS = -(-(DOC_MOST + BLOCK) // KEY_STEP)
 EXP_SCALE = HEAD_DIM**-0.5 * math.log2(math.e)
 GQ = GROUP * HEAD_DIM
+COST = {1: 0.3, 2: 1}
 VMEM_BYTES = 60 * 1024 * 1024
-COUNTS = tuple(range(1, MOST_STEPS + 1))
+WHOLE_VMEM = 64 * 1024 * 1024
+COUNTS = (2, 4, 6, MOST_STEPS)
 TOGETHER = {1: 2, 2: 2}
 
 
@@ -168,7 +170,7 @@
 
     smem = pl.BlockSpec(memory_space=pltpu.SMEM)
     hbm = pl.BlockSpec(memory_space=pl.ANY)
-    pairs = blocks * rows_here * heads * GROUP * 600
+    pairs = int(100 * blocks * rows_here * heads * GROUP * 6 * COST[heads])
     shapes = [jax.ShapeDtypeStruct((rows_here, q_width), jnp.bfloat16)] * blocks
     if column is not None:
         shapes[-1] = jax.ShapeDtypeStruct((rows_here, HEADS * HEAD_DIM), jnp.bfloat16)
@@ -194,12 +196,12 @@
     )(lengths, order, *arrays, *given)
 
 
-def split(name, arrays, widths, plan):
+def split(name, arrays, widths, plan, others=()):
     n, count = arrays[0].shape[0], len(widths)
 
     def kernel(*refs):
-        inputs, outs = refs[: len(arrays)], refs[len(arrays) : len(arrays) + count]
-        held, sems, sem_out = refs[len(arrays) + count : -2], refs[-2], refs[-1]
+        inputs, outs = refs[: len(arrays)], refs[-2 - 2 * count : -2 - count]
+        held, sems, sem_out = refs[-2 - count : -2], refs[-2], refs[-1]
         pair = lax.axis_index("seq") % 2
 
         def ins(o):
@@ -224,14 +226,14 @@
     return pl.pallas_call(
         kernel,
         out_shape=[jax.ShapeDtypeStruct((n, width), jnp.bfloat16) for width in widths],
-        in_specs=[hbm] * len(arrays),
+        in_specs=[hbm] * (len(arrays) + len(others)),
         out_specs=[hbm] * count,
         scratch_shapes=[pltpu.VMEM((n, width), jnp.bfloat16) for width in widths]
         + [pltpu.SemaphoreType.DMA((count,)), pltpu.SemaphoreType.DMA],
         compiler_params=pltpu.CompilerParams(vmem_limit_bytes=VMEM_BYTES),
         cost_estimate=pl.CostEstimate(flops=0, bytes_accessed=4 * n * sum(widths), transcendentals=0),
         name=name,
-    )(*arrays)
+    )(*arrays, *others)
 
 
 def columns(array, first, size):
@@ -297,8 +299,19 @@
     return assemble(pair, mine, theirs)
 
 
-def after(array, *others):
-    return lax.optimization_barrier((array,) + others)[0]
+def hold(arrays, others=(), token=False):
+    count = len(arrays)
+    hbm = pl.BlockSpec(memory_space=pl.ANY)
+    return pl.pallas_call(
+        lambda *refs: None,
+        out_shape=[jax.ShapeDtypeStruct(array.shape, array.dtype) for array in arrays]
+        + [jax.ShapeDtypeStruct((16, 128), jnp.bfloat16)] * token,
+        in_specs=[hbm] * (count + len(others)),
+        out_specs=[hbm] * (count + token),
+        input_output_aliases={i: i for i in range(count)},
+        compiler_params=pltpu.CompilerParams(vmem_limit_bytes=WHOLE_VMEM),
+        name="hold",
+    )(*arrays, *others)
 
 
 def short_shards(queries, keys, values, lengths, order):
@@ -310,10 +323,9 @@
     def permutation(links):
         return [(8 * d + 2 * a + x, 8 * d + 2 * b + x) for d in range(parts) for a, b in links for x in range(2)]
 
-    outer = permutation([(0, 1), (1, 0), (2, 3), (3, 2)])
-    inner = permutation([(1, 2), (2, 1)])
-    inner += [(8 * d + 2 * z + x, 8 * (d ^ 1) + 2 * z + x) for d in range(parts) for z in (0, 3) for x in range(2)]
     across = [(8 * d + i, 8 * d + (i ^ 1)) for d in range(parts) for i in range(8)]
+    outer = permutation([(z, z ^ 1) for z in range(4)])
+    ends = permutation([(z, z ^ 3) for z in range(4)])
 
     def swap_x(a):
         return lax.ppermute(a, both, across)
@@ -321,57 +333,43 @@
     def swap_outer(a):
         return lax.ppermute(a, both, outer)
 
-    def swap_inner(a):
-        return lax.ppermute(a, both, inner)
+    def swap_ends(a):
+        return lax.ppermute(a, both, ends)
 
     def rows(*blocks):
         return jnp.concatenate(blocks, axis=0)
 
-    def middle(place):
-        return (place == 1) | (place == 2)
-
-    def end(place):
-        return jnp.logical_not(middle(place))
-
     def near(place):
         return place + 1 - 2 * (place % 2)
 
     one, two = HEAD_DIM, 2 * HEAD_DIM
     kv_half, q_half = KV_HALF * HEAD_DIM, KV_HALF * GQ
 
-    def t_plan(pair):
-        return [[(a, half * kv_half, two) for a in range(2)] for half in (pair, 1 - pair)]
-
-    def w_plan(pair):
-        return [
+    def kv_plan(pair):
+        t = [[(a, half * kv_half, two) for a in range(2)] for half in (pair, 1 - pair)]
+        w = [
             [(a, half * kv_half + head * one, one) for head in (2, 3) for a in range(2)] for half in (pair, 1 - pair)
         ]
+        return t + w
 
     def q_plan(pair):
         return [[(0, (1 - pair) * q_half + i * 2 * GQ, 2 * GQ)] for i in range(2)]
 
-    t_own, t_send = split("split_t", [keys, values], [2 * two] * 2, t_plan)
+    t_own, t_send, w_own, w_send = split("split_kv", [keys, values], [2 * two] * 4, kv_plan)
     t_par = swap_x(t_send)
-    t_near_own = swap_outer(t_own)
-    t_in_own = swap_inner(t_own)
-    w_own, w_send = split("split_w", [keys, after(values, t_own)], [2 * two] * 2, w_plan)
+    t_near_own, t_far_own = swap_outer(t_own), swap_ends(t_own)
     w_par = swap_x(w_send)
-    qt_send, qw_send = split("split_q", [after(queries, w_own)], [2 * GQ] * 2, q_plan)
-    t_near_par = swap_outer(t_par)
-    t_in_par = swap_inner(t_par)
-    w_shard = rows(w_own, w_par)
-    qt_par = swap_x(after(qt_send, w_par))
-    t_far_own = swap_inner(t_near_own)
-    t_out_own = swap_outer(t_in_own)
-    t_far_par = swap_inner(t_near_par)
-    t_out_par = swap_outer(t_in_par)
-    w_near = swap_outer(w_shard)
-    w_in = swap_inner(w_shard)
-    qw_par = swap_x(after(qw_send, qt_par))
-    t_out_far_own = swap_outer(t_far_own)
-    t_out_far_par = swap_outer(t_far_par)
-    w_out = swap_outer(w_in)
-    w_far = swap_inner(w_near)
+    t_near_par, t_far_par = swap_outer(t_par), swap_ends(t_par)
+    t_out_own = swap_outer(t_far_own)
+    qt_send, qw_send = split("split_q", [queries], [2 * GQ] * 2, q_plan, [w_par])
+    qt_par, qw_par = swap_x(qt_send), swap_x(qw_send)
+    t_out_par = swap_outer(t_far_par)
+    (u_shard,) = hold([rows(w_own[:, :two], w_par[:, :two])], [t_far_par])
+    v_shard = rows(w_own[:, two:], w_par[:, two:])
+    u_far = swap_ends(u_shard)
+    u_near, u_out = swap_outer(u_shard), swap_outer(u_far)
+    v_far = swap_ends(v_shard)
+    v_near, v_out = swap_outer(v_shard), swap_outer(v_far)
 
     def each_half(plan):
         def full(place, pair):
@@ -390,10 +388,8 @@
         return [
             (None, 2 + half, 0, 0, place),
             (None, 4 + half, 0, 0, near(place)),
-            (middle(place), 6 + half, 0, 0, 3 - place),
-            (middle(place), 8 + half, 0, 0, 3 - near(place)),
-            (end(place), 10 + half, 0, 0, 3 - near(place)),
-            (end(place), 12 + half, 0, 0, 3 - place),
+            (None, 6 + half, 0, 0, 3 - place),
+            (None, 8 + half, 0, 0, 3 - near(place)),
         ]
 
     t_other, wide = attention(
@@ -401,48 +397,63 @@
         2,
         lengths,
         order,
-        [queries, qt_par, t_own, t_par, t_near_own, t_near_par, t_in_own, t_in_par]
-        + [t_far_own, t_far_par, t_out_own, t_out_par, t_out_far_own, t_out_far_par],
+        [queries, qt_par, t_own, t_par, t_near_own, t_near_par, t_far_own, t_far_par, t_out_own, t_out_par],
         t_queries,
         each_half(t_keys),
         column=lambda pair: pair * q_half,
     )
     t_theirs = swap_x(t_other)
 
-    mine, theirs = pair * q_half, (1 - pair) * q_half
-    blocks = [(t_theirs, theirs)]
-    for head in (2, 3):
-        first = (head - 2) * two
-        far = swap_outer(w_far[:, first : first + two])
-
-        def w_queries(place, pair, head=head):
-            return [(1, 0, (head - 2) * GQ, 2 * place + 1 - pair), (0, 0, pair * q_half + head * GQ, 2 * place + pair)]
-
-        def w_keys(place, half, first=first):
-            return [
-                (None, 2, half * n, first, place),
-                (None, 3, half * n, first, near(place)),
-                (middle(place), 4, half * n, first, 3 - place),
-                (middle(place), 5, half * n, first, 3 - near(place)),
-                (end(place), 6, half * n, first, 3 - near(place)),
-                (end(place), 7, half * n, 0, 3 - place),
-            ]
-
-        other, wide = attention(
-            "attention_" + str(head),
-            1,
-            lengths,
-            order,
-            [queries, qw_par, w_shard, w_near, w_in, w_far, w_out, far],
-            w_queries,
-            each_half(w_keys),
-            wide=wide,
-            column=lambda pair, head=head: pair * q_half + head * GQ,
-        )
-        blocks.append((swap_x(other), theirs + head * GQ))
-    for block, column in blocks:
-        wide = lax.dynamic_update_slice_in_dim(wide, block, column, 1)
-    return wide
+
+    def w_queries(head):
+        def own(place, pair):
+            return [(0, 0, pair * q_half + head * GQ, 2 * place + pair)]
+
+        def other(place, pair):
+            return [(1, 0, (head - 2) * GQ, 2 * place + 1 - pair)]
+
+        return own, other, lambda place, pair: other(place, pair) + own(place, pair)
+
+    def w_keys(place, half):
+        return [
+            (None, 2, half * n, 0, place),
+            (None, 3, half * n, 0, near(place)),
+            (None, 4, half * n, 0, 3 - place),
+            (None, 5, half * n, 0, 3 - near(place)),
+        ]
+
+    u_other, wide = attention(
+        "attention_u",
+        1,
+        lengths,
+        order,
+        [queries, qw_par, u_shard, u_near, u_far, u_out],
+        w_queries(2)[2],
+        each_half(w_keys),
+        wide=wide,
+        column=lambda pair: pair * q_half + 2 * GQ,
+    )
+    u_theirs = swap_x(u_other)
+    theirs = (1 - pair) * q_half
+    wide = lax.dynamic_update_slice_in_dim(wide, t_theirs, theirs, 1)
+    v_arrays = [queries, qw_par, v_shard, v_near, v_far, v_out]
+    (v_other,) = attention(
+        "attention_v_other", 1, lengths, order, v_arrays + [u_other], w_queries(3)[1], each_half(w_keys)
+    )
+    v_theirs = swap_x(v_other)
+    (wide,) = attention(
+        "attention_v_own",
+        1,
+        lengths,
+        order,
+        v_arrays + [v_other],
+        w_queries(3)[0],
+        each_half(w_keys),
+        wide=wide,
+        column=lambda pair: pair * q_half + 3 * GQ,
+    )
+    wide = lax.dynamic_update_slice_in_dim(wide, u_theirs, theirs + 2 * GQ, 1)
+    return lax.dynamic_update_slice_in_dim(wide, v_theirs, theirs + 3 * GQ, 1)
 
 
 def shards(queries, keys, values, lengths, order):

time: 102 us -> 91.7 us (0.90)
  waiting for transfers between devices: 31.4 us -> 13.2 us
  Pallas kernels: 26.5 us -> 29.9 us
  starting transfers between devices: 36.7 us -> 39.7 us
  other arithmetic: 0 us -> 1.71 us
    ppermute x10 -> x8, waiting for transfers between devices: 23.6 us -> 9.38 us  [swap_outer(): return lax.ppermute(a, both, outer)]
    ppermute x6 -> x4, starting transfers between devices: 0.09 us -> 12.1 us  [swap_ends(): return lax.ppermute(a, both, ends)]
    ppermute x10 -> x8, starting transfers between devices: 26.2 us -> 16.5 us  [swap_outer(): return lax.ppermute(a, both, outer)]
    pallas_call x3 -> x4, Pallas kernels: 20.7 us -> 25.8 us  [attention(): pl.pallas_call(kernel, out_shape=shapes, in_specs=[smem, smem] + [hbm] *...]
    ppermute x7, waiting for transfers between devices: 7.82 us -> 3.84 us  [swap_x(): return lax.ppermute(a, both, across)]
    slice x1 -> x2, local copies, waits for them, and re-layouts: 0.03 us -> 2.3 us  [short_shards(): u_shard, = hold([rows(w_own[:, :two], w_par[:, :two])], [t_far_par])]
    unnamed x39 -> x20, local copies, waits for them, and re-layouts: 3.94 us -> 2.17 us
    concatenate x0 -> x2, other arithmetic: none -> 1.71 us  [rows(): return jnp.concatenate(blocks, axis=0)]
  transfers between devices with their start and end apart: 23 -> 19, of which waited for: 6 -> 6; matrix products, arithmetic and copies ran while one was open for 3% -> 6% of each run, Pallas kernels for 23% -> 30%
where the time goes in v3:
time: 91.7 us; the launch traced here: 91.4 us
  starting transfers between devices  39.7 us (43%)
  Pallas kernels  29.9 us (33%)
  waiting for transfers between devices  13.2 us (14%)
  local copies, waits for them, and re-layouts  6.74 us (7%)
  other arithmetic  1.71 us (2%)
    pallas_call x4, Pallas kernels, attention(): pl.pallas_call(kernel, out_shape=shapes, in_specs=[smem, smem] + [hbm] *...  25.8 us
    ppermute x8, starting transfers between devices, swap_outer(): return lax.ppermute(a, both, outer)  16.5 us
    ppermute x4, starting transfers between devices, swap_ends(): return lax.ppermute(a, both, ends)  12.1 us
    ppermute x7, starting transfers between devices, swap_x(): return lax.ppermute(a, both, across)  11 us
    ppermute x8, waiting for transfers between devices, swap_outer(): return lax.ppermute(a, both, outer)  9.38 us
    pallas_call x2, Pallas kernels, split(): pl.pallas_call(kernel, out_shape=[jax.ShapeDtypeStruct((n, width), jnp.bf...  4.03 us
    ppermute x7, waiting for transfers between devices, swap_x(): return lax.ppermute(a, both, across)  3.84 us
    slice x2, local copies, waits for them, and re-layouts, short_shards(): u_shard, = hold([rows(w_own[:, :two], w_par[:, :two])], [t_far_par])  2.3 us
  transfers between devices with their start and end apart: 19, of which 6 were waited for; matrix products, arithmetic and copies ran while one was open for 6% of the time, Pallas kernels for 30%

profile of v3, /device:TPU:0, one launch (start us, length us, event | category | flops | bytes accessed | tf_op | source)
XLA Modules:
  0.0 91.4 jit_solution(6340926585758858353)
XLA Ops:
  0.0 2.0 %split_kv.1 = (bf16[256,512]{1,0:T(8,128)(2,1)}, bf16[256,512]{1,0:T(8,128)(2,1)}, bf16[256,512]{1,0:T(8,128)(2,1)}, bf16[256,512]{1,0:T(8,128)(2,1)}) custom-call(bf16[256,1024]{1,0:T(8,128)(2,1)} %refs_0_.6, bf16[256,1024]{1,0:T(8,128)(2,1)} %refs_1_.1), custom_call_target="tpu_custom_call" | custom-call | bytes 2097152 | tf_op jit(solution)/shard_map/split_kv/pallas_call | solution.py:226
  2.0 3.0 %collective-permute-start.5 = (bf16[256,512]{1,0:T(8,128)(2,1)}, bf16[256,512]{1,0:T(8,128)(2,1)}, u32[]{:S(2)}, u32[]{:S(2)}) collective-permute-start(bf16[256,512]{1,0:T(8,128)(2,1)} %get-tuple-element.18), channel_id=1, source_target_pairs={{0,1},{1,0},{2,3},{3,2},{4,5},{5,4},{6,7},{7,6},{8,9},{9,8},{10,11... | collective-permute-start | bytes 786440 | tf_op jit(solution)/shard_map/ppermute | solution.py:331
  5.0 0.1 collective-permute-start
  5.1 4.1 %collective-permute-start.13 = (bf16[256,512]{1,0:T(8,128)(2,1)}, bf16[256,512]{1,0:T(8,128)(2,1)}, u32[]{:S(2)}, u32[]{:S(2)}) collective-permute-start(bf16[256,512]{1,0:T(8,128)(2,1)} %get-tuple-element.20.refs_2_), channel_id=1, source_target_pairs={{0,6},{1,7},{2,4},{3,5},{4,2},{5,3},{6,0},{7,1},{8,14},{9,15},{10,... | collective-permute-start | bytes 786440 | tf_op jit(solution)/shard_map/ppermute | solution.py:337
  9.2 3.3 %collective-permute-done.5.refs_3_ = bf16[256,512]{1,0:T(8,128)(2,1)} collective-permute-done((bf16[256,512]{1,0:T(8,128)(2,1)}, bf16[256,512]{1,0:T(8,128)(2,1)}, u32[]{:S(2)}, u32[]{:S(2)}) %collective-permute-start.5) | collective-permute-done | bytes 262176 | tf_op jit(solution)/shard_map/ppermute | solution.py:331
  12.5 4.2 %collective-permute-start.6 = (bf16[256,512]{1,0:T(8,128)(2,1)}, bf16[256,512]{1,0:T(8,128)(2,1)}, u32[]{:S(2)}, u32[]{:S(2)}) collective-permute-start(bf16[256,512]{1,0:T(8,128)(2,1)} %collective-permute-done.5.refs_3_), channel_id=1, source_target_pairs={{0,6},{1,7},{2,4},{3,5},{4,2},{5,3},{6,0},{7,1},{8,14},{9,15},{10,... | collective-permute-start | bytes 786440 | tf_op jit(solution)/shard_map/ppermute | solution.py:337
  16.6 0.5 collective-permute-done.refs_1_
  17.2 0.7 copy-done.5
  17.9 2.0 %split_q.1 = (bf16[256,1024]{1,0:T(8,128)(2,1)}, bf16[256,1024]{1,0:T(8,128)(2,1)}) custom-call(bf16[256,4096]{1,0:T(8,128)(2,1)} %refs_0_.11, bf16[256,512]{1,0:T(8,128)(2,1)} %copy-done.5), custom_call_target="tpu_custom_call" | custom-call | bytes 2097152 | tf_op jit(solution)/shard_map/split_q/pallas_call | solution.py:226
  19.9 1.8 %collective-permute-start.10 = (bf16[256,1024]{1,0:T(8,128)(2,1)}, bf16[256,1024]{1,0:T(8,128)(2,1)}, u32[]{:S(2)}, u32[]{:S(2)}) collective-permute-start(bf16[256,1024]{1,0:T(8,128)(2,1)} %get-tuple-element.19), channel_id=1, source_target_pairs={{0,1},{1,0},{2,3},{3,2},{4,5},{5,4},{6,7},{7,6},{8,9},{9,8},{10,11... | collective-permute-start | bytes 1572872 | tf_op jit(solution)/shard_map/ppermute | solution.py:331
  21.7 0.7 fusion
  22.4 1.6 %collective-permute-start.12 = (bf16[256,512]{1,0:T(8,128)(2,1)}, bf16[256,512]{1,0:T(8,128)(2,1)}, u32[]{:S(2)}, u32[]{:S(2)}) collective-permute-start(bf16[256,512]{1,0:T(8,128)(2,1)} %collective-permute-done.5.refs_3_), channel_id=1, source_target_pairs={{0,2},{1,3},{2,0},{3,1},{4,6},{5,7},{6,4},{7,5},{8,10},{9,11},{10,... | collective-permute-start | bytes 786440 | tf_op jit(solution)/shard_map/ppermute | solution.py:334
  24.0 0.0 collective-permute-done.13.refs_6_
  24.0 3.2 %collective-permute-start.14 = (bf16[256,512]{1,0:T(8,128)(2,1)}, bf16[256,512]{1,0:T(8,128)(2,1)}, u32[]{:S(2)}, u32[]{:S(2)}) collective-permute-start(bf16[256,512]{1,0:T(8,128)(2,1)} %collective-permute-done.13.refs_6_), channel_id=1, source_target_pairs={{0,2},{1,3},{2,0},{3,1},{4,6},{5,7},{6,4},{7,5},{8,10},{9,11},{10,... | collective-permute-start | bytes 786440 | tf_op jit(solution)/shard_map/ppermute | solution.py:334
  27.2 0.0 collective-permute-done.6.refs_1_.refs_7_
  27.2 4.6 %collective-permute-start.15 = (bf16[256,512]{1,0:T(8,128)(2,1)}, bf16[256,512]{1,0:T(8,128)(2,1)}, u32[]{:S(2)}, u32[]{:S(2)}) collective-permute-start(bf16[256,512]{1,0:T(8,128)(2,1)} %collective-permute-done.6.refs_1_.refs_7_), channel_id=1, source_target_pairs={{0,2},{1,3},{2,0},{3,1},{4,6},{5,7},{6,4},{7,5},{8,10},{9,11},{10,... | collective-permute-start | bytes 786440 | tf_op jit(solution)/shard_map/ppermute | solution.py:334
  31.8 1.6 %fusion.1 = (bf16[256,256]{1,0:T(8,128)(2,1)S(1)}, bf16[256,256]{1,0:T(8,128)(2,1)}) fusion(bf16[256,512]{1,0:T(8,128)(2,1)} %copy-done.5), kind=kLoop, calls=%fused_computation.6 | loop fusion | bytes 524288 | tf_op jit(solution)/shard_map/slice | solution.py:367
  33.4 0.7 pad_maximum_fusion.1.refs_0_
  34.1 0.0 collective-permute-done.11.refs_4_
  34.1 1.5 %collective-permute-start.1 = (bf16[256,1024]{1,0:T(8,128)(2,1)}, bf16[256,1024]{1,0:T(8,128)(2,1)S(1)}, u32[]{:S(2)}, u32[]{:S(2)}) collective-permute-start(bf16[256,1024]{1,0:T(8,128)(2,1)} %get-tuple-element.16), channel_id=1, source_target_pairs={{0,1},{1,0},{2,3},{3,2},{4,5},{5,4},{6,7},{7,6},{8,9},{9,8},{10,11... | collective-permute-start | bytes 1572872 | tf_op jit(solution)/shard_map/ppermute | solution.py:331
  35.6 4.5 %collective-permute-done.14.refs_8_ = bf16[256,512]{1,0:T(8,128)(2,1)} collective-permute-done((bf16[256,512]{1,0:T(8,128)(2,1)}, bf16[256,512]{1,0:T(8,128)(2,1)}, u32[]{:S(2)}, u32[]{:S(2)}) %collective-permute-start.14) | collective-permute-done | bytes 262176 | tf_op jit(solution)/shard_map/ppermute | solution.py:334
  40.2 1.6 %collective-permute-start.8 = (bf16[512,256]{1,0:T(8,128)(2,1)}, bf16[512,256]{1,0:T(8,128)(2,1)S(1)}, u32[]{:S(2)}, u32[]{:S(2)}) collective-permute-start(bf16[512,256]{1,0:T(8,128)(2,1)} %hold.1.refs_2_), channel_id=1, source_target_pairs={{0,6},{1,7},{2,4},{3,5},{4,2},{5,3},{6,0},{7,1},{8,14},{9,15},{10,... | collective-permute-start | bytes 786440 | tf_op jit(solution)/shard_map/ppermute | solution.py:337
  41.8 1.0 %pad_maximum_fusion.refs_2_ = bf16[512,256]{1,0:T(8,128)(2,1)S(1)} fusion(bf16[256,256]{1,0:T(8,128)(2,1)} %get-tuple-element.28, bf16[256,256]{1,0:T(8,128)(2,1)} %get-tuple-element.26), kind=kLoop, calls=%fused_computation | loop fusion | flops 524288 | bytes 524288 | tf_op jit(solution)/shard_map/concatenate | solution.py:340
  42.8 0.0 collective-permute-done.12.refs_5_
  42.8 2.3 %collective-permute-start.3 = (bf16[512,256]{1,0:T(8,128)(2,1)S(1)}, bf16[512,256]{1,0:T(8,128)(2,1)S(1)}, u32[]{:S(2)}, u32[]{:S(2)}) collective-permute-start(bf16[512,256]{1,0:T(8,128)(2,1)S(1)} %pad_maximum_fusion.refs_2_), channel_id=1, source_target_pairs={{0,6},{1,7},{2,4},{3,5},{4,2},{5,3},{6,0},{7,1},{8,14},{9,15},{10,... | collective-permute-start | bytes 786440 | tf_op jit(solution)/shard_map/ppermute | solution.py:337
  45.1 0.2 collective-permute-done.15.refs_9_
  45.3 1.7 %collective-permute-start.7 = (bf16[512,256]{1,0:T(8,128)(2,1)}, bf16[512,256]{1,0:T(8,128)(2,1)S(1)}, u32[]{:S(2)}, u32[]{:S(2)}) collective-permute-start(bf16[512,256]{1,0:T(8,128)(2,1)} %hold.1.refs_2_), channel_id=1, source_target_pairs={{0,2},{1,3},{2,0},{3,1},{4,6},{5,7},{6,4},{7,5},{8,10},{9,11},{10,... | collective-permute-start | bytes 786440 | tf_op jit(solution)/shard_map/ppermute | solution.py:334
  47.0 9.8 %attention_t.1 = (bf16[256,1024]{1,0:T(8,128)(2,1)}, bf16[256,4096]{1,0:T(8,128)(2,1)}) custom-call(s32[8]{0:T(128)} %lengths.7, s32[32]{0:T(128)} %order.7, bf16[256,4096]{1,0:T(8,128)(2,1)} %refs_0_.11, bf16[256,1024]{1,0:T(8,128)(2,1)} %collective-permute-done.10.refs_1_, bf16[256,512]{1,0:T(8,128)(2,1)} %get-tuple-element.20.refs_2_, ...), custom_call_target="tpu_custom_call" | custom-call | flops 1258291200 | bytes 2097152 | tf_op jit(solution)/shard_map/attention_t/pallas_call | solution.py:178
  56.8 1.6 %collective-permute-start.16 = (bf16[256,1024]{1,0:T(8,128)(2,1)}, bf16[256,1024]{1,0:T(8,128)(2,1)S(1)}, u32[]{:S(2)}, u32[]{:S(2)}) collective-permute-start(bf16[256,1024]{1,0:T(8,128)(2,1)} %get-tuple-element.24), channel_id=1, source_target_pairs={{0,1},{1,0},{2,3},{3,2},{4,5},{5,4},{6,7},{7,6},{8,9},{9,8},{10,11... | collective-permute-start | bytes 1572872 | tf_op jit(solution)/shard_map/ppermute | solution.py:331
  58.3 0.0 collective-permute-done.8.refs_4_
  58.3 2.0 %collective-permute-start.9 = (bf16[512,256]{1,0:T(8,128)(2,1)S(1)}, bf16[512,256]{1,0:T(8,128)(2,1)S(1)}, u32[]{:S(2)}, u32[]{:S(2)}) collective-permute-start(bf16[512,256]{1,0:T(8,128)(2,1)S(1)} %collective-permute-done.8.refs_4_), channel_id=1, source_target_pairs={{0,2},{1,3},{2,0},{3,1},{4,6},{5,7},{6,4},{7,5},{8,10},{9,11},{10,... | collective-permute-start | bytes 786440 | tf_op jit(solution)/shard_map/ppermute | solution.py:334
  60.3 0.0 collective-permute-done.3.refs_4_
  60.4 2.8 %collective-permute-start.2 = (bf16[512,256]{1,0:T(8,128)(2,1)S(1)}, bf16[512,256]{1,0:T(8,128)(2,1)S(1)}, u32[]{:S(2)}, u32[]{:S(2)}) collective-permute-start(bf16[512,256]{1,0:T(8,128)(2,1)S(1)} %pad_maximum_fusion.refs_2_), channel_id=1, source_target_pairs={{0,2},{1,3},{2,0},{3,1},{4,6},{5,7},{6,4},{7,5},{8,10},{9,11},{10,... | collective-permute-start | bytes 786440 | tf_op jit(solution)/shard_map/ppermute | solution.py:334
  63.2 0.6 collective-permute-start.4
  63.8 0.0 collective-permute-done.1.refs_1_
  63.8 3.8 %collective-permute-done.9.refs_5_ = bf16[512,256]{1,0:T(8,128)(2,1)S(1)} collective-permute-done((bf16[512,256]{1,0:T(8,128)(2,1)S(1)}, bf16[512,256]{1,0:T(8,128)(2,1)S(1)}, u32[]{:S(2)}, u32[]{:S(2)}) %collective-permute-start.9) | collective-permute-done | bytes 262176 | tf_op jit(solution)/shard_map/ppermute | solution.py:334
  67.6 0.7 copy-done.8
  68.3 6.7 %attention_u.1 = (bf16[256,512]{1,0:T(8,128)(2,1)}, bf16[256,4096]{1,0:T(8,128)(2,1)}) custom-call(s32[8]{0:T(128)} %lengths.7, s32[32]{0:T(128)} %order.7, bf16[256,4096]{1,0:T(8,128)(2,1)} %refs_0_.11, bf16[256,1024]{1,0:T(8,128)(2,1)} %copy-done, bf16[512,256]{1,0:T(8,128)(2,1)} %hold.1.refs_2_, ...), custom_call_target="tpu_custom_call", output_to_operand_aliasing={{1}: (8, {})} | custom-call | flops 188743680 | bytes 1048576 | tf_op jit(solution)/shard_map/attention_u/pallas_call | solution.py:178
  75.0 1.6 %collective-permute-start.17 = (bf16[256,512]{1,0:T(8,128)(2,1)}, bf16[256,512]{1,0:T(8,128)(2,1)S(1)}, u32[]{:S(2)}, u32[]{:S(2)}) collective-permute-start(bf16[256,512]{1,0:T(8,128)(2,1)} %get-tuple-element.22.refs_6_), channel_id=1, source_target_pairs={{0,1},{1,0},{2,3},{3,2},{4,5},{5,4},{6,7},{7,6},{8,9},{9,8},{10,11... | collective-permute-start | bytes 786440 | tf_op jit(solution)/shard_map/ppermute | solution.py:331
  76.6 0.9 collective-permute-done.4.refs_5_
  77.4 0.7 copy-done.4
  78.2 4.7 %attention_v_other.1.refs_6_ = bf16[256,512]{1,0:T(8,128)(2,1)} custom-call(s32[8]{0:T(128)} %lengths.7, s32[32]{0:T(128)} %order.7, bf16[256,4096]{1,0:T(8,128)(2,1)} %refs_0_.11, bf16[256,1024]{1,0:T(8,128)(2,1)} %copy-done, bf16[512,256]{1,0:T(8,128)(2,1)} %copy-done.1, bf16[512,256]{1,0:T(8,128)(2,1)} %copy-done.3, bf16[512,256]{1,0:T(8,128)(2,1)} %copy-done.2, ...), custom_call_target="tpu_custom_call" | custom-call | flops 94371840 | bytes 524288 | tf_op jit(solution)/shard_map/attention_v_other/pallas_call | solution.py:178
  82.8 1.5 %collective-permute-start.18 = (bf16[256,512]{1,0:T(8,128)(2,1)}, bf16[256,512]{1,0:T(8,128)(2,1)S(1)}, u32[]{:S(2)}, u32[]{:S(2)}) collective-permute-start(bf16[256,512]{1,0:T(8,128)(2,1)} %attention_v_other.1.refs_6_), channel_id=1, source_target_pairs={{0,1},{1,0},{2,3},{3,2},{4,5},{5,4},{6,7},{7,6},{8,9},{9,8},{10,11... | collective-permute-start | bytes 786440 | tf_op jit(solution)/shard_map/ppermute | solution.py:331
  84.4 0.0 collective-permute-done.16
  84.4 0.8 constant_dynamic-update-slice_fusion.2.refs_7_
  85.2 4.7 %attention_v_own.1 = bf16[256,4096]{1,0:T(8,128)(2,1)} custom-call(s32[8]{0:T(128)} %lengths.7, s32[32]{0:T(128)} %order.7, bf16[256,4096]{1,0:T(8,128)(2,1)} %refs_0_.11, bf16[256,1024]{1,0:T(8,128)(2,1)} %copy-done, bf16[512,256]{1,0:T(8,128)(2,1)} %copy-done.1, bf16[512,256]{1,0:T(8,128)(2,1)} %copy-done.3, ...), custom_call_target="tpu_custom_call", output_to_operand_aliasing={{}: (9, {})} | custom-call | flops 94371840 | bytes 524288 | tf_op jit(solution)/shard_map/attention_v_own/pallas_call | solution.py:178
  89.9 0.7 constant_dynamic-update-slice_fusion.1
  90.6 0.7 constant_dynamic-update-slice_fusion
  (24 shorter events, 0.0 us)
Async XLA Ops:
  2.0 19.7 %copy-start.9 = (bf16[256,512]{1,0:T(8,128)(2,1)S(1)}, bf16[256,512]{1,0:T(8,128)(2,1)}, u32[]{:S(2)}) copy-start(bf16[256,512]{1,0:T(8,128)(2,1)} %get-tuple-element.17) | copy-start | bytes 786436
  2.0 10.5 %collective-permute-start.5 = (bf16[256,512]{1,0:T(8,128)(2,1)}, bf16[256,512]{1,0:T(8,128)(2,1)}, u32[]{:S(2)}, u32[]{:S(2)}) collective-permute-start(bf16[256,512]{1,0:T(8,128)(2,1)} %get-tuple-element.18), channel_id=1, source_target_pairs={{0,1},{1,0},{2,3},{3,2},{4,5},{5,4},{6,7},{7,6},{8,9},{9,8},{10,11... | collective-permute-start | bytes 786440 | tf_op jit(solution)/shard_map/ppermute | solution.py:331
  5.0 12.1 %collective-permute-start = (bf16[256,512]{1,0:T(8,128)(2,1)}, bf16[256,512]{1,0:T(8,128)(2,1)S(1)}, u32[]{:S(2)}, u32[]{:S(2)}) collective-permute-start(bf16[256,512]{1,0:T(8,128)(2,1)} %get-tuple-element.15), channel_id=1, source_target_pairs={{0,1},{1,0},{2,3},{3,2},{4,5},{5,4},{6,7},{7,6},{8,9},{9,8},{10,11... | collective-permute-start | bytes 786440 | tf_op jit(solution)/shard_map/ppermute | solution.py:331
  5.1 18.9 %collective-permute-start.13 = (bf16[256,512]{1,0:T(8,128)(2,1)}, bf16[256,512]{1,0:T(8,128)(2,1)}, u32[]{:S(2)}, u32[]{:S(2)}) collective-permute-start(bf16[256,512]{1,0:T(8,128)(2,1)} %get-tuple-element.20.refs_2_), channel_id=1, source_target_pairs={{0,6},{1,7},{2,4},{3,5},{4,2},{5,3},{6,0},{7,1},{8,14},{9,15},{10,... | collective-permute-start | bytes 786440 | tf_op jit(solution)/shard_map/ppermute | solution.py:337
  12.5 14.7 %collective-permute-start.6 = (bf16[256,512]{1,0:T(8,128)(2,1)}, bf16[256,512]{1,0:T(8,128)(2,1)}, u32[]{:S(2)}, u32[]{:S(2)}) collective-permute-start(bf16[256,512]{1,0:T(8,128)(2,1)} %collective-permute-done.5.refs_3_), channel_id=1, source_target_pairs={{0,6},{1,7},{2,4},{3,5},{4,2},{5,3},{6,0},{7,1},{8,14},{9,15},{10,... | collective-permute-start | bytes 786440 | tf_op jit(solution)/shard_map/ppermute | solution.py:337
  16.6 17.5 %collective-permute-start.11 = (bf16[256,512]{1,0:T(8,128)(2,1)}, bf16[256,512]{1,0:T(8,128)(2,1)}, u32[]{:S(2)}, u32[]{:S(2)}) collective-permute-start(bf16[256,512]{1,0:T(8,128)(2,1)} %get-tuple-element.20.refs_2_), channel_id=1, source_target_pairs={{0,2},{1,3},{2,0},{3,1},{4,6},{5,7},{6,4},{7,5},{8,10},{9,11},{10,... | collective-permute-start | bytes 786440 | tf_op jit(solution)/shard_map/ppermute | solution.py:334
  17.2 0.7 copy-start.5
  19.9 27.1 %collective-permute-start.10 = (bf16[256,1024]{1,0:T(8,128)(2,1)}, bf16[256,1024]{1,0:T(8,128)(2,1)}, u32[]{:S(2)}, u32[]{:S(2)}) collective-permute-start(bf16[256,1024]{1,0:T(8,128)(2,1)} %get-tuple-element.19), channel_id=1, source_target_pairs={{0,1},{1,0},{2,3},{3,2},{4,5},{5,4},{6,7},{7,6},{8,9},{9,8},{10,11... | collective-permute-start | bytes 1572872 | tf_op jit(solution)/shard_map/ppermute | solution.py:331
  22.4 20.4 %collective-permute-start.12 = (bf16[256,512]{1,0:T(8,128)(2,1)}, bf16[256,512]{1,0:T(8,128)(2,1)}, u32[]{:S(2)}, u32[]{:S(2)}) collective-permute-start(bf16[256,512]{1,0:T(8,128)(2,1)} %collective-permute-done.5.refs_3_), channel_id=1, source_target_pairs={{0,2},{1,3},{2,0},{3,1},{4,6},{5,7},{6,4},{7,5},{8,10},{9,11},{10,... | collective-permute-start | bytes 786440 | tf_op jit(solution)/shard_map/ppermute | solution.py:334
  24.0 16.2 %collective-permute-start.14 = (bf16[256,512]{1,0:T(8,128)(2,1)}, bf16[256,512]{1,0:T(8,128)(2,1)}, u32[]{:S(2)}, u32[]{:S(2)}) collective-permute-start(bf16[256,512]{1,0:T(8,128)(2,1)} %collective-permute-done.13.refs_6_), channel_id=1, source_target_pairs={{0,2},{1,3},{2,0},{3,1},{4,6},{5,7},{6,4},{7,5},{8,10},{9,11},{10,... | collective-permute-start | bytes 786440 | tf_op jit(solution)/shard_map/ppermute | solution.py:334
  27.2 18.1 %collective-permute-start.15 = (bf16[256,512]{1,0:T(8,128)(2,1)}, bf16[256,512]{1,0:T(8,128)(2,1)}, u32[]{:S(2)}, u32[]{:S(2)}) collective-permute-start(bf16[256,512]{1,0:T(8,128)(2,1)} %collective-permute-done.6.refs_1_.refs_7_), channel_id=1, source_target_pairs={{0,2},{1,3},{2,0},{3,1},{4,6},{5,7},{6,4},{7,5},{8,10},{9,11},{10,... | collective-permute-start | bytes 786440 | tf_op jit(solution)/shard_map/ppermute | solution.py:334
  34.1 29.7 %collective-permute-start.1 = (bf16[256,1024]{1,0:T(8,128)(2,1)}, bf16[256,1024]{1,0:T(8,128)(2,1)S(1)}, u32[]{:S(2)}, u32[]{:S(2)}) collective-permute-start(bf16[256,1024]{1,0:T(8,128)(2,1)} %get-tuple-element.16), channel_id=1, source_target_pairs={{0,1},{1,0},{2,3},{3,2},{4,5},{5,4},{6,7},{7,6},{8,9},{9,8},{10,11... | collective-permute-start | bytes 1572872 | tf_op jit(solution)/shard_map/ppermute | solution.py:331
  40.2 18.1 %collective-permute-start.8 = (bf16[512,256]{1,0:T(8,128)(2,1)}, bf16[512,256]{1,0:T(8,128)(2,1)S(1)}, u32[]{:S(2)}, u32[]{:S(2)}) collective-permute-start(bf16[512,256]{1,0:T(8,128)(2,1)} %hold.1.refs_2_), channel_id=1, source_target_pairs={{0,6},{1,7},{2,4},{3,5},{4,2},{5,3},{6,0},{7,1},{8,14},{9,15},{10,... | collective-permute-start | bytes 786440 | tf_op jit(solution)/shard_map/ppermute | solution.py:337
  42.8 17.6 %copy-start.1 = (bf16[512,256]{1,0:T(8,128)(2,1)}, bf16[512,256]{1,0:T(8,128)(2,1)S(1)}, u32[]{:S(2)}) copy-start(bf16[512,256]{1,0:T(8,128)(2,1)S(1)} %pad_maximum_fusion.refs_2_) | copy-start | bytes 786436
  42.8 17.5 %collective-permute-start.3 = (bf16[512,256]{1,0:T(8,128)(2,1)S(1)}, bf16[512,256]{1,0:T(8,128)(2,1)S(1)}, u32[]{:S(2)}, u32[]{:S(2)}) collective-permute-start(bf16[512,256]{1,0:T(8,128)(2,1)S(1)} %pad_maximum_fusion.refs_2_), channel_id=1, source_target_pairs={{0,6},{1,7},{2,4},{3,5},{4,2},{5,3},{6,0},{7,1},{8,14},{9,15},{10,... | collective-permute-start | bytes 786440 | tf_op jit(solution)/shard_map/ppermute | solution.py:337
  45.3 17.9 %collective-permute-start.7 = (bf16[512,256]{1,0:T(8,128)(2,1)}, bf16[512,256]{1,0:T(8,128)(2,1)S(1)}, u32[]{:S(2)}, u32[]{:S(2)}) collective-permute-start(bf16[512,256]{1,0:T(8,128)(2,1)} %hold.1.refs_2_), channel_id=1, source_target_pairs={{0,2},{1,3},{2,0},{3,1},{4,6},{5,7},{6,4},{7,5},{8,10},{9,11},{10,... | collective-permute-start | bytes 786440 | tf_op jit(solution)/shard_map/ppermute | solution.py:334
  56.8 27.6 %collective-permute-start.16 = (bf16[256,1024]{1,0:T(8,128)(2,1)}, bf16[256,1024]{1,0:T(8,128)(2,1)S(1)}, u32[]{:S(2)}, u32[]{:S(2)}) collective-permute-start(bf16[256,1024]{1,0:T(8,128)(2,1)} %get-tuple-element.24), channel_id=1, source_target_pairs={{0,1},{1,0},{2,3},{3,2},{4,5},{5,4},{6,7},{7,6},{8,9},{9,8},{10,11... | collective-permute-start | bytes 1572872 | tf_op jit(solution)/shard_map/ppermute | solution.py:331
  58.3 9.3 %copy-start.6 = (bf16[512,256]{1,0:T(8,128)(2,1)}, bf16[512,256]{1,0:T(8,128)(2,1)S(1)}, u32[]{:S(2)}) copy-start(bf16[512,256]{1,0:T(8,128)(2,1)S(1)} %collective-permute-done.8.refs_4_) | copy-start | bytes 786436
  58.3 9.2 %collective-permute-start.9 = (bf16[512,256]{1,0:T(8,128)(2,1)S(1)}, bf16[512,256]{1,0:T(8,128)(2,1)S(1)}, u32[]{:S(2)}, u32[]{:S(2)}) collective-permute-start(bf16[512,256]{1,0:T(8,128)(2,1)S(1)} %collective-permute-done.8.refs_4_), channel_id=1, source_target_pairs={{0,2},{1,3},{2,0},{3,1},{4,6},{5,7},{6,4},{7,5},{8,10},{9,11},{10,... | collective-permute-start | bytes 786440 | tf_op jit(solution)/shard_map/ppermute | solution.py:334
  60.4 17.1 %copy-start.2 = (bf16[512,256]{1,0:T(8,128)(2,1)}, bf16[512,256]{1,0:T(8,128)(2,1)S(1)}, u32[]{:S(2)}) copy-start(bf16[512,256]{1,0:T(8,128)(2,1)S(1)} %collective-permute-done.3.refs_4_) | copy-start | bytes 786436
  60.4 16.2 %collective-permute-start.2 = (bf16[512,256]{1,0:T(8,128)(2,1)S(1)}, bf16[512,256]{1,0:T(8,128)(2,1)S(1)}, u32[]{:S(2)}, u32[]{:S(2)}) collective-permute-start(bf16[512,256]{1,0:T(8,128)(2,1)S(1)} %pad_maximum_fusion.refs_2_), channel_id=1, source_target_pairs={{0,2},{1,3},{2,0},{3,1},{4,6},{5,7},{6,4},{7,5},{8,10},{9,11},{10,... | collective-permute-start | bytes 786440 | tf_op jit(solution)/shard_map/ppermute | solution.py:334
  63.2 4.4 %copy-start.7 = (bf16[512,256]{1,0:T(8,128)(2,1)}, bf16[512,256]{1,0:T(8,128)(2,1)S(1)}, u32[]{:S(2)}) copy-start(bf16[512,256]{1,0:T(8,128)(2,1)S(1)} %collective-permute-done.7.refs_3_) | copy-start | bytes 786436
  63.2 14.3 %collective-permute-start.4 = (bf16[512,256]{1,0:T(8,128)(2,1)S(1)}, bf16[512,256]{1,0:T(8,128)(2,1)S(1)}, u32[]{:S(2)}, u32[]{:S(2)}) collective-permute-start(bf16[512,256]{1,0:T(8,128)(2,1)S(1)} %collective-permute-done.3.refs_4_), channel_id=1, source_target_pairs={{0,2},{1,3},{2,0},{3,1},{4,6},{5,7},{6,4},{7,5},{8,10},{9,11},{10,... | collective-permute-start | bytes 786440 | tf_op jit(solution)/shard_map/ppermute | solution.py:334
  63.8 3.8 %copy-start = (bf16[256,1024]{1,0:T(8,128)(2,1)}, bf16[256,1024]{1,0:T(8,128)(2,1)S(1)}, u32[]{:S(2)}) copy-start(bf16[256,1024]{1,0:T(8,128)(2,1)S(1)} %collective-permute-done.1.refs_1_) | copy-start | bytes 1572868
  67.6 0.7 copy-start.8
  75.0 14.9 %collective-permute-start.17 = (bf16[256,512]{1,0:T(8,128)(2,1)}, bf16[256,512]{1,0:T(8,128)(2,1)S(1)}, u32[]{:S(2)}, u32[]{:S(2)}) collective-permute-start(bf16[256,512]{1,0:T(8,128)(2,1)} %get-tuple-element.22.refs_6_), channel_id=1, source_target_pairs={{0,1},{1,0},{2,3},{3,2},{4,5},{5,4},{6,7},{7,6},{8,9},{9,8},{10,11... | collective-permute-start | bytes 786440 | tf_op jit(solution)/shard_map/ppermute | solution.py:331
  76.6 0.9 copy-start.3
  77.4 0.7 copy-start.4
  82.8 7.8 %collective-permute-start.18 = (bf16[256,512]{1,0:T(8,128)(2,1)}, bf16[256,512]{1,0:T(8,128)(2,1)S(1)}, u32[]{:S(2)}, u32[]{:S(2)}) collective-permute-start(bf16[256,512]{1,0:T(8,128)(2,1)} %attention_v_other.1.refs_6_), channel_id=1, source_target_pairs={{0,1},{1,0},{2,3},{3,2},{4,5},{5,4},{6,7},{7,6},{8,9},{9,8},{10,11... | collective-permute-start | bytes 786440 | tf_op jit(solution)/shard_map/ppermute | solution.py:331

commit v4 on v3

--- a/solution.py
+++ b/solution.py
@@ -19,8 +19,7 @@
 GQ = GROUP * HEAD_DIM
 COST = {1: 0.3, 2: 1}
 VMEM_BYTES = 60 * 1024 * 1024
-WHOLE_VMEM = 64 * 1024 * 1024
-COUNTS = (2, 4, 6, MOST_STEPS)
+COUNTS = tuple(range(1, MOST_STEPS + 1))
 TOGETHER = {1: 2, 2: 2}
 
 
@@ -169,7 +168,7 @@
         body() if active is None else pl.when(active(place))(body)
 
     smem = pl.BlockSpec(memory_space=pltpu.SMEM)
-    hbm = pl.BlockSpec(memory_space=pl.ANY)
+    hbm = pl.BlockSpec(memory_space=pltpu.HBM)
     pairs = int(100 * blocks * rows_here * heads * GROUP * 6 * COST[heads])
     shapes = [jax.ShapeDtypeStruct((rows_here, q_width), jnp.bfloat16)] * blocks
     if column is not None:
@@ -222,7 +221,7 @@
         for o in range(count):
             pltpu.make_async_copy(held[o], outs[o], sem_out).wait()
 
-    hbm = pl.BlockSpec(memory_space=pl.ANY)
+    hbm = pl.BlockSpec(memory_space=pltpu.HBM)
     return pl.pallas_call(
         kernel,
         out_shape=[jax.ShapeDtypeStruct((n, width), jnp.bfloat16) for width in widths],
@@ -301,7 +300,7 @@
 
 def hold(arrays, others=(), token=False):
     count = len(arrays)
-    hbm = pl.BlockSpec(memory_space=pl.ANY)
+    hbm = pl.BlockSpec(memory_space=pltpu.HBM)
     return pl.pallas_call(
         lambda *refs: None,
         out_shape=[jax.ShapeDtypeStruct(array.shape, array.dtype) for array in arrays]
@@ -309,7 +308,7 @@
         in_specs=[hbm] * (count + len(others)),
         out_specs=[hbm] * (count + token),
         input_output_aliases={i: i for i in range(count)},
-        compiler_params=pltpu.CompilerParams(vmem_limit_bytes=WHOLE_VMEM),
+        compiler_params=pltpu.CompilerParams(vmem_limit_bytes=VMEM_BYTES),
         name="hold",
     )(*arrays, *others)
 

time: 91.7 us -> 91 us (level)
  other arithmetic: 1.71 us -> 0.75 us
    slice x2, local copies, waits for them, and re-layouts: 2.3 us -> 1 us  [short_shards(): u_shard, = hold([rows(w_own[:, :two], w_par[:, :two])], [t_far_par])]
    unnamed x20 -> x36, local copies, waits for them, and re-layouts: 2.17 us -> 3.43 us
    concatenate x2, other arithmetic: 1.71 us -> 0.75 us  [rows(): return jnp.concatenate(blocks, axis=0)]
  transfers between devices with their start and end apart: 19 -> 19, of which waited for: 6 -> 6; matrix products, arithmetic and copies ran while one was open for 6% -> 4% of each run, Pallas kernels for 30% -> 31%
where the time goes in v4:
time: 91 us; the launch traced here: 91.4 us
  starting transfers between devices  40 us (44%)
  Pallas kernels  29.9 us (33%)
  waiting for transfers between devices  13.8 us (15%)
  local copies, waits for them, and re-layouts  6.71 us (7%)
    pallas_call x4, Pallas kernels, attention(): pl.pallas_call(kernel, out_shape=shapes, in_specs=[smem, smem] + [hbm] *...  25.9 us
    ppermute x8, starting transfers between devices, swap_outer(): return lax.ppermute(a, both, outer)  17.1 us
    ppermute x4, starting transfers between devices, swap_ends(): return lax.ppermute(a, both, ends)  12.1 us
    ppermute x7, starting transfers between devices, swap_x(): return lax.ppermute(a, both, across)  10.9 us
    ppermute x8, waiting for transfers between devices, swap_outer(): return lax.ppermute(a, both, outer)  9.91 us
    pallas_call x2, Pallas kernels, split(): pl.pallas_call(kernel, out_shape=[jax.ShapeDtypeStruct((n, width), jnp.bf...  4.02 us
    ppermute x7, waiting for transfers between devices, swap_x(): return lax.ppermute(a, both, across)  3.83 us
    unnamed x36, local copies, waits for them, and re-layouts  3.43 us
  transfers between devices with their start and end apart: 19, of which 6 were waited for; matrix products, arithmetic and copies ran while one was open for 4% of the time, Pallas kernels for 31%

profile of v4, /device:TPU:0, one launch (start us, length us, event | category | flops | bytes accessed | tf_op | source)
XLA Modules:
  0.0 91.4 jit_solution(5764118326201310143)
XLA Ops:
  0.0 2.0 %split_kv.1 = (bf16[256,512]{1,0:T(8,128)(2,1)}, bf16[256,512]{1,0:T(8,128)(2,1)}, bf16[256,512]{1,0:T(8,128)(2,1)}, bf16[256,512]{1,0:T(8,128)(2,1)}) custom-call(bf16[256,1024]{1,0:T(8,128)(2,1)} %refs_0_.6, bf16[256,1024]{1,0:T(8,128)(2,1)} %refs_1_.1), custom_call_target="tpu_custom_call" | custom-call | bytes 2097152 | tf_op jit(solution)/shard_map/split_kv/pallas_call | solution.py:225
  2.0 3.0 %collective-permute-start.5 = (bf16[256,512]{1,0:T(8,128)(2,1)}, bf16[256,512]{1,0:T(8,128)(2,1)S(1)}, u32[]{:S(2)}, u32[]{:S(2)}) collective-permute-start(bf16[256,512]{1,0:T(8,128)(2,1)} %get-tuple-element.18), channel_id=1, source_target_pairs={{0,1},{1,0},{2,3},{3,2},{4,5},{5,4},{6,7},{7,6},{8,9},{9,8},{10,11... | collective-permute-start | bytes 786440 | tf_op jit(solution)/shard_map/ppermute | solution.py:330
  5.0 0.1 collective-permute-start
  5.1 4.1 %collective-permute-start.13 = (bf16[256,512]{1,0:T(8,128)(2,1)}, bf16[256,512]{1,0:T(8,128)(2,1)S(1)}, u32[]{:S(2)}, u32[]{:S(2)}) collective-permute-start(bf16[256,512]{1,0:T(8,128)(2,1)} %get-tuple-element.20.refs_2_), channel_id=1, source_target_pairs={{0,6},{1,7},{2,4},{3,5},{4,2},{5,3},{6,0},{7,1},{8,14},{9,15},{10,... | collective-permute-start | bytes 786440 | tf_op jit(solution)/shard_map/ppermute | solution.py:336
  9.2 3.2 %collective-permute-done.5.refs_3_ = bf16[256,512]{1,0:T(8,128)(2,1)S(1)} collective-permute-done((bf16[256,512]{1,0:T(8,128)(2,1)}, bf16[256,512]{1,0:T(8,128)(2,1)S(1)}, u32[]{:S(2)}, u32[]{:S(2)}) %collective-permute-start.5) | collective-permute-done | bytes 262176 | tf_op jit(solution)/shard_map/ppermute | solution.py:330
  12.4 4.2 %collective-permute-start.6 = (bf16[256,512]{1,0:T(8,128)(2,1)S(1)}, bf16[256,512]{1,0:T(8,128)(2,1)S(1)}, u32[]{:S(2)}, u32[]{:S(2)}) collective-permute-start(bf16[256,512]{1,0:T(8,128)(2,1)S(1)} %collective-permute-done.5.refs_3_), channel_id=1, source_target_pairs={{0,6},{1,7},{2,4},{3,5},{4,2},{5,3},{6,0},{7,1},{8,14},{9,15},{10,... | collective-permute-start | bytes 786440 | tf_op jit(solution)/shard_map/ppermute | solution.py:336
  16.5 0.0 collective-permute-start.11
  16.5 0.6 collective-permute-done.refs_1_
  17.2 0.7 copy-done.6
  17.9 2.0 %split_q.1 = (bf16[256,1024]{1,0:T(8,128)(2,1)}, bf16[256,1024]{1,0:T(8,128)(2,1)}) custom-call(bf16[256,4096]{1,0:T(8,128)(2,1)} %refs_0_.11, bf16[256,512]{1,0:T(8,128)(2,1)} %copy-done.6), custom_call_target="tpu_custom_call" | custom-call | bytes 2097152 | tf_op jit(solution)/shard_map/split_q/pallas_call | solution.py:225
  19.9 1.8 %collective-permute-start.10 = (bf16[256,1024]{1,0:T(8,128)(2,1)}, bf16[256,1024]{1,0:T(8,128)(2,1)S(1)}, u32[]{:S(2)}, u32[]{:S(2)}) collective-permute-start(bf16[256,1024]{1,0:T(8,128)(2,1)} %get-tuple-element.19), channel_id=1, source_target_pairs={{0,1},{1,0},{2,3},{3,2},{4,5},{5,4},{6,7},{7,6},{8,9},{9,8},{10,11... | collective-permute-start | bytes 1572872 | tf_op jit(solution)/shard_map/ppermute | solution.py:330
  21.7 1.6 %collective-permute-start.12 = (bf16[256,512]{1,0:T(8,128)(2,1)S(1)}, bf16[256,512]{1,0:T(8,128)(2,1)S(1)}, u32[]{:S(2)}, u32[]{:S(2)}) collective-permute-start(bf16[256,512]{1,0:T(8,128)(2,1)S(1)} %collective-permute-done.5.refs_3_), channel_id=1, source_target_pairs={{0,2},{1,3},{2,0},{3,1},{4,6},{5,7},{6,4},{7,5},{8,10},{9,11},{10,... | collective-permute-start | bytes 786440 | tf_op jit(solution)/shard_map/ppermute | solution.py:333
  23.4 0.0 collective-permute-done.13.refs_6_
  23.4 3.7 %collective-permute-start.14 = (bf16[256,512]{1,0:T(8,128)(2,1)S(1)}, bf16[256,512]{1,0:T(8,128)(2,1)S(1)}, u32[]{:S(2)}, u32[]{:S(2)}) collective-permute-start(bf16[256,512]{1,0:T(8,128)(2,1)S(1)} %collective-permute-done.13.refs_6_), channel_id=1, source_target_pairs={{0,2},{1,3},{2,0},{3,1},{4,6},{5,7},{6,4},{7,5},{8,10},{9,11},{10,... | collective-permute-start | bytes 786440 | tf_op jit(solution)/shard_map/ppermute | solution.py:333
  27.1 0.0 collective-permute-done.6.refs_1_.refs_7_
  27.1 4.6 %collective-permute-start.15 = (bf16[256,512]{1,0:T(8,128)(2,1)S(1)}, bf16[256,512]{1,0:T(8,128)(2,1)S(1)}, u32[]{:S(2)}, u32[]{:S(2)}) collective-permute-start(bf16[256,512]{1,0:T(8,128)(2,1)S(1)} %collective-permute-done.6.refs_1_.refs_7_), channel_id=1, source_target_pairs={{0,2},{1,3},{2,0},{3,1},{4,6},{5,7},{6,4},{7,5},{8,10},{9,11},{10,... | collective-permute-start | bytes 786440 | tf_op jit(solution)/shard_map/ppermute | solution.py:333
  31.7 1.0 %fusion.1 = (bf16[256,256]{1,0:T(8,128)(2,1)S(1)}, bf16[256,256]{1,0:T(8,128)(2,1)S(1)}) fusion(bf16[256,512]{1,0:T(8,128)(2,1)} %copy-done.6), kind=kLoop, calls=%fused_computation.6 | loop fusion | bytes 524288 | tf_op jit(solution)/shard_map/slice | solution.py:366
  32.7 0.7 pad_maximum_fusion.1.refs_0_
  33.4 0.0 collective-permute-done.11.refs_4_
  33.4 1.6 %collective-permute-start.1 = (bf16[256,1024]{1,0:T(8,128)(2,1)}, bf16[256,1024]{1,0:T(8,128)(2,1)S(1)}, u32[]{:S(2)}, u32[]{:S(2)}) collective-permute-start(bf16[256,1024]{1,0:T(8,128)(2,1)} %get-tuple-element.16), channel_id=1, source_target_pairs={{0,1},{1,0},{2,3},{3,2},{4,5},{5,4},{6,7},{7,6},{8,9},{9,8},{10,11... | collective-permute-start | bytes 1572872 | tf_op jit(solution)/shard_map/ppermute | solution.py:330
  35.0 4.8 %collective-permute-done.14.refs_8_ = bf16[256,512]{1,0:T(8,128)(2,1)S(1)} collective-permute-done((bf16[256,512]{1,0:T(8,128)(2,1)S(1)}, bf16[256,512]{1,0:T(8,128)(2,1)S(1)}, u32[]{:S(2)}, u32[]{:S(2)}) %collective-permute-start.14) | collective-permute-done | bytes 262176 | tf_op jit(solution)/shard_map/ppermute | solution.py:333
  39.8 1.6 %collective-permute-start.8 = (bf16[512,256]{1,0:T(8,128)(2,1)}, bf16[512,256]{1,0:T(8,128)(2,1)S(1)}, u32[]{:S(2)}, u32[]{:S(2)}) collective-permute-start(bf16[512,256]{1,0:T(8,128)(2,1)} %hold.1.refs_2_), channel_id=1, source_target_pairs={{0,6},{1,7},{2,4},{3,5},{4,2},{5,3},{6,0},{7,1},{8,14},{9,15},{10,... | collective-permute-start | bytes 786440 | tf_op jit(solution)/shard_map/ppermute | solution.py:336
  41.4 2.3 %collective-permute-start.3 = (bf16[512,256]{1,0:T(8,128)(2,1)S(1)}, bf16[512,256]{1,0:T(8,128)(2,1)S(1)}, u32[]{:S(2)}, u32[]{:S(2)}) collective-permute-start(bf16[512,256]{1,0:T(8,128)(2,1)S(1)} %pad_maximum_fusion.refs_2_), channel_id=1, source_target_pairs={{0,6},{1,7},{2,4},{3,5},{4,2},{5,3},{6,0},{7,1},{8,14},{9,15},{10,... | collective-permute-start | bytes 786440 | tf_op jit(solution)/shard_map/ppermute | solution.py:336
  43.7 0.6 collective-permute-done.15.refs_9_
  44.3 1.7 %collective-permute-start.7 = (bf16[512,256]{1,0:T(8,128)(2,1)}, bf16[512,256]{1,0:T(8,128)(2,1)S(1)}, u32[]{:S(2)}, u32[]{:S(2)}) collective-permute-start(bf16[512,256]{1,0:T(8,128)(2,1)} %hold.1.refs_2_), channel_id=1, source_target_pairs={{0,2},{1,3},{2,0},{3,1},{4,6},{5,7},{6,4},{7,5},{8,10},{9,11},{10,... | collective-permute-start | bytes 786440 | tf_op jit(solution)/shard_map/ppermute | solution.py:333
  46.0 0.0 collective-permute-done.10.refs_1_
  46.0 0.8 copy-done.7
  46.8 9.7 %attention_t.1 = (bf16[256,1024]{1,0:T(8,128)(2,1)}, bf16[256,4096]{1,0:T(8,128)(2,1)}) custom-call(s32[8]{0:T(128)} %lengths.7, s32[32]{0:T(128)} %order.7, bf16[256,4096]{1,0:T(8,128)(2,1)} %refs_0_.11, bf16[256,1024]{1,0:T(8,128)(2,1)} %copy-done.7, bf16[256,512]{1,0:T(8,128)(2,1)} %get-tuple-element.20.refs_2_, bf16[256,512]{1,0:T(8,128)(2,1)} %copy-done.8, ...), custom_call_target="tpu_custom_call" | custom-call | flops 1258291200 | bytes 2097152 | tf_op jit(solution)/shard_map/attention_t/pallas_call | solution.py:177
  56.5 1.6 %collective-permute-start.16 = (bf16[256,1024]{1,0:T(8,128)(2,1)}, bf16[256,1024]{1,0:T(8,128)(2,1)S(1)}, u32[]{:S(2)}, u32[]{:S(2)}) collective-permute-start(bf16[256,1024]{1,0:T(8,128)(2,1)} %get-tuple-element.24), channel_id=1, source_target_pairs={{0,1},{1,0},{2,3},{3,2},{4,5},{5,4},{6,7},{7,6},{8,9},{9,8},{10,11... | collective-permute-start | bytes 1572872 | tf_op jit(solution)/shard_map/ppermute | solution.py:330
  58.1 0.0 collective-permute-done.8.refs_4_
  58.1 2.5 %collective-permute-start.9 = (bf16[512,256]{1,0:T(8,128)(2,1)S(1)}, bf16[512,256]{1,0:T(8,128)(2,1)S(1)}, u32[]{:S(2)}, u32[]{:S(2)}) collective-permute-start(bf16[512,256]{1,0:T(8,128)(2,1)S(1)} %collective-permute-done.8.refs_4_), channel_id=1, source_target_pairs={{0,2},{1,3},{2,0},{3,1},{4,6},{5,7},{6,4},{7,5},{8,10},{9,11},{10,... | collective-permute-start | bytes 786440 | tf_op jit(solution)/shard_map/ppermute | solution.py:333
  60.6 2.8 %collective-permute-start.2 = (bf16[512,256]{1,0:T(8,128)(2,1)S(1)}, bf16[512,256]{1,0:T(8,128)(2,1)S(1)}, u32[]{:S(2)}, u32[]{:S(2)}) collective-permute-start(bf16[512,256]{1,0:T(8,128)(2,1)S(1)} %pad_maximum_fusion.refs_2_), channel_id=1, source_target_pairs={{0,2},{1,3},{2,0},{3,1},{4,6},{5,7},{6,4},{7,5},{8,10},{9,11},{10,... | collective-permute-start | bytes 786440 | tf_op jit(solution)/shard_map/ppermute | solution.py:333
  63.4 0.1 collective-permute-start.4
  63.5 4.3 %collective-permute-done.9.refs_5_ = bf16[512,256]{1,0:T(8,128)(2,1)S(1)} collective-permute-done((bf16[512,256]{1,0:T(8,128)(2,1)S(1)}, bf16[512,256]{1,0:T(8,128)(2,1)S(1)}, u32[]{:S(2)}, u32[]{:S(2)}) %collective-permute-start.9) | collective-permute-done | bytes 262176 | tf_op jit(solution)/shard_map/ppermute | solution.py:333
  67.9 0.7 copy-done.16
  68.6 6.8 %attention_u.1 = (bf16[256,512]{1,0:T(8,128)(2,1)}, bf16[256,4096]{1,0:T(8,128)(2,1)}) custom-call(s32[8]{0:T(128)} %lengths.7, s32[32]{0:T(128)} %order.7, bf16[256,4096]{1,0:T(8,128)(2,1)} %refs_0_.11, bf16[256,1024]{1,0:T(8,128)(2,1)} %copy-done, bf16[512,256]{1,0:T(8,128)(2,1)} %hold.1.refs_2_, ...), custom_call_target="tpu_custom_call", output_to_operand_aliasing={{1}: (8, {})} | custom-call | flops 188743680 | bytes 1048576 | tf_op jit(solution)/shard_map/attention_u/pallas_call | solution.py:177
  75.3 1.5 %collective-permute-start.17 = (bf16[256,512]{1,0:T(8,128)(2,1)}, bf16[256,512]{1,0:T(8,128)(2,1)S(1)}, u32[]{:S(2)}, u32[]{:S(2)}) collective-permute-start(bf16[256,512]{1,0:T(8,128)(2,1)} %get-tuple-element.22.refs_6_), channel_id=1, source_target_pairs={{0,1},{1,0},{2,3},{3,2},{4,5},{5,4},{6,7},{7,6},{8,9},{9,8},{10,11... | collective-permute-start | bytes 786440 | tf_op jit(solution)/shard_map/ppermute | solution.py:330
  76.9 0.0 collective-permute-done.2.refs_3_
  76.9 0.2 collective-permute-done.4.refs_5_
  77.1 0.5 copy-done.3
  77.6 0.7 copy-done.4
  78.3 4.6 %attention_v_other.1.refs_6_ = bf16[256,512]{1,0:T(8,128)(2,1)} custom-call(s32[8]{0:T(128)} %lengths.7, s32[32]{0:T(128)} %order.7, bf16[256,4096]{1,0:T(8,128)(2,1)} %refs_0_.11, bf16[256,1024]{1,0:T(8,128)(2,1)} %copy-done, bf16[512,256]{1,0:T(8,128)(2,1)} %copy-done.1, bf16[512,256]{1,0:T(8,128)(2,1)} %copy-done.3, bf16[512,256]{1,0:T(8,128)(2,1)} %copy-done.2, ...), custom_call_target="tpu_custom_call" | custom-call | flops 94371840 | bytes 524288 | tf_op jit(solution)/shard_map/attention_v_other/pallas_call | solution.py:177
  82.9 1.3 %collective-permute-start.18 = (bf16[256,512]{1,0:T(8,128)(2,1)}, bf16[256,512]{1,0:T(8,128)(2,1)S(1)}, u32[]{:S(2)}, u32[]{:S(2)}) collective-permute-start(bf16[256,512]{1,0:T(8,128)(2,1)} %attention_v_other.1.refs_6_), channel_id=1, source_target_pairs={{0,1},{1,0},{2,3},{3,2},{4,5},{5,4},{6,7},{7,6},{8,9},{9,8},{10,11... | collective-permute-start | bytes 786440 | tf_op jit(solution)/shard_map/ppermute | solution.py:330
  84.2 0.8 constant_dynamic-update-slice_fusion.2.refs_7_
  85.1 4.8 %attention_v_own.1 = bf16[256,4096]{1,0:T(8,128)(2,1)} custom-call(s32[8]{0:T(128)} %lengths.7, s32[32]{0:T(128)} %order.7, bf16[256,4096]{1,0:T(8,128)(2,1)} %refs_0_.11, bf16[256,1024]{1,0:T(8,128)(2,1)} %copy-done, bf16[512,256]{1,0:T(8,128)(2,1)} %copy-done.1, bf16[512,256]{1,0:T(8,128)(2,1)} %copy-done.3, ...), custom_call_target="tpu_custom_call", output_to_operand_aliasing={{}: (9, {})} | custom-call | flops 94371840 | bytes 524288 | tf_op jit(solution)/shard_map/attention_v_own/pallas_call | solution.py:177
  89.9 0.0 collective-permute-done.17
  89.9 0.7 constant_dynamic-update-slice_fusion.1
  90.6 0.7 constant_dynamic-update-slice_fusion
  (40 shorter events, 0.1 us)
Async XLA Ops:
  2.0 19.7 %copy-start.17 = (bf16[256,512]{1,0:T(8,128)(2,1)S(1)}, bf16[256,512]{1,0:T(8,128)(2,1)}, u32[]{:S(2)}) copy-start(bf16[256,512]{1,0:T(8,128)(2,1)} %get-tuple-element.17) | copy-start | bytes 786436
  2.0 10.3 %collective-permute-start.5 = (bf16[256,512]{1,0:T(8,128)(2,1)}, bf16[256,512]{1,0:T(8,128)(2,1)S(1)}, u32[]{:S(2)}, u32[]{:S(2)}) collective-permute-start(bf16[256,512]{1,0:T(8,128)(2,1)} %get-tuple-element.18), channel_id=1, source_target_pairs={{0,1},{1,0},{2,3},{3,2},{4,5},{5,4},{6,7},{7,6},{8,9},{9,8},{10,11... | collective-permute-start | bytes 786440 | tf_op jit(solution)/shard_map/ppermute | solution.py:330
  5.0 12.1 %collective-permute-start = (bf16[256,512]{1,0:T(8,128)(2,1)}, bf16[256,512]{1,0:T(8,128)(2,1)S(1)}, u32[]{:S(2)}, u32[]{:S(2)}) collective-permute-start(bf16[256,512]{1,0:T(8,128)(2,1)} %get-tuple-element.15), channel_id=1, source_target_pairs={{0,1},{1,0},{2,3},{3,2},{4,5},{5,4},{6,7},{7,6},{8,9},{9,8},{10,11... | collective-permute-start | bytes 786440 | tf_op jit(solution)/shard_map/ppermute | solution.py:330
  5.1 18.3 %collective-permute-start.13 = (bf16[256,512]{1,0:T(8,128)(2,1)}, bf16[256,512]{1,0:T(8,128)(2,1)S(1)}, u32[]{:S(2)}, u32[]{:S(2)}) collective-permute-start(bf16[256,512]{1,0:T(8,128)(2,1)} %get-tuple-element.20.refs_2_), channel_id=1, source_target_pairs={{0,6},{1,7},{2,4},{3,5},{4,2},{5,3},{6,0},{7,1},{8,14},{9,15},{10,... | collective-permute-start | bytes 786440 | tf_op jit(solution)/shard_map/ppermute | solution.py:336
  12.4 33.6 %copy-start.8 = (bf16[256,512]{1,0:T(8,128)(2,1)}, bf16[256,512]{1,0:T(8,128)(2,1)S(1)}, u32[]{:S(2)}) copy-start(bf16[256,512]{1,0:T(8,128)(2,1)S(1)} %collective-permute-done.5.refs_3_) | copy-start | bytes 786436
  12.4 14.7 %collective-permute-start.6 = (bf16[256,512]{1,0:T(8,128)(2,1)S(1)}, bf16[256,512]{1,0:T(8,128)(2,1)S(1)}, u32[]{:S(2)}, u32[]{:S(2)}) collective-permute-start(bf16[256,512]{1,0:T(8,128)(2,1)S(1)} %collective-permute-done.5.refs_3_), channel_id=1, source_target_pairs={{0,6},{1,7},{2,4},{3,5},{4,2},{5,3},{6,0},{7,1},{8,14},{9,15},{10,... | collective-permute-start | bytes 786440 | tf_op jit(solution)/shard_map/ppermute | solution.py:336
  16.5 16.9 %collective-permute-start.11 = (bf16[256,512]{1,0:T(8,128)(2,1)}, bf16[256,512]{1,0:T(8,128)(2,1)S(1)}, u32[]{:S(2)}, u32[]{:S(2)}) collective-permute-start(bf16[256,512]{1,0:T(8,128)(2,1)} %get-tuple-element.20.refs_2_), channel_id=1, source_target_pairs={{0,2},{1,3},{2,0},{3,1},{4,6},{5,7},{6,4},{7,5},{8,10},{9,11},{10,... | collective-permute-start | bytes 786440 | tf_op jit(solution)/shard_map/ppermute | solution.py:333
  17.2 0.7 copy-start.6
  19.9 26.1 %collective-permute-start.10 = (bf16[256,1024]{1,0:T(8,128)(2,1)}, bf16[256,1024]{1,0:T(8,128)(2,1)S(1)}, u32[]{:S(2)}, u32[]{:S(2)}) collective-permute-start(bf16[256,1024]{1,0:T(8,128)(2,1)} %get-tuple-element.19), channel_id=1, source_target_pairs={{0,1},{1,0},{2,3},{3,2},{4,5},{5,4},{6,7},{7,6},{8,9},{9,8},{10,11... | collective-permute-start | bytes 1572872 | tf_op jit(solution)/shard_map/ppermute | solution.py:330
  21.7 19.6 %collective-permute-start.12 = (bf16[256,512]{1,0:T(8,128)(2,1)S(1)}, bf16[256,512]{1,0:T(8,128)(2,1)S(1)}, u32[]{:S(2)}, u32[]{:S(2)}) collective-permute-start(bf16[256,512]{1,0:T(8,128)(2,1)S(1)} %collective-permute-done.5.refs_3_), channel_id=1, source_target_pairs={{0,2},{1,3},{2,0},{3,1},{4,6},{5,7},{6,4},{7,5},{8,10},{9,11},{10,... | collective-permute-start | bytes 786440 | tf_op jit(solution)/shard_map/ppermute | solution.py:333
  23.4 22.6 %copy-start.9 = (bf16[256,512]{1,0:T(8,128)(2,1)}, bf16[256,512]{1,0:T(8,128)(2,1)S(1)}, u32[]{:S(2)}) copy-start(bf16[256,512]{1,0:T(8,128)(2,1)S(1)} %collective-permute-done.13.refs_6_) | copy-start | bytes 786436
  23.4 16.4 %collective-permute-start.14 = (bf16[256,512]{1,0:T(8,128)(2,1)S(1)}, bf16[256,512]{1,0:T(8,128)(2,1)S(1)}, u32[]{:S(2)}, u32[]{:S(2)}) collective-permute-start(bf16[256,512]{1,0:T(8,128)(2,1)S(1)} %collective-permute-done.13.refs_6_), channel_id=1, source_target_pairs={{0,2},{1,3},{2,0},{3,1},{4,6},{5,7},{6,4},{7,5},{8,10},{9,11},{10,... | collective-permute-start | bytes 786440 | tf_op jit(solution)/shard_map/ppermute | solution.py:333
  27.1 6.3 %copy-start.5 = (bf16[256,512]{1,0:T(8,128)(2,1)}, bf16[256,512]{1,0:T(8,128)(2,1)S(1)}, u32[]{:S(2)}) copy-start(bf16[256,512]{1,0:T(8,128)(2,1)S(1)} %collective-permute-done.6.refs_1_.refs_7_) | copy-start | bytes 786436
  27.1 17.2 %collective-permute-start.15 = (bf16[256,512]{1,0:T(8,128)(2,1)S(1)}, bf16[256,512]{1,0:T(8,128)(2,1)S(1)}, u32[]{:S(2)}, u32[]{:S(2)}) collective-permute-start(bf16[256,512]{1,0:T(8,128)(2,1)S(1)} %collective-permute-done.6.refs_1_.refs_7_), channel_id=1, source_target_pairs={{0,2},{1,3},{2,0},{3,1},{4,6},{5,7},{6,4},{7,5},{8,10},{9,11},{10,... | collective-permute-start | bytes 786440 | tf_op jit(solution)/shard_map/ppermute | solution.py:333
  33.4 12.6 %copy-start.10 = (bf16[256,512]{1,0:T(8,128)(2,1)}, bf16[256,512]{1,0:T(8,128)(2,1)S(1)}, u32[]{:S(2)}) copy-start(bf16[256,512]{1,0:T(8,128)(2,1)S(1)} %collective-permute-done.11.refs_4_) | copy-start | bytes 786436
  33.4 30.1 %collective-permute-start.1 = (bf16[256,1024]{1,0:T(8,128)(2,1)}, bf16[256,1024]{1,0:T(8,128)(2,1)S(1)}, u32[]{:S(2)}, u32[]{:S(2)}) collective-permute-start(bf16[256,1024]{1,0:T(8,128)(2,1)} %get-tuple-element.16), channel_id=1, source_target_pairs={{0,1},{1,0},{2,3},{3,2},{4,5},{5,4},{6,7},{7,6},{8,9},{9,8},{10,11... | collective-permute-start | bytes 1572872 | tf_op jit(solution)/shard_map/ppermute | solution.py:330
  39.8 6.2 %copy-start.13 = (bf16[256,512]{1,0:T(8,128)(2,1)}, bf16[256,512]{1,0:T(8,128)(2,1)S(1)}, u32[]{:S(2)}) copy-start(bf16[256,512]{1,0:T(8,128)(2,1)S(1)} %collective-permute-done.14.refs_8_) | copy-start | bytes 786436
  39.8 18.3 %collective-permute-start.8 = (bf16[512,256]{1,0:T(8,128)(2,1)}, bf16[512,256]{1,0:T(8,128)(2,1)S(1)}, u32[]{:S(2)}, u32[]{:S(2)}) collective-permute-start(bf16[512,256]{1,0:T(8,128)(2,1)} %hold.1.refs_2_), channel_id=1, source_target_pairs={{0,6},{1,7},{2,4},{3,5},{4,2},{5,3},{6,0},{7,1},{8,14},{9,15},{10,... | collective-permute-start | bytes 786440 | tf_op jit(solution)/shard_map/ppermute | solution.py:336
  41.3 19.3 %copy-start.1 = (bf16[512,256]{1,0:T(8,128)(2,1)}, bf16[512,256]{1,0:T(8,128)(2,1)S(1)}, u32[]{:S(2)}) copy-start(bf16[512,256]{1,0:T(8,128)(2,1)S(1)} %pad_maximum_fusion.refs_2_) | copy-start | bytes 786436
  41.4 4.6 %copy-start.12 = (bf16[256,512]{1,0:T(8,128)(2,1)}, bf16[256,512]{1,0:T(8,128)(2,1)S(1)}, u32[]{:S(2)}) copy-start(bf16[256,512]{1,0:T(8,128)(2,1)S(1)} %collective-permute-done.12.refs_5_) | copy-start | bytes 786436
  41.4 19.2 %collective-permute-start.3 = (bf16[512,256]{1,0:T(8,128)(2,1)S(1)}, bf16[512,256]{1,0:T(8,128)(2,1)S(1)}, u32[]{:S(2)}, u32[]{:S(2)}) collective-permute-start(bf16[512,256]{1,0:T(8,128)(2,1)S(1)} %pad_maximum_fusion.refs_2_), channel_id=1, source_target_pairs={{0,6},{1,7},{2,4},{3,5},{4,2},{5,3},{6,0},{7,1},{8,14},{9,15},{10,... | collective-permute-start | bytes 786440 | tf_op jit(solution)/shard_map/ppermute | solution.py:336
  44.3 1.7 %copy-start.14 = (bf16[256,512]{1,0:T(8,128)(2,1)}, bf16[256,512]{1,0:T(8,128)(2,1)S(1)}, u32[]{:S(2)}) copy-start(bf16[256,512]{1,0:T(8,128)(2,1)S(1)} %collective-permute-done.15.refs_9_) | copy-start | bytes 786436
  44.3 19.1 %collective-permute-start.7 = (bf16[512,256]{1,0:T(8,128)(2,1)}, bf16[512,256]{1,0:T(8,128)(2,1)S(1)}, u32[]{:S(2)}, u32[]{:S(2)}) collective-permute-start(bf16[512,256]{1,0:T(8,128)(2,1)} %hold.1.refs_2_), channel_id=1, source_target_pairs={{0,2},{1,3},{2,0},{3,1},{4,6},{5,7},{6,4},{7,5},{8,10},{9,11},{10,... | collective-permute-start | bytes 786440 | tf_op jit(solution)/shard_map/ppermute | solution.py:333
  46.0 0.8 copy-start.7
  56.5 27.7 %collective-permute-start.16 = (bf16[256,1024]{1,0:T(8,128)(2,1)}, bf16[256,1024]{1,0:T(8,128)(2,1)S(1)}, u32[]{:S(2)}, u32[]{:S(2)}) collective-permute-start(bf16[256,1024]{1,0:T(8,128)(2,1)} %get-tuple-element.24), channel_id=1, source_target_pairs={{0,1},{1,0},{2,3},{3,2},{4,5},{5,4},{6,7},{7,6},{8,9},{9,8},{10,11... | collective-permute-start | bytes 1572872 | tf_op jit(solution)/shard_map/ppermute | solution.py:330
  58.1 9.8 %copy-start.11 = (bf16[512,256]{1,0:T(8,128)(2,1)}, bf16[512,256]{1,0:T(8,128)(2,1)S(1)}, u32[]{:S(2)}) copy-start(bf16[512,256]{1,0:T(8,128)(2,1)S(1)} %collective-permute-done.8.refs_4_) | copy-start | bytes 786436
  58.1 9.8 %collective-permute-start.9 = (bf16[512,256]{1,0:T(8,128)(2,1)S(1)}, bf16[512,256]{1,0:T(8,128)(2,1)S(1)}, u32[]{:S(2)}, u32[]{:S(2)}) collective-permute-start(bf16[512,256]{1,0:T(8,128)(2,1)S(1)} %collective-permute-done.8.refs_4_), channel_id=1, source_target_pairs={{0,2},{1,3},{2,0},{3,1},{4,6},{5,7},{6,4},{7,5},{8,10},{9,11},{10,... | collective-permute-start | bytes 786440 | tf_op jit(solution)/shard_map/ppermute | solution.py:333
  60.6 16.5 %copy-start.2 = (bf16[512,256]{1,0:T(8,128)(2,1)}, bf16[512,256]{1,0:T(8,128)(2,1)S(1)}, u32[]{:S(2)}) copy-start(bf16[512,256]{1,0:T(8,128)(2,1)S(1)} %collective-permute-done.3.refs_4_) | copy-start | bytes 786436
  60.6 16.3 %collective-permute-start.2 = (bf16[512,256]{1,0:T(8,128)(2,1)S(1)}, bf16[512,256]{1,0:T(8,128)(2,1)S(1)}, u32[]{:S(2)}, u32[]{:S(2)}) collective-permute-start(bf16[512,256]{1,0:T(8,128)(2,1)S(1)} %pad_maximum_fusion.refs_2_), channel_id=1, source_target_pairs={{0,2},{1,3},{2,0},{3,1},{4,6},{5,7},{6,4},{7,5},{8,10},{9,11},{10,... | collective-permute-start | bytes 786440 | tf_op jit(solution)/shard_map/ppermute | solution.py:333
  63.4 4.4 %copy-start.15 = (bf16[512,256]{1,0:T(8,128)(2,1)}, bf16[512,256]{1,0:T(8,128)(2,1)S(1)}, u32[]{:S(2)}) copy-start(bf16[512,256]{1,0:T(8,128)(2,1)S(1)} %collective-permute-done.7.refs_3_) | copy-start | bytes 786436
  63.4 13.7 %collective-permute-start.4 = (bf16[512,256]{1,0:T(8,128)(2,1)S(1)}, bf16[512,256]{1,0:T(8,128)(2,1)S(1)}, u32[]{:S(2)}, u32[]{:S(2)}) collective-permute-start(bf16[512,256]{1,0:T(8,128)(2,1)S(1)} %collective-permute-done.3.refs_4_), channel_id=1, source_target_pairs={{0,2},{1,3},{2,0},{3,1},{4,6},{5,7},{6,4},{7,5},{8,10},{9,11},{10,... | collective-permute-start | bytes 786440 | tf_op jit(solution)/shard_map/ppermute | solution.py:333
  63.5 4.3 %copy-start = (bf16[256,1024]{1,0:T(8,128)(2,1)}, bf16[256,1024]{1,0:T(8,128)(2,1)S(1)}, u32[]{:S(2)}) copy-start(bf16[256,1024]{1,0:T(8,128)(2,1)S(1)} %collective-permute-done.1.refs_1_) | copy-start | bytes 1572868
  67.8 0.7 copy-start.16
  75.3 14.6 %collective-permute-start.17 = (bf16[256,512]{1,0:T(8,128)(2,1)}, bf16[256,512]{1,0:T(8,128)(2,1)S(1)}, u32[]{:S(2)}, u32[]{:S(2)}) collective-permute-start(bf16[256,512]{1,0:T(8,128)(2,1)} %get-tuple-element.22.refs_6_), channel_id=1, source_target_pairs={{0,1},{1,0},{2,3},{3,2},{4,5},{5,4},{6,7},{7,6},{8,9},{9,8},{10,11... | collective-permute-start | bytes 786440 | tf_op jit(solution)/shard_map/ppermute | solution.py:330
  76.9 0.7 copy-start.3
  77.6 0.7 copy-start.4
  82.9 7.7 %collective-permute-start.18 = (bf16[256,512]{1,0:T(8,128)(2,1)}, bf16[256,512]{1,0:T(8,128)(2,1)S(1)}, u32[]{:S(2)}, u32[]{:S(2)}) collective-permute-start(bf16[256,512]{1,0:T(8,128)(2,1)} %attention_v_other.1.refs_6_), channel_id=1, source_target_pairs={{0,1},{1,0},{2,3},{3,2},{4,5},{5,4},{6,7},{7,6},{8,9},{9,8},{10,11... | collective-permute-start | bytes 786440 | tf_op jit(solution)/shard_map/ppermute | solution.py:330

commit v5 on v4

--- a/solution.py
+++ b/solution.py
@@ -20,7 +20,7 @@
 COST = {1: 0.3, 2: 1}
 VMEM_BYTES = 60 * 1024 * 1024
 COUNTS = tuple(range(1, MOST_STEPS + 1))
-TOGETHER = {1: 2, 2: 2}
+TOGETHER = {1: 2, 2: 1}
 
 
 def attend_spans(lengths, positions, heads, load_q, store_out, kv):

time: 91 us -> 91.2 us (level); the launches traced: 91.4 us -> 90.4 us
  Pallas kernels: 29.9 us -> 25.8 us
  starting transfers between devices: 40 us -> 42.4 us
  waiting for transfers between devices: 13.8 us -> 15 us
    pallas_call x4, Pallas kernels: 25.9 us -> 21.8 us  [attention(): pl.pallas_call(kernel, out_shape=shapes, in_specs=[smem, smem] + [hbm] *...]
    ppermute x8, starting transfers between devices: 17.1 us -> 18.7 us  [swap_outer(): return lax.ppermute(a, both, outer)]
    ppermute x8, waiting for transfers between devices: 9.91 us -> 11.1 us  [swap_outer(): return lax.ppermute(a, both, outer)]
  transfers between devices with their start and end apart: 19 -> 19, of which waited for: 6 -> 6; matrix products, arithmetic and copies ran while one was open for 4% -> 4% of each run, Pallas kernels for 31% -> 26%
where the time goes in v5:
time: 91.2 us; the launch traced here: 90.4 us
  starting transfers between devices  42.4 us (46%)
  Pallas kernels  25.8 us (28%)
  waiting for transfers between devices  15 us (16%)
  local copies, waits for them, and re-layouts  6.23 us (7%)
    pallas_call x4, Pallas kernels, attention(): pl.pallas_call(kernel, out_shape=shapes, in_specs=[smem, smem] + [hbm] *...  21.8 us
    ppermute x8, starting transfers between devices, swap_outer(): return lax.ppermute(a, both, outer)  18.7 us
    ppermute x4, starting transfers between devices, swap_ends(): return lax.ppermute(a, both, ends)  12.1 us
    ppermute x7, starting transfers between devices, swap_x(): return lax.ppermute(a, both, across)  11.6 us
    ppermute x8, waiting for transfers between devices, swap_outer(): return lax.ppermute(a, both, outer)  11.1 us
    pallas_call x2, Pallas kernels, split(): pl.pallas_call(kernel, out_shape=[jax.ShapeDtypeStruct((n, width), jnp.bf...  4.02 us
    ppermute x7, waiting for transfers between devices, swap_x(): return lax.ppermute(a, both, across)  3.83 us
    unnamed x36, local copies, waits for them, and re-layouts  2.96 us
  transfers between devices with their start and end apart: 19, of which 6 were waited for; matrix products, arithmetic and copies ran while one was open for 4% of the time, Pallas kernels for 26%

profile of v5, /device:TPU:0, one launch (start us, length us, event | category | flops | bytes accessed | tf_op | source)
XLA Modules:
  0.0 90.4 jit_solution(11482617935927943938)
XLA Ops:
  0.0 2.0 %split_kv.1 = (bf16[256,512]{1,0:T(8,128)(2,1)}, bf16[256,512]{1,0:T(8,128)(2,1)}, bf16[256,512]{1,0:T(8,128)(2,1)}, bf16[256,512]{1,0:T(8,128)(2,1)}) custom-call(bf16[256,1024]{1,0:T(8,128)(2,1)} %refs_0_.6, bf16[256,1024]{1,0:T(8,128)(2,1)} %refs_1_.1), custom_call_target="tpu_custom_call" | custom-call | bytes 2097152 | tf_op jit(solution)/shard_map/split_kv/pallas_call | solution.py:225
  2.0 3.0 %collective-permute-start.5 = (bf16[256,512]{1,0:T(8,128)(2,1)}, bf16[256,512]{1,0:T(8,128)(2,1)S(1)}, u32[]{:S(2)}, u32[]{:S(2)}) collective-permute-start(bf16[256,512]{1,0:T(8,128)(2,1)} %get-tuple-element.18), channel_id=1, source_target_pairs={{0,1},{1,0},{2,3},{3,2},{4,5},{5,4},{6,7},{7,6},{8,9},{9,8},{10,11... | collective-permute-start | bytes 786440 | tf_op jit(solution)/shard_map/ppermute | solution.py:330
  5.0 0.1 collective-permute-start
  5.1 4.1 %collective-permute-start.13 = (bf16[256,512]{1,0:T(8,128)(2,1)}, bf16[256,512]{1,0:T(8,128)(2,1)S(1)}, u32[]{:S(2)}, u32[]{:S(2)}) collective-permute-start(bf16[256,512]{1,0:T(8,128)(2,1)} %get-tuple-element.20.refs_2_), channel_id=1, source_target_pairs={{0,6},{1,7},{2,4},{3,5},{4,2},{5,3},{6,0},{7,1},{8,14},{9,15},{10,... | collective-permute-start | bytes 786440 | tf_op jit(solution)/shard_map/ppermute | solution.py:336
  9.2 3.2 %collective-permute-done.5.refs_3_ = bf16[256,512]{1,0:T(8,128)(2,1)S(1)} collective-permute-done((bf16[256,512]{1,0:T(8,128)(2,1)}, bf16[256,512]{1,0:T(8,128)(2,1)S(1)}, u32[]{:S(2)}, u32[]{:S(2)}) %collective-permute-start.5) | collective-permute-done | bytes 262176 | tf_op jit(solution)/shard_map/ppermute | solution.py:330
  12.4 4.2 %collective-permute-start.6 = (bf16[256,512]{1,0:T(8,128)(2,1)S(1)}, bf16[256,512]{1,0:T(8,128)(2,1)S(1)}, u32[]{:S(2)}, u32[]{:S(2)}) collective-permute-start(bf16[256,512]{1,0:T(8,128)(2,1)S(1)} %collective-permute-done.5.refs_3_), channel_id=1, source_target_pairs={{0,6},{1,7},{2,4},{3,5},{4,2},{5,3},{6,0},{7,1},{8,14},{9,15},{10,... | collective-permute-start | bytes 786440 | tf_op jit(solution)/shard_map/ppermute | solution.py:336
  16.5 0.0 collective-permute-start.11
  16.5 0.6 collective-permute-done.refs_1_
  17.2 0.7 copy-done.6
  17.9 2.0 %split_q.1 = (bf16[256,1024]{1,0:T(8,128)(2,1)}, bf16[256,1024]{1,0:T(8,128)(2,1)}) custom-call(bf16[256,4096]{1,0:T(8,128)(2,1)} %refs_0_.11, bf16[256,512]{1,0:T(8,128)(2,1)} %copy-done.6), custom_call_target="tpu_custom_call" | custom-call | bytes 2097152 | tf_op jit(solution)/shard_map/split_q/pallas_call | solution.py:225
  19.9 1.8 %collective-permute-start.10 = (bf16[256,1024]{1,0:T(8,128)(2,1)}, bf16[256,1024]{1,0:T(8,128)(2,1)S(1)}, u32[]{:S(2)}, u32[]{:S(2)}) collective-permute-start(bf16[256,1024]{1,0:T(8,128)(2,1)} %get-tuple-element.19), channel_id=1, source_target_pairs={{0,1},{1,0},{2,3},{3,2},{4,5},{5,4},{6,7},{7,6},{8,9},{9,8},{10,11... | collective-permute-start | bytes 1572872 | tf_op jit(solution)/shard_map/ppermute | solution.py:330
  21.7 1.6 %collective-permute-start.12 = (bf16[256,512]{1,0:T(8,128)(2,1)S(1)}, bf16[256,512]{1,0:T(8,128)(2,1)S(1)}, u32[]{:S(2)}, u32[]{:S(2)}) collective-permute-start(bf16[256,512]{1,0:T(8,128)(2,1)S(1)} %collective-permute-done.5.refs_3_), channel_id=1, source_target_pairs={{0,2},{1,3},{2,0},{3,1},{4,6},{5,7},{6,4},{7,5},{8,10},{9,11},{10,... | collective-permute-start | bytes 786440 | tf_op jit(solution)/shard_map/ppermute | solution.py:333
  23.4 0.0 collective-permute-done.13.refs_6_
  23.4 3.7 %collective-permute-start.14 = (bf16[256,512]{1,0:T(8,128)(2,1)S(1)}, bf16[256,512]{1,0:T(8,128)(2,1)S(1)}, u32[]{:S(2)}, u32[]{:S(2)}) collective-permute-start(bf16[256,512]{1,0:T(8,128)(2,1)S(1)} %collective-permute-done.13.refs_6_), channel_id=1, source_target_pairs={{0,2},{1,3},{2,0},{3,1},{4,6},{5,7},{6,4},{7,5},{8,10},{9,11},{10,... | collective-permute-start | bytes 786440 | tf_op jit(solution)/shard_map/ppermute | solution.py:333
  27.1 0.0 collective-permute-done.6.refs_1_.refs_7_
  27.1 4.6 %collective-permute-start.15 = (bf16[256,512]{1,0:T(8,128)(2,1)S(1)}, bf16[256,512]{1,0:T(8,128)(2,1)S(1)}, u32[]{:S(2)}, u32[]{:S(2)}) collective-permute-start(bf16[256,512]{1,0:T(8,128)(2,1)S(1)} %collective-permute-done.6.refs_1_.refs_7_), channel_id=1, source_target_pairs={{0,2},{1,3},{2,0},{3,1},{4,6},{5,7},{6,4},{7,5},{8,10},{9,11},{10,... | collective-permute-start | bytes 786440 | tf_op jit(solution)/shard_map/ppermute | solution.py:333
  31.7 1.0 %fusion.1 = (bf16[256,256]{1,0:T(8,128)(2,1)S(1)}, bf16[256,256]{1,0:T(8,128)(2,1)S(1)}) fusion(bf16[256,512]{1,0:T(8,128)(2,1)} %copy-done.6), kind=kLoop, calls=%fused_computation.6 | loop fusion | bytes 524288 | tf_op jit(solution)/shard_map/slice | solution.py:366
  32.7 0.7 pad_maximum_fusion.1.refs_0_
  33.4 1.6 %collective-permute-start.1 = (bf16[256,1024]{1,0:T(8,128)(2,1)}, bf16[256,1024]{1,0:T(8,128)(2,1)S(1)}, u32[]{:S(2)}, u32[]{:S(2)}) collective-permute-start(bf16[256,1024]{1,0:T(8,128)(2,1)} %get-tuple-element.16), channel_id=1, source_target_pairs={{0,1},{1,0},{2,3},{3,2},{4,5},{5,4},{6,7},{7,6},{8,9},{9,8},{10,11... | collective-permute-start | bytes 1572872 | tf_op jit(solution)/shard_map/ppermute | solution.py:330
  35.0 4.8 %collective-permute-done.14.refs_8_ = bf16[256,512]{1,0:T(8,128)(2,1)S(1)} collective-permute-done((bf16[256,512]{1,0:T(8,128)(2,1)S(1)}, bf16[256,512]{1,0:T(8,128)(2,1)S(1)}, u32[]{:S(2)}, u32[]{:S(2)}) %collective-permute-start.14) | collective-permute-done | bytes 262176 | tf_op jit(solution)/shard_map/ppermute | solution.py:333
  39.8 1.6 %collective-permute-start.8 = (bf16[512,256]{1,0:T(8,128)(2,1)}, bf16[512,256]{1,0:T(8,128)(2,1)S(1)}, u32[]{:S(2)}, u32[]{:S(2)}) collective-permute-start(bf16[512,256]{1,0:T(8,128)(2,1)} %hold.1.refs_2_), channel_id=1, source_target_pairs={{0,6},{1,7},{2,4},{3,5},{4,2},{5,3},{6,0},{7,1},{8,14},{9,15},{10,... | collective-permute-start | bytes 786440 | tf_op jit(solution)/shard_map/ppermute | solution.py:336
  41.4 0.0 collective-permute-done.12.refs_5_
  41.4 2.3 %collective-permute-start.3 = (bf16[512,256]{1,0:T(8,128)(2,1)S(1)}, bf16[512,256]{1,0:T(8,128)(2,1)S(1)}, u32[]{:S(2)}, u32[]{:S(2)}) collective-permute-start(bf16[512,256]{1,0:T(8,128)(2,1)S(1)} %pad_maximum_fusion.refs_2_), channel_id=1, source_target_pairs={{0,6},{1,7},{2,4},{3,5},{4,2},{5,3},{6,0},{7,1},{8,14},{9,15},{10,... | collective-permute-start | bytes 786440 | tf_op jit(solution)/shard_map/ppermute | solution.py:336
  43.7 0.6 collective-permute-done.15.refs_9_
  44.3 1.7 %collective-permute-start.7 = (bf16[512,256]{1,0:T(8,128)(2,1)}, bf16[512,256]{1,0:T(8,128)(2,1)S(1)}, u32[]{:S(2)}, u32[]{:S(2)}) collective-permute-start(bf16[512,256]{1,0:T(8,128)(2,1)} %hold.1.refs_2_), channel_id=1, source_target_pairs={{0,2},{1,3},{2,0},{3,1},{4,6},{5,7},{6,4},{7,5},{8,10},{9,11},{10,... | collective-permute-start | bytes 786440 | tf_op jit(solution)/shard_map/ppermute | solution.py:333
  46.0 0.8 copy-done.7
  46.8 8.1 %attention_t.1 = (bf16[256,1024]{1,0:T(8,128)(2,1)}, bf16[256,4096]{1,0:T(8,128)(2,1)}) custom-call(s32[8]{0:T(128)} %lengths.7, s32[32]{0:T(128)} %order.7, bf16[256,4096]{1,0:T(8,128)(2,1)} %refs_0_.11, bf16[256,1024]{1,0:T(8,128)(2,1)} %copy-done.7, bf16[256,512]{1,0:T(8,128)(2,1)} %get-tuple-element.20.refs_2_, bf16[256,512]{1,0:T(8,128)(2,1)} %copy-done.8, ...), custom_call_target="tpu_custom_call" | custom-call | flops 1258291200 | bytes 2097152 | tf_op jit(solution)/shard_map/attention_t/pallas_call | solution.py:177
  54.9 1.5 %collective-permute-start.16 = (bf16[256,1024]{1,0:T(8,128)(2,1)}, bf16[256,1024]{1,0:T(8,128)(2,1)S(1)}, u32[]{:S(2)}, u32[]{:S(2)}) collective-permute-start(bf16[256,1024]{1,0:T(8,128)(2,1)} %get-tuple-element.24), channel_id=1, source_target_pairs={{0,1},{1,0},{2,3},{3,2},{4,5},{5,4},{6,7},{7,6},{8,9},{9,8},{10,11... | collective-permute-start | bytes 1572872 | tf_op jit(solution)/shard_map/ppermute | solution.py:330
  56.4 4.2 %collective-permute-start.9 = (bf16[512,256]{1,0:T(8,128)(2,1)S(1)}, bf16[512,256]{1,0:T(8,128)(2,1)S(1)}, u32[]{:S(2)}, u32[]{:S(2)}) collective-permute-start(bf16[512,256]{1,0:T(8,128)(2,1)S(1)} %collective-permute-done.8.refs_4_), channel_id=1, source_target_pairs={{0,2},{1,3},{2,0},{3,1},{4,6},{5,7},{6,4},{7,5},{8,10},{9,11},{10,... | collective-permute-start | bytes 786440 | tf_op jit(solution)/shard_map/ppermute | solution.py:333
  60.6 0.0 collective-permute-done.3.refs_4_
  60.6 2.8 %collective-permute-start.2 = (bf16[512,256]{1,0:T(8,128)(2,1)S(1)}, bf16[512,256]{1,0:T(8,128)(2,1)S(1)}, u32[]{:S(2)}, u32[]{:S(2)}) collective-permute-start(bf16[512,256]{1,0:T(8,128)(2,1)S(1)} %pad_maximum_fusion.refs_2_), channel_id=1, source_target_pairs={{0,2},{1,3},{2,0},{3,1},{4,6},{5,7},{6,4},{7,5},{8,10},{9,11},{10,... | collective-permute-start | bytes 786440 | tf_op jit(solution)/shard_map/ppermute | solution.py:333
  63.4 0.1 collective-permute-start.4
  63.5 0.0 collective-permute-done.1.refs_1_
  63.5 4.3 %collective-permute-done.9.refs_5_ = bf16[512,256]{1,0:T(8,128)(2,1)S(1)} collective-permute-done((bf16[512,256]{1,0:T(8,128)(2,1)S(1)}, bf16[512,256]{1,0:T(8,128)(2,1)S(1)}, u32[]{:S(2)}, u32[]{:S(2)}) %collective-permute-start.9) | collective-permute-done | bytes 262176 | tf_op jit(solution)/shard_map/ppermute | solution.py:333
  67.9 0.7 copy-done.16
  68.6 5.5 %attention_u.1 = (bf16[256,512]{1,0:T(8,128)(2,1)}, bf16[256,4096]{1,0:T(8,128)(2,1)}) custom-call(s32[8]{0:T(128)} %lengths.7, s32[32]{0:T(128)} %order.7, bf16[256,4096]{1,0:T(8,128)(2,1)} %refs_0_.11, bf16[256,1024]{1,0:T(8,128)(2,1)} %copy-done, bf16[512,256]{1,0:T(8,128)(2,1)} %hold.1.refs_2_, ...), custom_call_target="tpu_custom_call", output_to_operand_aliasing={{1}: (8, {})} | custom-call | flops 188743680 | bytes 1048576 | tf_op jit(solution)/shard_map/attention_u/pallas_call | solution.py:177
  74.1 1.6 %collective-permute-start.17 = (bf16[256,512]{1,0:T(8,128)(2,1)}, bf16[256,512]{1,0:T(8,128)(2,1)S(1)}, u32[]{:S(2)}, u32[]{:S(2)}) collective-permute-start(bf16[256,512]{1,0:T(8,128)(2,1)} %get-tuple-element.22.refs_6_), channel_id=1, source_target_pairs={{0,1},{1,0},{2,3},{3,2},{4,5},{5,4},{6,7},{7,6},{8,9},{9,8},{10,11... | collective-permute-start | bytes 786440 | tf_op jit(solution)/shard_map/ppermute | solution.py:330
  75.7 1.4 %collective-permute-done.4.refs_5_ = bf16[512,256]{1,0:T(8,128)(2,1)S(1)} collective-permute-done((bf16[512,256]{1,0:T(8,128)(2,1)S(1)}, bf16[512,256]{1,0:T(8,128)(2,1)S(1)}, u32[]{:S(2)}, u32[]{:S(2)}) %collective-permute-start.4) | collective-permute-done | bytes 262176 | tf_op jit(solution)/shard_map/ppermute | solution.py:333
  77.1 0.7 copy-done.4
  77.8 3.8 %attention_v_other.1.refs_6_ = bf16[256,512]{1,0:T(8,128)(2,1)} custom-call(s32[8]{0:T(128)} %lengths.7, s32[32]{0:T(128)} %order.7, bf16[256,4096]{1,0:T(8,128)(2,1)} %refs_0_.11, bf16[256,1024]{1,0:T(8,128)(2,1)} %copy-done, bf16[512,256]{1,0:T(8,128)(2,1)} %copy-done.1, bf16[512,256]{1,0:T(8,128)(2,1)} %copy-done.3, bf16[512,256]{1,0:T(8,128)(2,1)} %copy-done.2, ...), custom_call_target="tpu_custom_call" | custom-call | flops 94371840 | bytes 524288 | tf_op jit(solution)/shard_map/attention_v_other/pallas_call | solution.py:177
  81.7 2.1 %collective-permute-start.18 = (bf16[256,512]{1,0:T(8,128)(2,1)}, bf16[256,512]{1,0:T(8,128)(2,1)S(1)}, u32[]{:S(2)}, u32[]{:S(2)}) collective-permute-start(bf16[256,512]{1,0:T(8,128)(2,1)} %attention_v_other.1.refs_6_), channel_id=1, source_target_pairs={{0,1},{1,0},{2,3},{3,2},{4,5},{5,4},{6,7},{7,6},{8,9},{9,8},{10,11... | collective-permute-start | bytes 786440 | tf_op jit(solution)/shard_map/ppermute | solution.py:330
  83.7 0.0 collective-permute-done.16
  83.8 0.8 constant_dynamic-update-slice_fusion.2.refs_7_
  84.6 4.4 %attention_v_own.1 = bf16[256,4096]{1,0:T(8,128)(2,1)} custom-call(s32[8]{0:T(128)} %lengths.7, s32[32]{0:T(128)} %order.7, bf16[256,4096]{1,0:T(8,128)(2,1)} %refs_0_.11, bf16[256,1024]{1,0:T(8,128)(2,1)} %copy-done, bf16[512,256]{1,0:T(8,128)(2,1)} %copy-done.1, bf16[512,256]{1,0:T(8,128)(2,1)} %copy-done.3, ...), custom_call_target="tpu_custom_call", output_to_operand_aliasing={{}: (9, {})} | custom-call | flops 94371840 | bytes 524288 | tf_op jit(solution)/shard_map/attention_v_own/pallas_call | solution.py:177
  88.9 0.0 collective-permute-done.17
  89.0 0.7 constant_dynamic-update-slice_fusion.1
  89.7 0.0 collective-permute-done.18
  89.7 0.7 constant_dynamic-update-slice_fusion
  (40 shorter events, 0.1 us)
Async XLA Ops:
  2.0 19.7 %copy-start.17 = (bf16[256,512]{1,0:T(8,128)(2,1)S(1)}, bf16[256,512]{1,0:T(8,128)(2,1)}, u32[]{:S(2)}) copy-start(bf16[256,512]{1,0:T(8,128)(2,1)} %get-tuple-element.17) | copy-start | bytes 786436
  2.0 10.3 %collective-permute-start.5 = (bf16[256,512]{1,0:T(8,128)(2,1)}, bf16[256,512]{1,0:T(8,128)(2,1)S(1)}, u32[]{:S(2)}, u32[]{:S(2)}) collective-permute-start(bf16[256,512]{1,0:T(8,128)(2,1)} %get-tuple-element.18), channel_id=1, source_target_pairs={{0,1},{1,0},{2,3},{3,2},{4,5},{5,4},{6,7},{7,6},{8,9},{9,8},{10,11... | collective-permute-start | bytes 786440 | tf_op jit(solution)/shard_map/ppermute | solution.py:330
  5.0 12.1 %collective-permute-start = (bf16[256,512]{1,0:T(8,128)(2,1)}, bf16[256,512]{1,0:T(8,128)(2,1)S(1)}, u32[]{:S(2)}, u32[]{:S(2)}) collective-permute-start(bf16[256,512]{1,0:T(8,128)(2,1)} %get-tuple-element.15), channel_id=1, source_target_pairs={{0,1},{1,0},{2,3},{3,2},{4,5},{5,4},{6,7},{7,6},{8,9},{9,8},{10,11... | collective-permute-start | bytes 786440 | tf_op jit(solution)/shard_map/ppermute | solution.py:330
  5.1 18.3 %collective-permute-start.13 = (bf16[256,512]{1,0:T(8,128)(2,1)}, bf16[256,512]{1,0:T(8,128)(2,1)S(1)}, u32[]{:S(2)}, u32[]{:S(2)}) collective-permute-start(bf16[256,512]{1,0:T(8,128)(2,1)} %get-tuple-element.20.refs_2_), channel_id=1, source_target_pairs={{0,6},{1,7},{2,4},{3,5},{4,2},{5,3},{6,0},{7,1},{8,14},{9,15},{10,... | collective-permute-start | bytes 786440 | tf_op jit(solution)/shard_map/ppermute | solution.py:336
  12.4 33.6 %copy-start.8 = (bf16[256,512]{1,0:T(8,128)(2,1)}, bf16[256,512]{1,0:T(8,128)(2,1)S(1)}, u32[]{:S(2)}) copy-start(bf16[256,512]{1,0:T(8,128)(2,1)S(1)} %collective-permute-done.5.refs_3_) | copy-start | bytes 786436
  12.4 14.7 %collective-permute-start.6 = (bf16[256,512]{1,0:T(8,128)(2,1)S(1)}, bf16[256,512]{1,0:T(8,128)(2,1)S(1)}, u32[]{:S(2)}, u32[]{:S(2)}) collective-permute-start(bf16[256,512]{1,0:T(8,128)(2,1)S(1)} %collective-permute-done.5.refs_3_), channel_id=1, source_target_pairs={{0,6},{1,7},{2,4},{3,5},{4,2},{5,3},{6,0},{7,1},{8,14},{9,15},{10,... | collective-permute-start | bytes 786440 | tf_op jit(solution)/shard_map/ppermute | solution.py:336
  16.5 16.9 %collective-permute-start.11 = (bf16[256,512]{1,0:T(8,128)(2,1)}, bf16[256,512]{1,0:T(8,128)(2,1)S(1)}, u32[]{:S(2)}, u32[]{:S(2)}) collective-permute-start(bf16[256,512]{1,0:T(8,128)(2,1)} %get-tuple-element.20.refs_2_), channel_id=1, source_target_pairs={{0,2},{1,3},{2,0},{3,1},{4,6},{5,7},{6,4},{7,5},{8,10},{9,11},{10,... | collective-permute-start | bytes 786440 | tf_op jit(solution)/shard_map/ppermute | solution.py:333
  17.2 0.7 copy-start.6
  19.9 26.1 %collective-permute-start.10 = (bf16[256,1024]{1,0:T(8,128)(2,1)}, bf16[256,1024]{1,0:T(8,128)(2,1)S(1)}, u32[]{:S(2)}, u32[]{:S(2)}) collective-permute-start(bf16[256,1024]{1,0:T(8,128)(2,1)} %get-tuple-element.19), channel_id=1, source_target_pairs={{0,1},{1,0},{2,3},{3,2},{4,5},{5,4},{6,7},{7,6},{8,9},{9,8},{10,11... | collective-permute-start | bytes 1572872 | tf_op jit(solution)/shard_map/ppermute | solution.py:330
  21.7 19.6 %collective-permute-start.12 = (bf16[256,512]{1,0:T(8,128)(2,1)S(1)}, bf16[256,512]{1,0:T(8,128)(2,1)S(1)}, u32[]{:S(2)}, u32[]{:S(2)}) collective-permute-start(bf16[256,512]{1,0:T(8,128)(2,1)S(1)} %collective-permute-done.5.refs_3_), channel_id=1, source_target_pairs={{0,2},{1,3},{2,0},{3,1},{4,6},{5,7},{6,4},{7,5},{8,10},{9,11},{10,... | collective-permute-start | bytes 786440 | tf_op jit(solution)/shard_map/ppermute | solution.py:333
  23.4 22.6 %copy-start.9 = (bf16[256,512]{1,0:T(8,128)(2,1)}, bf16[256,512]{1,0:T(8,128)(2,1)S(1)}, u32[]{:S(2)}) copy-start(bf16[256,512]{1,0:T(8,128)(2,1)S(1)} %collective-permute-done.13.refs_6_) | copy-start | bytes 786436
  23.4 16.4 %collective-permute-start.14 = (bf16[256,512]{1,0:T(8,128)(2,1)S(1)}, bf16[256,512]{1,0:T(8,128)(2,1)S(1)}, u32[]{:S(2)}, u32[]{:S(2)}) collective-permute-start(bf16[256,512]{1,0:T(8,128)(2,1)S(1)} %collective-permute-done.13.refs_6_), channel_id=1, source_target_pairs={{0,2},{1,3},{2,0},{3,1},{4,6},{5,7},{6,4},{7,5},{8,10},{9,11},{10,... | collective-permute-start | bytes 786440 | tf_op jit(solution)/shard_map/ppermute | solution.py:333
  27.1 6.3 %copy-start.5 = (bf16[256,512]{1,0:T(8,128)(2,1)}, bf16[256,512]{1,0:T(8,128)(2,1)S(1)}, u32[]{:S(2)}) copy-start(bf16[256,512]{1,0:T(8,128)(2,1)S(1)} %collective-permute-done.6.refs_1_.refs_7_) | copy-start | bytes 786436
  27.1 17.2 %collective-permute-start.15 = (bf16[256,512]{1,0:T(8,128)(2,1)S(1)}, bf16[256,512]{1,0:T(8,128)(2,1)S(1)}, u32[]{:S(2)}, u32[]{:S(2)}) collective-permute-start(bf16[256,512]{1,0:T(8,128)(2,1)S(1)} %collective-permute-done.6.refs_1_.refs_7_), channel_id=1, source_target_pairs={{0,2},{1,3},{2,0},{3,1},{4,6},{5,7},{6,4},{7,5},{8,10},{9,11},{10,... | collective-permute-start | bytes 786440 | tf_op jit(solution)/shard_map/ppermute | solution.py:333
  33.4 12.6 %copy-start.10 = (bf16[256,512]{1,0:T(8,128)(2,1)}, bf16[256,512]{1,0:T(8,128)(2,1)S(1)}, u32[]{:S(2)}) copy-start(bf16[256,512]{1,0:T(8,128)(2,1)S(1)} %collective-permute-done.11.refs_4_) | copy-start | bytes 786436
  33.4 30.1 %collective-permute-start.1 = (bf16[256,1024]{1,0:T(8,128)(2,1)}, bf16[256,1024]{1,0:T(8,128)(2,1)S(1)}, u32[]{:S(2)}, u32[]{:S(2)}) collective-permute-start(bf16[256,1024]{1,0:T(8,128)(2,1)} %get-tuple-element.16), channel_id=1, source_target_pairs={{0,1},{1,0},{2,3},{3,2},{4,5},{5,4},{6,7},{7,6},{8,9},{9,8},{10,11... | collective-permute-start | bytes 1572872 | tf_op jit(solution)/shard_map/ppermute | solution.py:330
  39.8 6.2 %copy-start.13 = (bf16[256,512]{1,0:T(8,128)(2,1)}, bf16[256,512]{1,0:T(8,128)(2,1)S(1)}, u32[]{:S(2)}) copy-start(bf16[256,512]{1,0:T(8,128)(2,1)S(1)} %collective-permute-done.14.refs_8_) | copy-start | bytes 786436
  39.8 16.7 %collective-permute-start.8 = (bf16[512,256]{1,0:T(8,128)(2,1)}, bf16[512,256]{1,0:T(8,128)(2,1)S(1)}, u32[]{:S(2)}, u32[]{:S(2)}) collective-permute-start(bf16[512,256]{1,0:T(8,128)(2,1)} %hold.1.refs_2_), channel_id=1, source_target_pairs={{0,6},{1,7},{2,4},{3,5},{4,2},{5,3},{6,0},{7,1},{8,14},{9,15},{10,... | collective-permute-start | bytes 786440 | tf_op jit(solution)/shard_map/ppermute | solution.py:336
  41.3 19.3 %copy-start.1 = (bf16[512,256]{1,0:T(8,128)(2,1)}, bf16[512,256]{1,0:T(8,128)(2,1)S(1)}, u32[]{:S(2)}) copy-start(bf16[512,256]{1,0:T(8,128)(2,1)S(1)} %pad_maximum_fusion.refs_2_) | copy-start | bytes 786436
  41.4 4.6 %copy-start.12 = (bf16[256,512]{1,0:T(8,128)(2,1)}, bf16[256,512]{1,0:T(8,128)(2,1)S(1)}, u32[]{:S(2)}) copy-start(bf16[256,512]{1,0:T(8,128)(2,1)S(1)} %collective-permute-done.12.refs_5_) | copy-start | bytes 786436
  41.4 19.2 %collective-permute-start.3 = (bf16[512,256]{1,0:T(8,128)(2,1)S(1)}, bf16[512,256]{1,0:T(8,128)(2,1)S(1)}, u32[]{:S(2)}, u32[]{:S(2)}) collective-permute-start(bf16[512,256]{1,0:T(8,128)(2,1)S(1)} %pad_maximum_fusion.refs_2_), channel_id=1, source_target_pairs={{0,6},{1,7},{2,4},{3,5},{4,2},{5,3},{6,0},{7,1},{8,14},{9,15},{10,... | collective-permute-start | bytes 786440 | tf_op jit(solution)/shard_map/ppermute | solution.py:336
  44.3 1.7 %copy-start.14 = (bf16[256,512]{1,0:T(8,128)(2,1)}, bf16[256,512]{1,0:T(8,128)(2,1)S(1)}, u32[]{:S(2)}) copy-start(bf16[256,512]{1,0:T(8,128)(2,1)S(1)} %collective-permute-done.15.refs_9_) | copy-start | bytes 786436
  44.3 19.1 %collective-permute-start.7 = (bf16[512,256]{1,0:T(8,128)(2,1)}, bf16[512,256]{1,0:T(8,128)(2,1)S(1)}, u32[]{:S(2)}, u32[]{:S(2)}) collective-permute-start(bf16[512,256]{1,0:T(8,128)(2,1)} %hold.1.refs_2_), channel_id=1, source_target_pairs={{0,2},{1,3},{2,0},{3,1},{4,6},{5,7},{6,4},{7,5},{8,10},{9,11},{10,... | collective-permute-start | bytes 786440 | tf_op jit(solution)/shard_map/ppermute | solution.py:333
  46.0 0.8 copy-start.7
  54.9 28.9 %collective-permute-start.16 = (bf16[256,1024]{1,0:T(8,128)(2,1)}, bf16[256,1024]{1,0:T(8,128)(2,1)S(1)}, u32[]{:S(2)}, u32[]{:S(2)}) collective-permute-start(bf16[256,1024]{1,0:T(8,128)(2,1)} %get-tuple-element.24), channel_id=1, source_target_pairs={{0,1},{1,0},{2,3},{3,2},{4,5},{5,4},{6,7},{7,6},{8,9},{9,8},{10,11... | collective-permute-start | bytes 1572872 | tf_op jit(solution)/shard_map/ppermute | solution.py:330
  56.4 11.4 %copy-start.11 = (bf16[512,256]{1,0:T(8,128)(2,1)}, bf16[512,256]{1,0:T(8,128)(2,1)S(1)}, u32[]{:S(2)}) copy-start(bf16[512,256]{1,0:T(8,128)(2,1)S(1)} %collective-permute-done.8.refs_4_) | copy-start | bytes 786436
  56.4 11.4 %collective-permute-start.9 = (bf16[512,256]{1,0:T(8,128)(2,1)S(1)}, bf16[512,256]{1,0:T(8,128)(2,1)S(1)}, u32[]{:S(2)}, u32[]{:S(2)}) collective-permute-start(bf16[512,256]{1,0:T(8,128)(2,1)S(1)} %collective-permute-done.8.refs_4_), channel_id=1, source_target_pairs={{0,2},{1,3},{2,0},{3,1},{4,6},{5,7},{6,4},{7,5},{8,10},{9,11},{10,... | collective-permute-start | bytes 786440 | tf_op jit(solution)/shard_map/ppermute | solution.py:333
  60.6 16.5 %copy-start.2 = (bf16[512,256]{1,0:T(8,128)(2,1)}, bf16[512,256]{1,0:T(8,128)(2,1)S(1)}, u32[]{:S(2)}) copy-start(bf16[512,256]{1,0:T(8,128)(2,1)S(1)} %collective-permute-done.3.refs_4_) | copy-start | bytes 786436
  60.6 15.0 %collective-permute-start.2 = (bf16[512,256]{1,0:T(8,128)(2,1)S(1)}, bf16[512,256]{1,0:T(8,128)(2,1)S(1)}, u32[]{:S(2)}, u32[]{:S(2)}) collective-permute-start(bf16[512,256]{1,0:T(8,128)(2,1)S(1)} %pad_maximum_fusion.refs_2_), channel_id=1, source_target_pairs={{0,2},{1,3},{2,0},{3,1},{4,6},{5,7},{6,4},{7,5},{8,10},{9,11},{10,... | collective-permute-start | bytes 786440 | tf_op jit(solution)/shard_map/ppermute | solution.py:333
  63.4 4.4 %copy-start.15 = (bf16[512,256]{1,0:T(8,128)(2,1)}, bf16[512,256]{1,0:T(8,128)(2,1)S(1)}, u32[]{:S(2)}) copy-start(bf16[512,256]{1,0:T(8,128)(2,1)S(1)} %collective-permute-done.7.refs_3_) | copy-start | bytes 786436
  63.4 13.7 %collective-permute-start.4 = (bf16[512,256]{1,0:T(8,128)(2,1)S(1)}, bf16[512,256]{1,0:T(8,128)(2,1)S(1)}, u32[]{:S(2)}, u32[]{:S(2)}) collective-permute-start(bf16[512,256]{1,0:T(8,128)(2,1)S(1)} %collective-permute-done.3.refs_4_), channel_id=1, source_target_pairs={{0,2},{1,3},{2,0},{3,1},{4,6},{5,7},{6,4},{7,5},{8,10},{9,11},{10,... | collective-permute-start | bytes 786440 | tf_op jit(solution)/shard_map/ppermute | solution.py:333
  63.5 4.3 %copy-start = (bf16[256,1024]{1,0:T(8,128)(2,1)}, bf16[256,1024]{1,0:T(8,128)(2,1)S(1)}, u32[]{:S(2)}) copy-start(bf16[256,1024]{1,0:T(8,128)(2,1)S(1)} %collective-permute-done.1.refs_1_) | copy-start | bytes 1572868
  67.8 0.7 copy-start.16
  74.1 14.9 %collective-permute-start.17 = (bf16[256,512]{1,0:T(8,128)(2,1)}, bf16[256,512]{1,0:T(8,128)(2,1)S(1)}, u32[]{:S(2)}, u32[]{:S(2)}) collective-permute-start(bf16[256,512]{1,0:T(8,128)(2,1)} %get-tuple-element.22.refs_6_), channel_id=1, source_target_pairs={{0,1},{1,0},{2,3},{3,2},{4,5},{5,4},{6,7},{7,6},{8,9},{9,8},{10,11... | collective-permute-start | bytes 786440 | tf_op jit(solution)/shard_map/ppermute | solution.py:330
  75.7 1.5 %copy-start.3 = (bf16[512,256]{1,0:T(8,128)(2,1)}, bf16[512,256]{1,0:T(8,128)(2,1)S(1)}, u32[]{:S(2)}) copy-start(bf16[512,256]{1,0:T(8,128)(2,1)S(1)} %collective-permute-done.2.refs_3_) | copy-start | bytes 786436
  77.1 0.7 copy-start.4
  81.7 8.0 %collective-permute-start.18 = (bf16[256,512]{1,0:T(8,128)(2,1)}, bf16[256,512]{1,0:T(8,128)(2,1)S(1)}, u32[]{:S(2)}, u32[]{:S(2)}) collective-permute-start(bf16[256,512]{1,0:T(8,128)(2,1)} %attention_v_other.1.refs_6_), channel_id=1, source_target_pairs={{0,1},{1,0},{2,3},{3,2},{4,5},{5,4},{6,7},{7,6},{8,9},{9,8},{10,11... | collective-permute-start | bytes 786440 | tf_op jit(solution)/shard_map/ppermute | solution.py:330

commit v6 on v5

--- a/solution.py
+++ b/solution.py
@@ -60,7 +60,7 @@
             p = jnp.exp2((s - top) * EXP_SCALE)
             total = jnp.sum(p, axis=1, keepdims=True)
             mixed = jnp.dot(p.astype(jnp.bfloat16), v, preferred_element_type=jnp.float32)
-            store_out(u, g, (mixed / total).astype(jnp.bfloat16))
+            store_out(u, g, (mixed * (1.0 / total)).astype(jnp.bfloat16))
 
     def choose(counts):
         if len(counts) == 1:

time: 91.2 us -> 90.8 us (level)
  Pallas kernels: 25.8 us -> 27.7 us
  starting transfers between devices: 42.4 us -> 40.9 us
    pallas_call x4, Pallas kernels: 21.8 us -> 23.7 us  [attention(): pl.pallas_call(kernel, out_shape=shapes, in_specs=[smem, smem] + [hbm] *...]
  transfers between devices with their start and end apart: 19 -> 19, of which waited for: 6 -> 6; matrix products, arithmetic and copies ran while one was open for 4% -> 4% of each run, Pallas kernels for 26% -> 29%
where the time goes in v6:
time: 90.8 us; the launch traced here: 90.2 us
  starting transfers between devices  40.9 us (45%)
  Pallas kernels  27.7 us (31%)
  waiting for transfers between devices  14.3 us (16%)
  local copies, waits for them, and re-layouts  6.23 us (7%)
    pallas_call x4, Pallas kernels, attention(): pl.pallas_call(kernel, out_shape=shapes, in_specs=[smem, smem] + [hbm] *...  23.7 us
    ppermute x8, starting transfers between devices, swap_outer(): return lax.ppermute(a, both, outer)  18.1 us
    ppermute x4, starting transfers between devices, swap_ends(): return lax.ppermute(a, both, ends)  12.1 us
    ppermute x7, starting transfers between devices, swap_x(): return lax.ppermute(a, both, across)  10.7 us
    ppermute x8, waiting for transfers between devices, swap_outer(): return lax.ppermute(a, both, outer)  10.5 us
    pallas_call x2, Pallas kernels, split(): pl.pallas_call(kernel, out_shape=[jax.ShapeDtypeStruct((n, width), jnp.bf...  4.02 us
    ppermute x7, waiting for transfers between devices, swap_x(): return lax.ppermute(a, both, across)  3.83 us
    unnamed x36, local copies, waits for them, and re-layouts  2.96 us
  transfers between devices with their start and end apart: 19, of which 6 were waited for; matrix products, arithmetic and copies ran while one was open for 4% of the time, Pallas kernels for 29%

profile of v6, /device:TPU:0, one launch (start us, length us, event | category | flops | bytes accessed | tf_op | source)
XLA Modules:
  0.0 90.2 jit_solution(11482617935927943938)
XLA Ops:
  0.0 2.0 %split_kv.1 = (bf16[256,512]{1,0:T(8,128)(2,1)}, bf16[256,512]{1,0:T(8,128)(2,1)}, bf16[256,512]{1,0:T(8,128)(2,1)}, bf16[256,512]{1,0:T(8,128)(2,1)}) custom-call(bf16[256,1024]{1,0:T(8,128)(2,1)} %refs_0_.6, bf16[256,1024]{1,0:T(8,128)(2,1)} %refs_1_.1), custom_call_target="tpu_custom_call" | custom-call | bytes 2097152 | tf_op jit(solution)/shard_map/split_kv/pallas_call | solution.py:225
  2.0 3.0 %collective-permute-start.5 = (bf16[256,512]{1,0:T(8,128)(2,1)}, bf16[256,512]{1,0:T(8,128)(2,1)S(1)}, u32[]{:S(2)}, u32[]{:S(2)}) collective-permute-start(bf16[256,512]{1,0:T(8,128)(2,1)} %get-tuple-element.18), channel_id=1, source_target_pairs={{0,1},{1,0},{2,3},{3,2},{4,5},{5,4},{6,7},{7,6},{8,9},{9,8},{10,11... | collective-permute-start | bytes 786440 | tf_op jit(solution)/shard_map/ppermute | solution.py:330
  5.0 0.1 collective-permute-start
  5.1 4.1 %collective-permute-start.13 = (bf16[256,512]{1,0:T(8,128)(2,1)}, bf16[256,512]{1,0:T(8,128)(2,1)S(1)}, u32[]{:S(2)}, u32[]{:S(2)}) collective-permute-start(bf16[256,512]{1,0:T(8,128)(2,1)} %get-tuple-element.20.refs_2_), channel_id=1, source_target_pairs={{0,6},{1,7},{2,4},{3,5},{4,2},{5,3},{6,0},{7,1},{8,14},{9,15},{10,... | collective-permute-start | bytes 786440 | tf_op jit(solution)/shard_map/ppermute | solution.py:336
  9.2 3.2 %collective-permute-done.5.refs_3_ = bf16[256,512]{1,0:T(8,128)(2,1)S(1)} collective-permute-done((bf16[256,512]{1,0:T(8,128)(2,1)}, bf16[256,512]{1,0:T(8,128)(2,1)S(1)}, u32[]{:S(2)}, u32[]{:S(2)}) %collective-permute-start.5) | collective-permute-done | bytes 262176 | tf_op jit(solution)/shard_map/ppermute | solution.py:330
  12.4 4.2 %collective-permute-start.6 = (bf16[256,512]{1,0:T(8,128)(2,1)S(1)}, bf16[256,512]{1,0:T(8,128)(2,1)S(1)}, u32[]{:S(2)}, u32[]{:S(2)}) collective-permute-start(bf16[256,512]{1,0:T(8,128)(2,1)S(1)} %collective-permute-done.5.refs_3_), channel_id=1, source_target_pairs={{0,6},{1,7},{2,4},{3,5},{4,2},{5,3},{6,0},{7,1},{8,14},{9,15},{10,... | collective-permute-start | bytes 786440 | tf_op jit(solution)/shard_map/ppermute | solution.py:336
  16.5 0.6 collective-permute-done.refs_1_
  17.2 0.7 copy-done.6
  17.9 2.0 %split_q.1 = (bf16[256,1024]{1,0:T(8,128)(2,1)}, bf16[256,1024]{1,0:T(8,128)(2,1)}) custom-call(bf16[256,4096]{1,0:T(8,128)(2,1)} %refs_0_.11, bf16[256,512]{1,0:T(8,128)(2,1)} %copy-done.6), custom_call_target="tpu_custom_call" | custom-call | bytes 2097152 | tf_op jit(solution)/shard_map/split_q/pallas_call | solution.py:225
  19.9 1.8 %collective-permute-start.10 = (bf16[256,1024]{1,0:T(8,128)(2,1)}, bf16[256,1024]{1,0:T(8,128)(2,1)S(1)}, u32[]{:S(2)}, u32[]{:S(2)}) collective-permute-start(bf16[256,1024]{1,0:T(8,128)(2,1)} %get-tuple-element.19), channel_id=1, source_target_pairs={{0,1},{1,0},{2,3},{3,2},{4,5},{5,4},{6,7},{7,6},{8,9},{9,8},{10,11... | collective-permute-start | bytes 1572872 | tf_op jit(solution)/shard_map/ppermute | solution.py:330
  21.7 1.6 %collective-permute-start.12 = (bf16[256,512]{1,0:T(8,128)(2,1)S(1)}, bf16[256,512]{1,0:T(8,128)(2,1)S(1)}, u32[]{:S(2)}, u32[]{:S(2)}) collective-permute-start(bf16[256,512]{1,0:T(8,128)(2,1)S(1)} %collective-permute-done.5.refs_3_), channel_id=1, source_target_pairs={{0,2},{1,3},{2,0},{3,1},{4,6},{5,7},{6,4},{7,5},{8,10},{9,11},{10,... | collective-permute-start | bytes 786440 | tf_op jit(solution)/shard_map/ppermute | solution.py:333
  23.4 0.0 collective-permute-done.13.refs_6_
  23.4 3.7 %collective-permute-start.14 = (bf16[256,512]{1,0:T(8,128)(2,1)S(1)}, bf16[256,512]{1,0:T(8,128)(2,1)S(1)}, u32[]{:S(2)}, u32[]{:S(2)}) collective-permute-start(bf16[256,512]{1,0:T(8,128)(2,1)S(1)} %collective-permute-done.13.refs_6_), channel_id=1, source_target_pairs={{0,2},{1,3},{2,0},{3,1},{4,6},{5,7},{6,4},{7,5},{8,10},{9,11},{10,... | collective-permute-start | bytes 786440 | tf_op jit(solution)/shard_map/ppermute | solution.py:333
  27.1 0.0 collective-permute-done.6.refs_1_.refs_7_
  27.1 4.6 %collective-permute-start.15 = (bf16[256,512]{1,0:T(8,128)(2,1)S(1)}, bf16[256,512]{1,0:T(8,128)(2,1)S(1)}, u32[]{:S(2)}, u32[]{:S(2)}) collective-permute-start(bf16[256,512]{1,0:T(8,128)(2,1)S(1)} %collective-permute-done.6.refs_1_.refs_7_), channel_id=1, source_target_pairs={{0,2},{1,3},{2,0},{3,1},{4,6},{5,7},{6,4},{7,5},{8,10},{9,11},{10,... | collective-permute-start | bytes 786440 | tf_op jit(solution)/shard_map/ppermute | solution.py:333
  31.7 1.0 %fusion.1 = (bf16[256,256]{1,0:T(8,128)(2,1)S(1)}, bf16[256,256]{1,0:T(8,128)(2,1)S(1)}) fusion(bf16[256,512]{1,0:T(8,128)(2,1)} %copy-done.6), kind=kLoop, calls=%fused_computation.6 | loop fusion | bytes 524288 | tf_op jit(solution)/shard_map/slice | solution.py:366
  32.7 0.7 pad_maximum_fusion.1.refs_0_
  33.4 1.6 %collective-permute-start.1 = (bf16[256,1024]{1,0:T(8,128)(2,1)}, bf16[256,1024]{1,0:T(8,128)(2,1)S(1)}, u32[]{:S(2)}, u32[]{:S(2)}) collective-permute-start(bf16[256,1024]{1,0:T(8,128)(2,1)} %get-tuple-element.16), channel_id=1, source_target_pairs={{0,1},{1,0},{2,3},{3,2},{4,5},{5,4},{6,7},{7,6},{8,9},{9,8},{10,11... | collective-permute-start | bytes 1572872 | tf_op jit(solution)/shard_map/ppermute | solution.py:330
  35.0 4.8 %collective-permute-done.14.refs_8_ = bf16[256,512]{1,0:T(8,128)(2,1)S(1)} collective-permute-done((bf16[256,512]{1,0:T(8,128)(2,1)S(1)}, bf16[256,512]{1,0:T(8,128)(2,1)S(1)}, u32[]{:S(2)}, u32[]{:S(2)}) %collective-permute-start.14) | collective-permute-done | bytes 262176 | tf_op jit(solution)/shard_map/ppermute | solution.py:333
  39.8 1.6 %collective-permute-start.8 = (bf16[512,256]{1,0:T(8,128)(2,1)}, bf16[512,256]{1,0:T(8,128)(2,1)S(1)}, u32[]{:S(2)}, u32[]{:S(2)}) collective-permute-start(bf16[512,256]{1,0:T(8,128)(2,1)} %hold.1.refs_2_), channel_id=1, source_target_pairs={{0,6},{1,7},{2,4},{3,5},{4,2},{5,3},{6,0},{7,1},{8,14},{9,15},{10,... | collective-permute-start | bytes 786440 | tf_op jit(solution)/shard_map/ppermute | solution.py:336
  41.4 0.0 collective-permute-done.12.refs_5_
  41.4 2.3 %collective-permute-start.3 = (bf16[512,256]{1,0:T(8,128)(2,1)S(1)}, bf16[512,256]{1,0:T(8,128)(2,1)S(1)}, u32[]{:S(2)}, u32[]{:S(2)}) collective-permute-start(bf16[512,256]{1,0:T(8,128)(2,1)S(1)} %pad_maximum_fusion.refs_2_), channel_id=1, source_target_pairs={{0,6},{1,7},{2,4},{3,5},{4,2},{5,3},{6,0},{7,1},{8,14},{9,15},{10,... | collective-permute-start | bytes 786440 | tf_op jit(solution)/shard_map/ppermute | solution.py:336
  43.7 0.6 collective-permute-done.15.refs_9_
  44.3 1.7 %collective-permute-start.7 = (bf16[512,256]{1,0:T(8,128)(2,1)}, bf16[512,256]{1,0:T(8,128)(2,1)S(1)}, u32[]{:S(2)}, u32[]{:S(2)}) collective-permute-start(bf16[512,256]{1,0:T(8,128)(2,1)} %hold.1.refs_2_), channel_id=1, source_target_pairs={{0,2},{1,3},{2,0},{3,1},{4,6},{5,7},{6,4},{7,5},{8,10},{9,11},{10,... | collective-permute-start | bytes 786440 | tf_op jit(solution)/shard_map/ppermute | solution.py:333
  46.0 0.8 copy-done.7
  46.8 8.7 %attention_t.1 = (bf16[256,1024]{1,0:T(8,128)(2,1)}, bf16[256,4096]{1,0:T(8,128)(2,1)}) custom-call(s32[8]{0:T(128)} %lengths.7, s32[32]{0:T(128)} %order.7, bf16[256,4096]{1,0:T(8,128)(2,1)} %refs_0_.11, bf16[256,1024]{1,0:T(8,128)(2,1)} %copy-done.7, bf16[256,512]{1,0:T(8,128)(2,1)} %get-tuple-element.20.refs_2_, bf16[256,512]{1,0:T(8,128)(2,1)} %copy-done.8, ...), custom_call_target="tpu_custom_call" | custom-call | flops 1258291200 | bytes 2097152 | tf_op jit(solution)/shard_map/attention_t/pallas_call | solution.py:177
  55.5 1.5 %collective-permute-start.16 = (bf16[256,1024]{1,0:T(8,128)(2,1)}, bf16[256,1024]{1,0:T(8,128)(2,1)S(1)}, u32[]{:S(2)}, u32[]{:S(2)}) collective-permute-start(bf16[256,1024]{1,0:T(8,128)(2,1)} %get-tuple-element.24), channel_id=1, source_target_pairs={{0,1},{1,0},{2,3},{3,2},{4,5},{5,4},{6,7},{7,6},{8,9},{9,8},{10,11... | collective-permute-start | bytes 1572872 | tf_op jit(solution)/shard_map/ppermute | solution.py:330
  57.1 0.0 collective-permute-done.8.refs_4_
  57.1 3.6 %collective-permute-start.9 = (bf16[512,256]{1,0:T(8,128)(2,1)S(1)}, bf16[512,256]{1,0:T(8,128)(2,1)S(1)}, u32[]{:S(2)}, u32[]{:S(2)}) collective-permute-start(bf16[512,256]{1,0:T(8,128)(2,1)S(1)} %collective-permute-done.8.refs_4_), channel_id=1, source_target_pairs={{0,2},{1,3},{2,0},{3,1},{4,6},{5,7},{6,4},{7,5},{8,10},{9,11},{10,... | collective-permute-start | bytes 786440 | tf_op jit(solution)/shard_map/ppermute | solution.py:333
  60.6 0.0 collective-permute-done.3.refs_4_
  60.6 2.8 %collective-permute-start.2 = (bf16[512,256]{1,0:T(8,128)(2,1)S(1)}, bf16[512,256]{1,0:T(8,128)(2,1)S(1)}, u32[]{:S(2)}, u32[]{:S(2)}) collective-permute-start(bf16[512,256]{1,0:T(8,128)(2,1)S(1)} %pad_maximum_fusion.refs_2_), channel_id=1, source_target_pairs={{0,2},{1,3},{2,0},{3,1},{4,6},{5,7},{6,4},{7,5},{8,10},{9,11},{10,... | collective-permute-start | bytes 786440 | tf_op jit(solution)/shard_map/ppermute | solution.py:333
  63.4 0.1 collective-permute-start.4
  63.5 0.0 collective-permute-done.1.refs_1_
  63.5 4.3 %collective-permute-done.9.refs_5_ = bf16[512,256]{1,0:T(8,128)(2,1)S(1)} collective-permute-done((bf16[512,256]{1,0:T(8,128)(2,1)S(1)}, bf16[512,256]{1,0:T(8,128)(2,1)S(1)}, u32[]{:S(2)}, u32[]{:S(2)}) %collective-permute-start.9) | collective-permute-done | bytes 262176 | tf_op jit(solution)/shard_map/ppermute | solution.py:333
  67.9 0.7 copy-done.16
  68.6 6.2 %attention_u.1 = (bf16[256,512]{1,0:T(8,128)(2,1)}, bf16[256,4096]{1,0:T(8,128)(2,1)}) custom-call(s32[8]{0:T(128)} %lengths.7, s32[32]{0:T(128)} %order.7, bf16[256,4096]{1,0:T(8,128)(2,1)} %refs_0_.11, bf16[256,1024]{1,0:T(8,128)(2,1)} %copy-done, bf16[512,256]{1,0:T(8,128)(2,1)} %hold.1.refs_2_, ...), custom_call_target="tpu_custom_call", output_to_operand_aliasing={{1}: (8, {})} | custom-call | flops 188743680 | bytes 1048576 | tf_op jit(solution)/shard_map/attention_u/pallas_call | solution.py:177
  74.7 1.6 %collective-permute-start.17 = (bf16[256,512]{1,0:T(8,128)(2,1)}, bf16[256,512]{1,0:T(8,128)(2,1)S(1)}, u32[]{:S(2)}, u32[]{:S(2)}) collective-permute-start(bf16[256,512]{1,0:T(8,128)(2,1)} %get-tuple-element.22.refs_6_), channel_id=1, source_target_pairs={{0,1},{1,0},{2,3},{3,2},{4,5},{5,4},{6,7},{7,6},{8,9},{9,8},{10,11... | collective-permute-start | bytes 786440 | tf_op jit(solution)/shard_map/ppermute | solution.py:330
  76.3 0.0 collective-permute-done.2.refs_3_
  76.3 0.8 collective-permute-done.4.refs_5_
  77.1 0.7 copy-done.4
  77.8 4.6 %attention_v_other.1.refs_6_ = bf16[256,512]{1,0:T(8,128)(2,1)} custom-call(s32[8]{0:T(128)} %lengths.7, s32[32]{0:T(128)} %order.7, bf16[256,4096]{1,0:T(8,128)(2,1)} %refs_0_.11, bf16[256,1024]{1,0:T(8,128)(2,1)} %copy-done, bf16[512,256]{1,0:T(8,128)(2,1)} %copy-done.1, bf16[512,256]{1,0:T(8,128)(2,1)} %copy-done.3, bf16[512,256]{1,0:T(8,128)(2,1)} %copy-done.2, ...), custom_call_target="tpu_custom_call" | custom-call | flops 94371840 | bytes 524288 | tf_op jit(solution)/shard_map/attention_v_other/pallas_call | solution.py:177
  82.4 1.2 %collective-permute-start.18 = (bf16[256,512]{1,0:T(8,128)(2,1)}, bf16[256,512]{1,0:T(8,128)(2,1)S(1)}, u32[]{:S(2)}, u32[]{:S(2)}) collective-permute-start(bf16[256,512]{1,0:T(8,128)(2,1)} %attention_v_other.1.refs_6_), channel_id=1, source_target_pairs={{0,1},{1,0},{2,3},{3,2},{4,5},{5,4},{6,7},{7,6},{8,9},{9,8},{10,11... | collective-permute-start | bytes 786440 | tf_op jit(solution)/shard_map/ppermute | solution.py:330
  83.6 0.0 collective-permute-done.16
  83.6 0.8 constant_dynamic-update-slice_fusion.2.refs_7_
  84.5 4.2 %attention_v_own.1 = bf16[256,4096]{1,0:T(8,128)(2,1)} custom-call(s32[8]{0:T(128)} %lengths.7, s32[32]{0:T(128)} %order.7, bf16[256,4096]{1,0:T(8,128)(2,1)} %refs_0_.11, bf16[256,1024]{1,0:T(8,128)(2,1)} %copy-done, bf16[512,256]{1,0:T(8,128)(2,1)} %copy-done.1, bf16[512,256]{1,0:T(8,128)(2,1)} %copy-done.3, ...), custom_call_target="tpu_custom_call", output_to_operand_aliasing={{}: (9, {})} | custom-call | flops 94371840 | bytes 524288 | tf_op jit(solution)/shard_map/attention_v_own/pallas_call | solution.py:177
  88.7 0.0 collective-permute-done.17
  88.7 0.7 constant_dynamic-update-slice_fusion.1
  89.4 0.7 constant_dynamic-update-slice_fusion
  (40 shorter events, 0.1 us)
Async XLA Ops:
  2.0 19.7 %copy-start.17 = (bf16[256,512]{1,0:T(8,128)(2,1)S(1)}, bf16[256,512]{1,0:T(8,128)(2,1)}, u32[]{:S(2)}) copy-start(bf16[256,512]{1,0:T(8,128)(2,1)} %get-tuple-element.17) | copy-start | bytes 786436
  2.0 10.3 %collective-permute-start.5 = (bf16[256,512]{1,0:T(8,128)(2,1)}, bf16[256,512]{1,0:T(8,128)(2,1)S(1)}, u32[]{:S(2)}, u32[]{:S(2)}) collective-permute-start(bf16[256,512]{1,0:T(8,128)(2,1)} %get-tuple-element.18), channel_id=1, source_target_pairs={{0,1},{1,0},{2,3},{3,2},{4,5},{5,4},{6,7},{7,6},{8,9},{9,8},{10,11... | collective-permute-start | bytes 786440 | tf_op jit(solution)/shard_map/ppermute | solution.py:330
  5.0 12.1 %collective-permute-start = (bf16[256,512]{1,0:T(8,128)(2,1)}, bf16[256,512]{1,0:T(8,128)(2,1)S(1)}, u32[]{:S(2)}, u32[]{:S(2)}) collective-permute-start(bf16[256,512]{1,0:T(8,128)(2,1)} %get-tuple-element.15), channel_id=1, source_target_pairs={{0,1},{1,0},{2,3},{3,2},{4,5},{5,4},{6,7},{7,6},{8,9},{9,8},{10,11... | collective-permute-start | bytes 786440 | tf_op jit(solution)/shard_map/ppermute | solution.py:330
  5.1 18.3 %collective-permute-start.13 = (bf16[256,512]{1,0:T(8,128)(2,1)}, bf16[256,512]{1,0:T(8,128)(2,1)S(1)}, u32[]{:S(2)}, u32[]{:S(2)}) collective-permute-start(bf16[256,512]{1,0:T(8,128)(2,1)} %get-tuple-element.20.refs_2_), channel_id=1, source_target_pairs={{0,6},{1,7},{2,4},{3,5},{4,2},{5,3},{6,0},{7,1},{8,14},{9,15},{10,... | collective-permute-start | bytes 786440 | tf_op jit(solution)/shard_map/ppermute | solution.py:336
  12.4 33.6 %copy-start.8 = (bf16[256,512]{1,0:T(8,128)(2,1)}, bf16[256,512]{1,0:T(8,128)(2,1)S(1)}, u32[]{:S(2)}) copy-start(bf16[256,512]{1,0:T(8,128)(2,1)S(1)} %collective-permute-done.5.refs_3_) | copy-start | bytes 786436
  12.4 14.7 %collective-permute-start.6 = (bf16[256,512]{1,0:T(8,128)(2,1)S(1)}, bf16[256,512]{1,0:T(8,128)(2,1)S(1)}, u32[]{:S(2)}, u32[]{:S(2)}) collective-permute-start(bf16[256,512]{1,0:T(8,128)(2,1)S(1)} %collective-permute-done.5.refs_3_), channel_id=1, source_target_pairs={{0,6},{1,7},{2,4},{3,5},{4,2},{5,3},{6,0},{7,1},{8,14},{9,15},{10,... | collective-permute-start | bytes 786440 | tf_op jit(solution)/shard_map/ppermute | solution.py:336
  16.5 16.9 %collective-permute-start.11 = (bf16[256,512]{1,0:T(8,128)(2,1)}, bf16[256,512]{1,0:T(8,128)(2,1)S(1)}, u32[]{:S(2)}, u32[]{:S(2)}) collective-permute-start(bf16[256,512]{1,0:T(8,128)(2,1)} %get-tuple-element.20.refs_2_), channel_id=1, source_target_pairs={{0,2},{1,3},{2,0},{3,1},{4,6},{5,7},{6,4},{7,5},{8,10},{9,11},{10,... | collective-permute-start | bytes 786440 | tf_op jit(solution)/shard_map/ppermute | solution.py:333
  17.2 0.7 copy-start.6
  19.9 26.1 %collective-permute-start.10 = (bf16[256,1024]{1,0:T(8,128)(2,1)}, bf16[256,1024]{1,0:T(8,128)(2,1)S(1)}, u32[]{:S(2)}, u32[]{:S(2)}) collective-permute-start(bf16[256,1024]{1,0:T(8,128)(2,1)} %get-tuple-element.19), channel_id=1, source_target_pairs={{0,1},{1,0},{2,3},{3,2},{4,5},{5,4},{6,7},{7,6},{8,9},{9,8},{10,11... | collective-permute-start | bytes 1572872 | tf_op jit(solution)/shard_map/ppermute | solution.py:330
  21.7 19.6 %collective-permute-start.12 = (bf16[256,512]{1,0:T(8,128)(2,1)S(1)}, bf16[256,512]{1,0:T(8,128)(2,1)S(1)}, u32[]{:S(2)}, u32[]{:S(2)}) collective-permute-start(bf16[256,512]{1,0:T(8,128)(2,1)S(1)} %collective-permute-done.5.refs_3_), channel_id=1, source_target_pairs={{0,2},{1,3},{2,0},{3,1},{4,6},{5,7},{6,4},{7,5},{8,10},{9,11},{10,... | collective-permute-start | bytes 786440 | tf_op jit(solution)/shard_map/ppermute | solution.py:333
  23.4 22.6 %copy-start.9 = (bf16[256,512]{1,0:T(8,128)(2,1)}, bf16[256,512]{1,0:T(8,128)(2,1)S(1)}, u32[]{:S(2)}) copy-start(bf16[256,512]{1,0:T(8,128)(2,1)S(1)} %collective-permute-done.13.refs_6_) | copy-start | bytes 786436
  23.4 16.4 %collective-permute-start.14 = (bf16[256,512]{1,0:T(8,128)(2,1)S(1)}, bf16[256,512]{1,0:T(8,128)(2,1)S(1)}, u32[]{:S(2)}, u32[]{:S(2)}) collective-permute-start(bf16[256,512]{1,0:T(8,128)(2,1)S(1)} %collective-permute-done.13.refs_6_), channel_id=1, source_target_pairs={{0,2},{1,3},{2,0},{3,1},{4,6},{5,7},{6,4},{7,5},{8,10},{9,11},{10,... | collective-permute-start | bytes 786440 | tf_op jit(solution)/shard_map/ppermute | solution.py:333
  27.1 6.3 %copy-start.5 = (bf16[256,512]{1,0:T(8,128)(2,1)}, bf16[256,512]{1,0:T(8,128)(2,1)S(1)}, u32[]{:S(2)}) copy-start(bf16[256,512]{1,0:T(8,128)(2,1)S(1)} %collective-permute-done.6.refs_1_.refs_7_) | copy-start | bytes 786436
  27.1 17.2 %collective-permute-start.15 = (bf16[256,512]{1,0:T(8,128)(2,1)S(1)}, bf16[256,512]{1,0:T(8,128)(2,1)S(1)}, u32[]{:S(2)}, u32[]{:S(2)}) collective-permute-start(bf16[256,512]{1,0:T(8,128)(2,1)S(1)} %collective-permute-done.6.refs_1_.refs_7_), channel_id=1, source_target_pairs={{0,2},{1,3},{2,0},{3,1},{4,6},{5,7},{6,4},{7,5},{8,10},{9,11},{10,... | collective-permute-start | bytes 786440 | tf_op jit(solution)/shard_map/ppermute | solution.py:333
  33.4 12.6 %copy-start.10 = (bf16[256,512]{1,0:T(8,128)(2,1)}, bf16[256,512]{1,0:T(8,128)(2,1)S(1)}, u32[]{:S(2)}) copy-start(bf16[256,512]{1,0:T(8,128)(2,1)S(1)} %collective-permute-done.11.refs_4_) | copy-start | bytes 786436
  33.4 30.1 %collective-permute-start.1 = (bf16[256,1024]{1,0:T(8,128)(2,1)}, bf16[256,1024]{1,0:T(8,128)(2,1)S(1)}, u32[]{:S(2)}, u32[]{:S(2)}) collective-permute-start(bf16[256,1024]{1,0:T(8,128)(2,1)} %get-tuple-element.16), channel_id=1, source_target_pairs={{0,1},{1,0},{2,3},{3,2},{4,5},{5,4},{6,7},{7,6},{8,9},{9,8},{10,11... | collective-permute-start | bytes 1572872 | tf_op jit(solution)/shard_map/ppermute | solution.py:330
  39.8 6.2 %copy-start.13 = (bf16[256,512]{1,0:T(8,128)(2,1)}, bf16[256,512]{1,0:T(8,128)(2,1)S(1)}, u32[]{:S(2)}) copy-start(bf16[256,512]{1,0:T(8,128)(2,1)S(1)} %collective-permute-done.14.refs_8_) | copy-start | bytes 786436
  39.8 17.3 %collective-permute-start.8 = (bf16[512,256]{1,0:T(8,128)(2,1)}, bf16[512,256]{1,0:T(8,128)(2,1)S(1)}, u32[]{:S(2)}, u32[]{:S(2)}) collective-permute-start(bf16[512,256]{1,0:T(8,128)(2,1)} %hold.1.refs_2_), channel_id=1, source_target_pairs={{0,6},{1,7},{2,4},{3,5},{4,2},{5,3},{6,0},{7,1},{8,14},{9,15},{10,... | collective-permute-start | bytes 786440 | tf_op jit(solution)/shard_map/ppermute | solution.py:336
  41.3 19.3 %copy-start.1 = (bf16[512,256]{1,0:T(8,128)(2,1)}, bf16[512,256]{1,0:T(8,128)(2,1)S(1)}, u32[]{:S(2)}) copy-start(bf16[512,256]{1,0:T(8,128)(2,1)S(1)} %pad_maximum_fusion.refs_2_) | copy-start | bytes 786436
  41.4 4.6 %copy-start.12 = (bf16[256,512]{1,0:T(8,128)(2,1)}, bf16[256,512]{1,0:T(8,128)(2,1)S(1)}, u32[]{:S(2)}) copy-start(bf16[256,512]{1,0:T(8,128)(2,1)S(1)} %collective-permute-done.12.refs_5_) | copy-start | bytes 786436
  41.4 19.2 %collective-permute-start.3 = (bf16[512,256]{1,0:T(8,128)(2,1)S(1)}, bf16[512,256]{1,0:T(8,128)(2,1)S(1)}, u32[]{:S(2)}, u32[]{:S(2)}) collective-permute-start(bf16[512,256]{1,0:T(8,128)(2,1)S(1)} %pad_maximum_fusion.refs_2_), channel_id=1, source_target_pairs={{0,6},{1,7},{2,4},{3,5},{4,2},{5,3},{6,0},{7,1},{8,14},{9,15},{10,... | collective-permute-start | bytes 786440 | tf_op jit(solution)/shard_map/ppermute | solution.py:336
  44.3 1.7 %copy-start.14 = (bf16[256,512]{1,0:T(8,128)(2,1)}, bf16[256,512]{1,0:T(8,128)(2,1)S(1)}, u32[]{:S(2)}) copy-start(bf16[256,512]{1,0:T(8,128)(2,1)S(1)} %collective-permute-done.15.refs_9_) | copy-start | bytes 786436
  44.3 19.1 %collective-permute-start.7 = (bf16[512,256]{1,0:T(8,128)(2,1)}, bf16[512,256]{1,0:T(8,128)(2,1)S(1)}, u32[]{:S(2)}, u32[]{:S(2)}) collective-permute-start(bf16[512,256]{1,0:T(8,128)(2,1)} %hold.1.refs_2_), channel_id=1, source_target_pairs={{0,2},{1,3},{2,0},{3,1},{4,6},{5,7},{6,4},{7,5},{8,10},{9,11},{10,... | collective-permute-start | bytes 786440 | tf_op jit(solution)/shard_map/ppermute | solution.py:333
  46.0 0.8 copy-start.7
  55.5 28.1 %collective-permute-start.16 = (bf16[256,1024]{1,0:T(8,128)(2,1)}, bf16[256,1024]{1,0:T(8,128)(2,1)S(1)}, u32[]{:S(2)}, u32[]{:S(2)}) collective-permute-start(bf16[256,1024]{1,0:T(8,128)(2,1)} %get-tuple-element.24), channel_id=1, source_target_pairs={{0,1},{1,0},{2,3},{3,2},{4,5},{5,4},{6,7},{7,6},{8,9},{9,8},{10,11... | collective-permute-start | bytes 1572872 | tf_op jit(solution)/shard_map/ppermute | solution.py:330
  57.1 10.8 %copy-start.11 = (bf16[512,256]{1,0:T(8,128)(2,1)}, bf16[512,256]{1,0:T(8,128)(2,1)S(1)}, u32[]{:S(2)}) copy-start(bf16[512,256]{1,0:T(8,128)(2,1)S(1)} %collective-permute-done.8.refs_4_) | copy-start | bytes 786436
  57.1 10.8 %collective-permute-start.9 = (bf16[512,256]{1,0:T(8,128)(2,1)S(1)}, bf16[512,256]{1,0:T(8,128)(2,1)S(1)}, u32[]{:S(2)}, u32[]{:S(2)}) collective-permute-start(bf16[512,256]{1,0:T(8,128)(2,1)S(1)} %collective-permute-done.8.refs_4_), channel_id=1, source_target_pairs={{0,2},{1,3},{2,0},{3,1},{4,6},{5,7},{6,4},{7,5},{8,10},{9,11},{10,... | collective-permute-start | bytes 786440 | tf_op jit(solution)/shard_map/ppermute | solution.py:333
  60.6 16.5 %copy-start.2 = (bf16[512,256]{1,0:T(8,128)(2,1)}, bf16[512,256]{1,0:T(8,128)(2,1)S(1)}, u32[]{:S(2)}) copy-start(bf16[512,256]{1,0:T(8,128)(2,1)S(1)} %collective-permute-done.3.refs_4_) | copy-start | bytes 786436
  60.6 15.7 %collective-permute-start.2 = (bf16[512,256]{1,0:T(8,128)(2,1)S(1)}, bf16[512,256]{1,0:T(8,128)(2,1)S(1)}, u32[]{:S(2)}, u32[]{:S(2)}) collective-permute-start(bf16[512,256]{1,0:T(8,128)(2,1)S(1)} %pad_maximum_fusion.refs_2_), channel_id=1, source_target_pairs={{0,2},{1,3},{2,0},{3,1},{4,6},{5,7},{6,4},{7,5},{8,10},{9,11},{10,... | collective-permute-start | bytes 786440 | tf_op jit(solution)/shard_map/ppermute | solution.py:333
  63.4 4.4 %copy-start.15 = (bf16[512,256]{1,0:T(8,128)(2,1)}, bf16[512,256]{1,0:T(8,128)(2,1)S(1)}, u32[]{:S(2)}) copy-start(bf16[512,256]{1,0:T(8,128)(2,1)S(1)} %collective-permute-done.7.refs_3_) | copy-start | bytes 786436
  63.4 13.7 %collective-permute-start.4 = (bf16[512,256]{1,0:T(8,128)(2,1)S(1)}, bf16[512,256]{1,0:T(8,128)(2,1)S(1)}, u32[]{:S(2)}, u32[]{:S(2)}) collective-permute-start(bf16[512,256]{1,0:T(8,128)(2,1)S(1)} %collective-permute-done.3.refs_4_), channel_id=1, source_target_pairs={{0,2},{1,3},{2,0},{3,1},{4,6},{5,7},{6,4},{7,5},{8,10},{9,11},{10,... | collective-permute-start | bytes 786440 | tf_op jit(solution)/shard_map/ppermute | solution.py:333
  63.5 4.3 %copy-start = (bf16[256,1024]{1,0:T(8,128)(2,1)}, bf16[256,1024]{1,0:T(8,128)(2,1)S(1)}, u32[]{:S(2)}) copy-start(bf16[256,1024]{1,0:T(8,128)(2,1)S(1)} %collective-permute-done.1.refs_1_) | copy-start | bytes 1572868
  67.8 0.7 copy-start.16
  74.7 14.0 %collective-permute-start.17 = (bf16[256,512]{1,0:T(8,128)(2,1)}, bf16[256,512]{1,0:T(8,128)(2,1)S(1)}, u32[]{:S(2)}, u32[]{:S(2)}) collective-permute-start(bf16[256,512]{1,0:T(8,128)(2,1)} %get-tuple-element.22.refs_6_), channel_id=1, source_target_pairs={{0,1},{1,0},{2,3},{3,2},{4,5},{5,4},{6,7},{7,6},{8,9},{9,8},{10,11... | collective-permute-start | bytes 786440 | tf_op jit(solution)/shard_map/ppermute | solution.py:330
  76.3 0.8 copy-start.3
  77.1 0.7 copy-start.4
  82.4 7.0 %collective-permute-start.18 = (bf16[256,512]{1,0:T(8,128)(2,1)}, bf16[256,512]{1,0:T(8,128)(2,1)S(1)}, u32[]{:S(2)}, u32[]{:S(2)}) collective-permute-start(bf16[256,512]{1,0:T(8,128)(2,1)} %attention_v_other.1.refs_6_), channel_id=1, source_target_pairs={{0,1},{1,0},{2,3},{3,2},{4,5},{5,4},{6,7},{7,6},{8,9},{9,8},{10,11... | collective-permute-start | bytes 786440 | tf_op jit(solution)/shard_map/ppermute | solution.py:330
